TPU v7x, 32 devices: a whole 2x2x4 slice. The times are simulated.
32 devices in a mesh: sp: 4 (over y, x), fsdp: 8 (over z, core).
Axes of the slice: x: 2, y: 2, z: 4, core: 2. Of those that a mesh axis runs over, the one named last changes fastest.
Arguments:
- tokens: bfloat16 [8, 1024, 2048], P('fsdp', 'sp'), may hold values from -6 to 6
- cotangent: bfloat16 [8, 1024, 2048], P('fsdp', 'sp'), may hold values from -6 to 6
- positions: int32 [8, 1024], P('fsdp', 'sp'), may hold values from 0 to 1023, as said below
- domain_ids: int32 [8], P('fsdp'), may hold values from 0 to 7
- counts: int32 [8], P('fsdp'), may hold values from 512 to 1024
- loss_weight: float32 [8], P('fsdp'), may hold values from 0.5 to 2
- domain_weights: float32 [8], replicated, may hold values from 0.5 to 2
- q_weight: bfloat16 [2048, 2048], P('fsdp'), may hold values from -0.125 to 0.125
- k_weight: bfloat16 [2048, 1024], P('fsdp'), may hold values from -0.125 to 0.125
- v_weight: bfloat16 [2048, 1024], P('fsdp'), may hold values from -0.125 to 0.125
- g_weight: bfloat16 [2048, 2048], P('fsdp'), may hold values from -0.125 to 0.125
- o_weight: bfloat16 [2048, 2048], P('fsdp'), may hold values from -2 to 2
- gate_weight: bfloat16 [2048, 6144], P('fsdp'), may hold values from -0.125 to 0.125
- up_weight: bfloat16 [2048, 6144], P('fsdp'), may hold values from -0.125 to 0.125
- down_weight: bfloat16 [6144, 2048], P('fsdp'), may hold values from -0.078125 to 0.078125
- attn_gain: bfloat16 [2048], P('fsdp'), may hold values from 0.5 to 1.5
- mlp_gain: bfloat16 [2048], P('fsdp'), may hold values from 0.5 to 1.5
- q_gain: bfloat16 [128], P('fsdp'), may hold values from 0.099609375 to 1.8984375
- k_gain: bfloat16 [128], P('fsdp'), may hold values from 0.099609375 to 1.8984375
Outputs:
- block_out: bfloat16 [8, 1024, 2048], P('fsdp', 'sp')
- input_grad: float32 [8, 1024, 2048], P('fsdp', 'sp')
- q_weight_grad: float32 [2048, 2048], P('fsdp')
- k_weight_grad: float32 [2048, 1024], P('fsdp')
- v_weight_grad: float32 [2048, 1024], P('fsdp')
- g_weight_grad: float32 [2048, 2048], P('fsdp')
- o_weight_grad: float32 [2048, 2048], P('fsdp')
- gate_weight_grad: float32 [2048, 6144], P('fsdp')
- up_weight_gradient: float32 [2048, 6144], P('fsdp')
- down_weight_grad: float32 [6144, 2048], P('fsdp')
- attn_gain_grad: float32 [2048], P('fsdp')
- mlp_gain_grad: float32 [2048], P('fsdp')
- q_gain_grad: float32 [128], P('fsdp')
- k_gain_grad: float32 [128], P('fsdp')
Inputs may be any that keep to these rules, and one draw needn't show every extreme that they name: `positions`: within each sequence a position is 0 at the first token and at a few other tokens, and one more than the position before it elsewhere; one sequence has no such restart after its first token.
All inputs are finite; a program needn't handle non-finite values.
Results may differ from a plain program's by a relative error of at most 0.022.
Values may be sent and summed in bfloat16 or wider, within the bound.
No kernel may reach another device: no remote copies, remote signals or barrier semaphores. Data moves between devices by JAX's collectives and lax.ppermute only.
A program may use at most 448 MiB of HBM per device.

v0:
```python
import jax
import jax.numpy as jnp
from jax import lax
from jax.sharding import PartitionSpec as P

HEAD = 128
SEQ_LEN = 1024


EPS = 1e-06
ROPE_BASE = 1000000.0


def rms_scale(values, gain):
    return values * lax.rsqrt(jnp.mean(values * values, axis=-1, keepdims=True) + EPS) * gain


def rotate(values, cosines, sines):
    half_size = values.shape[-1] // 2
    first_half = values[..., :half_size]
    second_half = values[..., half_size:]
    return jnp.concatenate(
        [first_half * cosines - second_half * sines, second_half * cosines + first_half * sines],
        axis=-1,
    )


def rope_tables(positions, head_width):
    half_size = head_width // 2
    inverse = ROPE_BASE ** (-(2.0 * jnp.arange(half_size, dtype=jnp.float32)) / head_width)
    angles = positions.astype(jnp.float32)[..., None] * inverse
    return (jnp.cos(angles)[..., None, :], jnp.sin(angles)[..., None, :])


def normed_rotary(raw_values, gain, cosines, sines):
    return rotate(rms_scale(raw_values, gain), cosines, sines)


def causal_mask(length):
    row_index = lax.broadcasted_iota(jnp.int32, (length, length), 0)
    col_index = lax.broadcasted_iota(jnp.int32, (length, length), 1)
    return row_index >= col_index


def attend_forward(queries, keys_in, values):
    length, head_total, head_width = queries.shape
    shared = keys_in.shape[1]
    grouped = queries.reshape(length, shared, head_total // shared, head_width)
    products = jnp.einsum("qkgd,tkd->kgqt", grouped, keys_in, preferred_element_type=jnp.float32)
    scores = jnp.where(causal_mask(length), products * head_width ** (-0.5), -1e30)
    peaks = jnp.max(scores, axis=-1, keepdims=True)
    lifted = jnp.exp(scores - peaks)
    totals = jnp.sum(lifted, axis=-1, keepdims=True)
    chances_low = (lifted / totals).astype(jnp.bfloat16)
    mixture = jnp.einsum("kgqt,tkd->qkgd", chances_low, values, preferred_element_type=jnp.float32)
    return (mixture.reshape(length, head_total, head_width), (peaks + jnp.log(totals))[..., 0])


def attend_backward(queries, keys_in, values, gate_logits, logsum, grad_gated):
    length, head_total, head_width = queries.shape
    shared = keys_in.shape[1]
    groups = head_total // shared
    scale = head_width ** (-0.5)
    grouped = queries.reshape(length, shared, groups, head_width)
    products = jnp.einsum("qkgd,tkd->kgqt", grouped, keys_in, preferred_element_type=jnp.float32)
    scores = jnp.where(causal_mask(length), products * scale, -1e30)
    chances = jnp.exp(scores - logsum[..., None])
    chances_low = chances.astype(jnp.bfloat16)
    mixture = jnp.einsum(
        "kgqt,tkd->qkgd", chances_low, values, preferred_element_type=jnp.float32
    ).reshape(length, head_total, head_width)
    opening = jax.nn.sigmoid(gate_logits.astype(jnp.float32))
    upstream = grad_gated.astype(jnp.float32)
    grad_mix = (upstream * opening).astype(jnp.bfloat16)
    grad_logits = (upstream * mixture * opening * (1.0 - opening)).astype(jnp.bfloat16)
    grad_grouped = grad_mix.reshape(length, shared, groups, head_width)
    grad_values = jnp.einsum(
        "kgqt,qkgd->tkd", chances_low, grad_grouped, preferred_element_type=jnp.float32
    ).astype(jnp.bfloat16)
    grad_chances = jnp.einsum(
        "qkgd,tkd->kgqt", grad_grouped, values, preferred_element_type=jnp.float32
    )
    centre = jnp.sum(grad_chances * chances, axis=-1, keepdims=True)
    grad_products = (chances * (grad_chances - centre) * scale).astype(jnp.bfloat16)
    grad_queries = (
        jnp.einsum("kgqt,tkd->qkgd", grad_products, keys_in, preferred_element_type=jnp.float32)
        .reshape(length, head_total, head_width)
        .astype(jnp.bfloat16)
    )
    grad_keys = jnp.einsum(
        "kgqt,qkgd->tkd", grad_products, grouped, preferred_element_type=jnp.float32
    ).astype(jnp.bfloat16)
    return (grad_queries, grad_keys, grad_values, grad_logits)


def partial_rows(left_side, right_sides):
    share_rows = left_side.shape[2] // lax.axis_size("fsdp")
    outcomes = []
    for right_side in right_sides:

        def contribution(start, count, operand=right_side):
            return jnp.einsum("slc,slw->cw", left_side, operand, preferred_element_type=jnp.float32)

        outcomes.append(
            lax.psum_scatter(
                contribution(jnp.int32(0), lax.axis_size("fsdp") * share_rows).astype(jnp.bfloat16),
                "fsdp",
                scatter_dimension=0,
                tiled=True,
            ).astype(jnp.float32)
        )
    return outcomes


def on_device(
    tokens,
    cotangent,
    positions,
    domain_ids,
    counts,
    loss_weight,
    domain_weights,
    q_weight,
    k_weight,
    v_weight,
    g_weight,
    o_weight,
    gate_weight,
    up_weight,
    down_weight,
    attn_gain,
    mlp_gain,
    q_gain,
    k_gain,
):
    seq_count, local_rows = (tokens.shape[0], tokens.shape[1])
    (
        query_full,
        key_full,
        value_full,
        logit_full,
        output_complete,
        gain_first,
        gain_query,
        gain_key,
    ) = (
        lax.all_gather(q_weight, "fsdp", axis=0, tiled=True),
        lax.all_gather(k_weight, "fsdp", axis=0, tiled=True),
        lax.all_gather(v_weight, "fsdp", axis=0, tiled=True),
        lax.all_gather(g_weight, "fsdp", axis=0, tiled=True),
        lax.all_gather(o_weight, "fsdp", axis=0, tiled=True),
        lax.all_gather(attn_gain, "fsdp", axis=0, tiled=True),
        lax.all_gather(q_gain, "fsdp", axis=0, tiled=True),
        lax.all_gather(k_gain, "fsdp", axis=0, tiled=True),
    )
    first_gain = gain_first.astype(jnp.float32)
    query_norm_scale = gain_query.astype(jnp.float32)
    key_gain = gain_key.astype(jnp.float32)
    inputs = tokens.astype(jnp.float32)
    cosines, sines = rope_tables(positions, HEAD)
    first_low = rms_scale(inputs, first_gain).astype(jnp.bfloat16)
    query_unnormed = jnp.einsum(
        "slc,cw->slw", first_low, query_full, preferred_element_type=jnp.float32
    ).reshape(seq_count, local_rows, -1, HEAD)
    key_raw = jnp.einsum(
        "slc,cw->slw", first_low, key_full, preferred_element_type=jnp.float32
    ).reshape(seq_count, local_rows, -1, HEAD)
    query_send = normed_rotary(query_unnormed, query_norm_scale, cosines, sines).astype(
        jnp.bfloat16
    )
    key_send = normed_rotary(key_raw, key_gain, cosines, sines).astype(jnp.bfloat16)
    value_send = (
        jnp.einsum("slc,cw->slw", first_low, value_full, preferred_element_type=jnp.float32)
        .astype(jnp.bfloat16)
        .reshape(seq_count, local_rows, -1, HEAD)
    )
    logit_send = (
        jnp.einsum("slc,cw->slw", first_low, logit_full, preferred_element_type=jnp.float32)
        .astype(jnp.bfloat16)
        .reshape(seq_count, local_rows, -1, HEAD)
    )
    query_heads, key_heads, value_heads, logit_heads = (
        lax.all_to_all(query_send, "sp", split_axis=2, concat_axis=1, tiled=True),
        lax.all_to_all(key_send, "sp", split_axis=2, concat_axis=1, tiled=True),
        lax.all_to_all(value_send, "sp", split_axis=2, concat_axis=1, tiled=True),
        lax.all_to_all(logit_send, "sp", split_axis=2, concat_axis=1, tiled=True),
    )
    mixture, logsum = lax.map(
        lambda pieces: attend_forward(pieces[0], pieces[1], pieces[2]),
        (query_heads, key_heads, value_heads),
    )
    opening = jax.nn.sigmoid(logit_heads.astype(jnp.float32))
    gated_heads = (mixture * opening).astype(jnp.bfloat16)
    gated_rows = lax.all_to_all(gated_heads, "sp", split_axis=1, concat_axis=2, tiled=True).reshape(
        seq_count, local_rows, -1
    )
    middle = inputs + jnp.einsum(
        "slc,cw->slw", gated_rows, output_complete, preferred_element_type=jnp.float32
    )
    gate_full, up_full, down_full, gain_second = (
        lax.all_gather(gate_weight, "fsdp", axis=0, tiled=True),
        lax.all_gather(up_weight, "fsdp", axis=0, tiled=True),
        lax.all_gather(down_weight, "fsdp", axis=0, tiled=True),
        lax.all_gather(mlp_gain, "fsdp", axis=0, tiled=True),
    )
    second_gain = gain_second.astype(jnp.float32)
    second_low = rms_scale(middle, second_gain).astype(jnp.bfloat16)
    gate_act = jnp.einsum("slc,cf->slf", second_low, gate_full, preferred_element_type=jnp.float32)
    up_act = jnp.einsum("slc,cf->slf", second_low, up_full, preferred_element_type=jnp.float32)
    hidden_low = (jax.nn.silu(gate_act) * up_act).astype(jnp.bfloat16)
    block_out = (
        middle
        + jnp.einsum("slf,fc->slc", hidden_low, down_full, preferred_element_type=jnp.float32)
    ).astype(jnp.bfloat16)
    onehot_table = (
        domain_ids[:, None] == jnp.arange(domain_weights.shape[0], dtype=jnp.int32)[None, :]
    ).astype(jnp.float32)
    domain_scale = jnp.sum(onehot_table * domain_weights[None, :], axis=1)
    seq_scale = loss_weight * domain_scale * SEQ_LEN / counts.astype(jnp.float32)
    upstream = cotangent.astype(jnp.float32) * seq_scale[:, None, None]
    upstream_low = upstream.astype(jnp.bfloat16)
    grad_hidden = jnp.einsum(
        "slc,fc->slf", upstream_low, down_full, preferred_element_type=jnp.float32
    )
    _, silu_pull = jax.vjp(lambda gate_in, up_in: jax.nn.silu(gate_in) * up_in, gate_act, up_act)
    grad_gate_act, grad_up_act = silu_pull(grad_hidden)
    grad_gate_low = grad_gate_act.astype(jnp.bfloat16)
    grad_up_low = grad_up_act.astype(jnp.bfloat16)
    grad_second = jnp.einsum(
        "slf,cf->slc", grad_gate_low, gate_full, preferred_element_type=jnp.float32
    ) + jnp.einsum("slf,cf->slc", grad_up_low, up_full, preferred_element_type=jnp.float32)
    _, second_pull = jax.vjp(rms_scale, middle, second_gain)
    middle_norm_gradient, grad_second_gain = second_pull(grad_second)
    grad_middle = upstream + middle_norm_gradient
    attention_gradient_reduced = grad_middle.astype(jnp.bfloat16)
    grad_gated_rows = (
        jnp.einsum(
            "muk,rk->mur",
            attention_gradient_reduced,
            output_complete,
            preferred_element_type=jnp.float32,
        )
        .astype(jnp.bfloat16)
        .reshape(seq_count, local_rows, -1, HEAD)
    )
    grad_gated_heads = lax.all_to_all(
        grad_gated_rows, "sp", split_axis=2, concat_axis=1, tiled=True
    )
    head_query, head_key, head_value, head_logit = lax.map(
        lambda pieces: attend_backward(
            pieces[0], pieces[1], pieces[2], pieces[3], pieces[4], pieces[5]
        ),
        (query_heads, key_heads, value_heads, logit_heads, logsum, grad_gated_heads),
    )
    grad_query, grad_key, grad_value, grad_logit = (
        lax.all_to_all(head_query, "sp", split_axis=1, concat_axis=2, tiled=True),
        lax.all_to_all(head_key, "sp", split_axis=1, concat_axis=2, tiled=True),
        lax.all_to_all(head_value, "sp", split_axis=1, concat_axis=2, tiled=True),
        lax.all_to_all(head_logit, "sp", split_axis=1, concat_axis=2, tiled=True),
    )
    _, query_pull = jax.vjp(
        lambda raw_in, gain_in: normed_rotary(raw_in, gain_in, cosines, sines),
        query_unnormed,
        query_norm_scale,
    )
    grad_query_raw, grad_query_gain = query_pull(grad_query.astype(jnp.float32))
    _, key_pull = jax.vjp(
        lambda raw_in, gain_in: normed_rotary(raw_in, gain_in, cosines, sines), key_raw, key_gain
    )
    grad_key_raw, grad_key_gain = key_pull(grad_key.astype(jnp.float32))
    rows_query = grad_query_raw.astype(jnp.bfloat16).reshape(seq_count, local_rows, -1)
    rows_key = grad_key_raw.astype(jnp.bfloat16).reshape(seq_count, local_rows, -1)
    rows_value = grad_value.reshape(seq_count, local_rows, -1)
    rows_logit = grad_logit.reshape(seq_count, local_rows, -1)
    grad_first = jnp.einsum(
        "slw,cw->slc", rows_query, query_full, preferred_element_type=jnp.float32
    )
    grad_first = grad_first + jnp.einsum(
        "slw,cw->slc", rows_key, key_full, preferred_element_type=jnp.float32
    )
    grad_first = grad_first + jnp.einsum(
        "slw,cw->slc", rows_value, value_full, preferred_element_type=jnp.float32
    )
    grad_first = grad_first + jnp.einsum(
        "slw,cw->slc", rows_logit, logit_full, preferred_element_type=jnp.float32
    )
    _, first_pull = jax.vjp(rms_scale, inputs, first_gain)
    grad_input_norm, grad_first_gain = first_pull(grad_first)
    input_grad = grad_middle + grad_input_norm
    pairings = (
        (first_low, (rows_query, rows_key, rows_value, rows_logit)),
        (gated_rows, (attention_gradient_reduced,)),
        (second_low, (grad_gate_low, grad_up_low)),
        (hidden_low, (upstream_low,)),
    )
    shares = []
    for left_side, right_sides in pairings:
        shares.extend(partial_rows(left_side, right_sides))
    weight_grads = (
        lax.psum(shares[0].astype(jnp.bfloat16), "sp").astype(jnp.float32),
        lax.psum(shares[1].astype(jnp.bfloat16), "sp").astype(jnp.float32),
        lax.psum(shares[2].astype(jnp.bfloat16), "sp").astype(jnp.float32),
        lax.psum(shares[3].astype(jnp.bfloat16), "sp").astype(jnp.float32),
        lax.psum(shares[4].astype(jnp.bfloat16), "sp").astype(jnp.float32),
        lax.psum(shares[5].astype(jnp.bfloat16), "sp").astype(jnp.float32),
        lax.psum(shares[6].astype(jnp.bfloat16), "sp").astype(jnp.float32),
        lax.psum(shares[7].astype(jnp.bfloat16), "sp").astype(jnp.float32),
    )
    gain_totals = lax.psum(
        (grad_first_gain, grad_second_gain, grad_query_gain, grad_key_gain), ("sp", "fsdp")
    )
    fsdp_rank = lax.axis_index("fsdp")
    fsdp_count = lax.axis_size("fsdp")

    def own_share(full_grad):
        share_len = full_grad.shape[0] // fsdp_count
        return lax.dynamic_slice_in_dim(full_grad, fsdp_rank * share_len, share_len, 0)

    return (
        block_out,
        input_grad,
        weight_grads[0],
        weight_grads[1],
        weight_grads[2],
        weight_grads[3],
        weight_grads[4],
        weight_grads[5],
        weight_grads[6],
        weight_grads[7],
        own_share(gain_totals[0]),
        own_share(gain_totals[1]),
        own_share(gain_totals[2]),
        own_share(gain_totals[3]),
    )


def solution(mesh):
    return jax.shard_map(
        on_device,
        mesh=mesh,
        in_specs=(
            P("fsdp", "sp", None),
            P("fsdp", "sp", None),
            P("fsdp", "sp"),
            P("fsdp"),
            P("fsdp"),
            P("fsdp"),
            P(),
            P("fsdp", None),
            P("fsdp", None),
            P("fsdp", None),
            P("fsdp", None),
            P("fsdp", None),
            P("fsdp", None),
            P("fsdp", None),
            P("fsdp", None),
            P("fsdp"),
            P("fsdp"),
            P("fsdp"),
            P("fsdp"),
        ),
        out_specs=(
            P("fsdp", "sp", None),
            P("fsdp", "sp", None),
            P("fsdp", None),
            P("fsdp", None),
            P("fsdp", None),
            P("fsdp", None),
            P("fsdp", None),
            P("fsdp", None),
            P("fsdp", None),
            P("fsdp", None),
            P("fsdp"),
            P("fsdp"),
            P("fsdp"),
            P("fsdp"),
        ),
        check_vma=False,
    )
```

profile of v0, /device:TPU:0, one launch (start us, length us, event | category | flops | bytes accessed | tf_op | source)
XLA Modules:
  0.0 2562.2 jit_solution(18217452166362948088)
XLA Ops:
  43.3 16.5 all-gather.13.cloned.1.call-done
  70.2 37.2 %all-gather.11.cloned.1.call-done = bf16[2048,1024]{1,0:T(8,128)(2,1)} async-done(((bf16[256,1024]{1,0:T(8,128)(2,1)}), bf16[2048,1024]{1,0:T(8,128)(2,1)}) %all-gather.11.cloned.1.call-update) | async-done | bytes 4194320 | tf_op jit(solution)/shard_map/all_gather | solution.py:149
  111.8 77.9 %all-gather.15.cloned.1.call-done = bf16[2048,2048]{1,0:T(8,128)(2,1)} async-done(((bf16[256,2048]{1,0:T(8,128)(2,1)}), bf16[2048,2048]{1,0:T(8,128)(2,1)}) %all-gather.15.cloned.1.call-update) | async-done | bytes 8388624 | tf_op jit(solution)/shard_map/all_gather | solution.py:147
  223.6 48.2 %all-gather.17.cloned.1.call-done = bf16[2048,2048]{1,0:T(8,128)(2,1)} async-done(((bf16[256,2048]{1,0:T(8,128)(2,1)}), bf16[2048,2048]{1,0:T(8,128)(2,1)}) %all-gather.17.cloned.1.call-update) | async-done | bytes 8388624 | tf_op jit(solution)/shard_map/all_gather | solution.py:150
  336.2 17.8 all-gather.19.cloned.1.call-done
  361.6 212.3 %all-gather.21.cloned.1.call-done = bf16[2048,6144]{1,0:T(8,128)(2,1)} async-done(((bf16[256,6144]{1,0:T(8,128)(2,1)}), bf16[2048,6144]{1,0:T(8,128)(2,1)}) %all-gather.21.cloned.1.call-update) | async-done | bytes 25165840 | tf_op jit(solution)/shard_map/all_gather | solution.py:201
  573.9 15.2 fusion.79
  589.1 204.6 %all-gather.23.cloned.1.call-done = bf16[2048,6144]{1,0:T(8,128)(2,1)} async-done(((bf16[256,6144]{1,0:T(8,128)(2,1)}), bf16[2048,6144]{1,0:T(8,128)(2,1)}) %all-gather.23.cloned.1.call-update) | async-done | bytes 25165840 | tf_op jit(solution)/shard_map/all_gather | solution.py:202
  793.6 15.1 fusion.80
  808.8 204.6 %all-gather.25.cloned.1.call-done = bf16[6144,2048]{1,0:T(8,128)(2,1)} async-done(((bf16[768,2048]{1,0:T(8,128)(2,1)}), bf16[6144,2048]{1,0:T(8,128)(2,1)}) %all-gather.25.cloned.1.call-update) | async-done | bytes 25165840 | tf_op jit(solution)/shard_map/all_gather | solution.py:203
  1013.4 20.5 multiply_convert_fusion
  1047.5 14.8 fusion.29
  1109.8 24.5 fusion.47
  1197.5 24.0 fusion.32
  1222.3 15.1 all_to_all.128
  1331.9 14.9 reduce-scatter.17.cloned.1.call-done
  1346.8 90.2 %reduce-scatter.9.cloned.1.call-done = bf16[256,2048]{1,0:T(8,128)(2,1)} async-done(((bf16[2048,2048]{1,0:T(8,128)(2,1)}), bf16[256,2048]{1,0:T(8,128)(2,1)}) %reduce-scatter.9.cloned.1.call-update) | async-done | bytes 1048592 | tf_op jit(solution)/shard_map/reduce_scatter | solution.py:105
  1436.9 90.3 %reduce-scatter.15.cloned.1.call-done = bf16[256,2048]{1,0:T(8,128)(2,1)} async-done(((bf16[2048,2048]{1,0:T(8,128)(2,1)}), bf16[256,2048]{1,0:T(8,128)(2,1)}) %reduce-scatter.15.cloned.1.call-update) | async-done | bytes 1048592 | tf_op jit(solution)/shard_map/reduce_scatter | solution.py:105
  1527.2 247.8 %reduce-scatter.19.cloned.1.call-done = bf16[256,6144]{1,0:T(8,128)(2,1)} async-done(((bf16[2048,6144]{1,0:T(8,128)(2,1)}), bf16[256,6144]{1,0:T(8,128)(2,1)}) %reduce-scatter.19.cloned.1.call-update) | async-done | bytes 3145744 | tf_op jit(solution)/shard_map/reduce_scatter | solution.py:105
  1775.0 247.8 %reduce-scatter.21.cloned.1.call-done = bf16[256,6144]{1,0:T(8,128)(2,1)} async-done(((bf16[2048,6144]{1,0:T(8,128)(2,1)}), bf16[256,6144]{1,0:T(8,128)(2,1)}) %reduce-scatter.21.cloned.1.call-update) | async-done | bytes 3145744 | tf_op jit(solution)/shard_map/reduce_scatter | solution.py:105
  2022.7 247.8 %reduce-scatter.23.cloned.1.call-done = bf16[768,2048]{1,0:T(8,128)(2,1)} async-done(((bf16[6144,2048]{1,0:T(8,128)(2,1)}), bf16[768,2048]{1,0:T(8,128)(2,1)}) %reduce-scatter.23.cloned.1.call-update) | async-done | bytes 3145744 | tf_op jit(solution)/shard_map/reduce_scatter | solution.py:105
  2272.1 14.7 fusion.15
  2301.3 38.8 %all-reduce.6 = (f32[2048]{0:T(1024)S(1)}, f32[2048]{0:T(1024)S(1)}, f32[128]{0:T(128)S(1)}, f32[128]{0:T(128)S(1)}) all-reduce(f32[2048]{0:T(1024)S(1)} %get-tuple-element.69, f32[2048]{0:T(1024)S(1)} %copy-done.55, f32[128]{0:T(128)S(1)} %get-tuple-element.54, ...), channel_id=1, replica_groups=mesh['sp'=4,'fsdp'=8] {'sp','fsdp'}, use_global_device_ids=true, to_apply=%region_29.30 | all-reduce | flops 4352 | bytes 34816 | tf_op jit(solution)/shard_map/psum | solution.py:309
  2346.1 190.4 %all-reduce.11.cloned.1.call-done = (bf16[256,2048]{1,0:T(8,128)(2,1)}, bf16[256,1024]{1,0:T(8,128)(2,1)}, bf16[256,1024]{1,0:T(8,128)(2,1)}, bf16[256,2048]{1,0...) async-done(((bf16[256,2048]{1,0:T(8,128)(2,1)}, bf16[256,1024]{1,0:T(8,128)(2,1)}, ...) | async-done | bytes 13631504 | tf_op jit(solution)/shard_map/psum | solution.py:300
  (314 shorter events, 412.6 us)
Async XLA Ops:
  7.2 52.7 %all-gather.13.cloned.1.call-start = ((), (), s32[]{:S(2)}) async-start(), calls=%async_computation.19 | async-start | bytes 4718592 | tf_op jit(solution)/shard_map/all_gather | solution.py:148
  7.9 99.4 %all-gather.11.cloned.1.call-start = ((), (), s32[]{:S(2)}) async-start(), calls=%async_computation.18 | async-start | bytes 4718592 | tf_op jit(solution)/shard_map/all_gather | solution.py:149
  8.7 181.1 %all-gather.15.cloned.1.call-start = ((), (), s32[]{:S(2)}) async-start(), calls=%async_computation.20 | async-start | bytes 9437184 | tf_op jit(solution)/shard_map/all_gather | solution.py:147
  9.4 262.4 %all-gather.17.cloned.1.call-start = ((), (), s32[]{:S(2)}) async-start(), calls=%async_computation.21 | async-start | bytes 9437184 | tf_op jit(solution)/shard_map/all_gather | solution.py:150
  10.0 344.0 %all-gather.19.cloned.1.call-start = ((), (), s32[]{:S(2)}) async-start(), calls=%async_computation.22 | async-start | bytes 9437184 | tf_op jit(solution)/shard_map/all_gather | solution.py:151
  10.6 563.3 %all-gather.21.cloned.1.call-start = ((), (), s32[]{:S(2)}) async-start(), calls=%async_computation.23 | async-start | bytes 28311552 | tf_op jit(solution)/shard_map/all_gather | solution.py:201
  11.2 782.4 %all-gather.23.cloned.1.call-start = ((), (), s32[]{:S(2)}) async-start(), calls=%async_computation.24 | async-start | bytes 28311552 | tf_op jit(solution)/shard_map/all_gather | solution.py:202
  12.0 1001.4 %all-gather.25.cloned.1.call-start = ((), (), s32[]{:S(2)}) async-start(), calls=%async_computation.25 | async-start | bytes 28311552 | tf_op jit(solution)/shard_map/all_gather | solution.py:203
  66.0 135.3 %all-to-all-start.1 = ((bf16[1,256,8,128]{3,1,0,2:T(8,128)(2,1)}), bf16[1,256,8,128]{3,1,0,2:T(8,128)(2,1)}, u32[]{:S(2)}, u32[]{:S(2)}) async-start(bf16[1,256,8,128]{3,1,0,2:T(8,128)(2,1)} %copy.257), calls=%async_computation.1 | async-start | bytes 1048576 | tf_op jit(solution)/shard_map/all_to_all | solution.py:184
  201.3 13.0 all-to-all-start
  214.2 64.9 %all-to-all-start.2 = ((bf16[1,256,16,128]{3,1,0,2:T(8,128)(2,1)}), bf16[1,256,16,128]{3,1,0,2:T(8,128)(2,1)S(1)}, u32[]{:S(2)}, u32[]{:S(2)}) async-start(bf16[1,256,16,128]{3,1,0,2:T(8,128)(2,1)} %copy.261), calls=%async_computation.2 | async-start | bytes 2097152 | tf_op jit(solution)/shard_map/all_to_all | solution.py:183
  279.1 33.0 %all-to-all-start.3 = ((bf16[1,256,16,128]{3,1,0,2:T(8,128)(2,1)}), bf16[1,256,16,128]{3,1,0,2:T(8,128)(2,1)S(1)}, u32[]{:S(2)}, u32[]{:S(2)}) async-start(bf16[1,256,16,128]{3,1,0,2:T(8,128)(2,1)} %copy.264), calls=%async_computation.3 | async-start | bytes 2097152 | tf_op jit(solution)/shard_map/all_to_all | solution.py:186
  317.0 17.8 all-to-all-start.4
  360.1 687.4 %copy-start.5 = (f32[1,256,2048]{2,1,0:T(8,128)}, f32[1,256,2048]{2,1,0:T(8,128)S(1)}, u32[]{:S(2)}) copy-start(f32[1,256,2048]{2,1,0:T(8,128)S(1)} %get-tuple-element.103) | copy-start | bytes 6291460
  1073.5 18.7 all-to-all-start.5
  1077.8 254.1 %reduce-scatter.11.cloned.1.call-start = ((), (), s32[]{:S(2)}) async-start(), calls=%async_computation.27 | async-start | bytes 4718592 | tf_op jit(solution)/shard_map/reduce_scatter | solution.py:105
  1158.9 173.0 %reduce-scatter.13.cloned.1.call-start = ((), (), s32[]{:S(2)}) async-start(), calls=%async_computation.28 | async-start | bytes 4718592 | tf_op jit(solution)/shard_map/reduce_scatter | solution.py:105
  1189.5 157.2 %reduce-scatter.17.cloned.1.call-start = ((), (), s32[]{:S(2)}) async-start(), calls=%async_computation.30 | async-start | bytes 9437184 | tf_op jit(solution)/shard_map/reduce_scatter | solution.py:105
  1196.5 240.4 %reduce-scatter.9.cloned.1.call-start = ((), (), s32[]{:S(2)}) async-start(), calls=%async_computation.26 | async-start | bytes 9437184 | tf_op jit(solution)/shard_map/reduce_scatter | solution.py:105
  1250.4 276.8 %reduce-scatter.15.cloned.1.call-start = ((), (), s32[]{:S(2)}) async-start(), calls=%async_computation.29 | async-start | bytes 9437184 | tf_op jit(solution)/shard_map/reduce_scatter | solution.py:105
  1287.1 487.8 %reduce-scatter.19.cloned.1.call-start = ((), (), s32[]{:S(2)}) async-start(), calls=%async_computation.31 | async-start | bytes 28311552 | tf_op jit(solution)/shard_map/reduce_scatter | solution.py:105
  1302.2 720.5 %reduce-scatter.21.cloned.1.call-start = ((), (), s32[]{:S(2)}) async-start(), calls=%async_computation.32 | async-start | bytes 28311552 | tf_op jit(solution)/shard_map/reduce_scatter | solution.py:105
  1316.4 954.1 %reduce-scatter.23.cloned.1.call-start = ((), (), s32[]{:S(2)}) async-start(), calls=%async_computation.33 | async-start | bytes 28311552 | tf_op jit(solution)/shard_map/reduce_scatter | solution.py:105
  1331.5 1205.0 %all-reduce.11.cloned.1.call-start = ((), (), s32[]{:S(2)}) async-start(), calls=%async_computation.34 | async-start | bytes 27262976 | tf_op jit(solution)/shard_map/psum | solution.py:300
  (68 other events, 1645.7 us)
Sparse Core Ops, SparseCore 0:
  9.6 50.1 all-gather.12
  61.4 45.8 all-gather.10
  109.0 80.7 all-gather.14
  191.2 80.5 all-gather.16
  273.3 80.6 all-gather.18
  355.5 218.3 all-gather.20
  575.5 218.0 all-gather.22
  795.3 218.0 all-gather.24
  1159.0 46.7 reduce-scatter.10
  1208.5 48.1 reduce-scatter.12
  1259.0 87.7 reduce-scatter.16
  1348.9 87.9 reduce-scatter.8
  1439.2 87.9 reduce-scatter.14
  1529.4 245.5 reduce-scatter.18
  1777.2 245.5 reduce-scatter.20
  2024.9 245.5 reduce-scatter.22
  2275.0 261.3 all-reduce.10
where the time goes:
time: 2570 us; the launch traced here: 2560 us
  waiting for transfers between devices  1970 us (77%)
  matrix products  303 us (12%)
  blocking collectives  129 us (5%)
  local copies, waits for them, and re-layouts  58.4 us (2%)
  other arithmetic  56.9 us (2%)
    reduce_scatter x8, waiting for transfers between devices, partial_rows(): lax.psum_scatter(contribution(jnp.int32(0), lax.axis_size('fsdp') * share...  939 us
    all_gather x1, waiting for transfers between devices, on_device(): lax.all_gather(gate_weight, 'fsdp', axis=0, tiled=True)  212 us
    all_gather x1, waiting for transfers between devices, on_device(): lax.all_gather(down_weight, 'fsdp', axis=0, tiled=True)  205 us
    all_gather x1, waiting for transfers between devices, on_device(): lax.all_gather(up_weight, 'fsdp', axis=0, tiled=True)  205 us
    psum x1, waiting for transfers between devices, on_device(): lax.psum(shares[0].astype(jnp.bfloat16), 'sp').astype(jnp.float32)  190 us
    all_gather x1, waiting for transfers between devices, on_device(): lax.all_gather(q_weight, 'fsdp', axis=0, tiled=True)  77.9 us
    dot_general x8, matrix products, contribution(): jnp.einsum('slc,slw->cw', left_side, operand, preferred_element_type=jnp....  67.9 us
  transfers between devices with their start and end apart: 23, of which 18 were waited for; matrix products, arithmetic and copies ran while one was open for 11% of the time, Pallas kernels for 0%

commit v1 on v0

v1 whole, which is shorter than its diff:
```python
import functools

import jax
import jax.numpy as jnp
from jax import lax
from jax.experimental import pallas as pl
from jax.experimental.pallas import tpu as pltpu
from jax.sharding import PartitionSpec as P

HEAD = 128
HALF = HEAD // 2
SEQ_LEN = 1024
EPS = 1e-06
ROPE_BASE = 1000000.0
SCALE = HEAD ** (-0.5)
LOG2E = 1.4426950408889634
VMEM_LIMIT = 56 * 1024 * 1024
NT = (((1,), (1,)), ((), ()))
NN = (((1,), (0,)), ((), ()))
TN = (((0,), (0,)), ((), ()))
F32 = jnp.float32
BF16 = jnp.bfloat16


def mm(left, right, dims=NN):
    return lax.dot_general(left, right, dims, preferred_element_type=F32)


def head_norm(raw):
    return lax.rsqrt(jnp.mean(raw * raw, axis=-1, keepdims=True) + EPS)


def turn(values, cosines, sines):
    return values * cosines + pltpu.roll(values, HALF, 1) * sines


def turn_back(values, cosines, sines):
    return values * cosines - pltpu.roll(values, HALF, 1) * sines


def norm_turn(raw, gain, cosines, sines):
    return turn(raw * head_norm(raw) * gain, cosines, sines).astype(BF16)


def norm_turn_back(raw, gain, grad, cosines, sines):
    back = turn_back(grad, cosines, sines)
    scale = head_norm(raw)
    pulled = back * gain
    inner = jnp.mean(raw * pulled, axis=-1, keepdims=True)
    gain_part = jnp.sum(raw * scale * back, axis=0, keepdims=True)
    return scale * pulled - raw * (scale * scale * scale * inner), gain_part


def diagonal_mask(rows, groups):
    keys = lax.broadcasted_iota(jnp.int32, (rows, groups * rows), 0)
    places = lax.broadcasted_iota(jnp.int32, (rows, groups * rows), 1)
    return keys <= lax.rem(places, rows)


def row_block(block, rank, rows):
    return pl.ds(pl.multiple_of(jnp.bitwise_xor(block, rank) * rows, rows), rows)


def attend_fwd_kernel(
    blocks, rows, groups,
    rank_ref, q_ref, k_ref, v_ref, g_ref, cos_ref, sin_ref, qg_ref, kg_ref,
    gated_ref, mix_ref, lse_ref, keys, vals_t,
):
    rank = rank_ref[0]
    factor = SCALE * LOG2E
    for a in range(blocks):
        place = row_block(a, rank, rows)
        here = slice(a * rows, (a + 1) * rows)
        keys[here, :] = norm_turn(k_ref[place, :], kg_ref[...], cos_ref[place, :], sin_ref[place, :])
        vals_t[:, here] = v_ref[place, :].T.astype(BF16)
    mask = diagonal_mask(rows, groups)
    for a in range(blocks):
        place = row_block(a, rank, rows)
        cosines, sines = cos_ref[place, :], sin_ref[place, :]
        queries = jnp.concatenate(
            [
                norm_turn(q_ref[place, h * HEAD : (h + 1) * HEAD], qg_ref[...], cosines, sines)
                for h in range(groups)
            ],
            axis=0,
        )
        low, high = a * rows, (a + 1) * rows
        near = jnp.where(mask, mm(keys[low:high, :], queries, NT), -1e30)
        peak = jnp.max(near, axis=0, keepdims=True)
        if a:
            far = mm(keys[:low, :], queries, NT)
            peak = jnp.maximum(peak, jnp.max(far, axis=0, keepdims=True))
        near = jnp.exp2((near - peak) * factor)
        total = jnp.sum(near, axis=0, keepdims=True)
        if a:
            far = jnp.exp2((far - peak) * factor)
            total = total + jnp.sum(far, axis=0, keepdims=True)
        inverse = 1.0 / total
        mix_t = mm(vals_t[:, low:high], (near * inverse).astype(BF16))
        if a:
            mix_t = mix_t + mm(vals_t[:, :low], (far * inverse).astype(BF16))
        mix = mix_t.T
        for h in range(groups):
            cols = slice(h * HEAD, (h + 1) * HEAD)
            part = mix[h * rows : (h + 1) * rows, :]
            opening = jax.nn.sigmoid(g_ref[place, cols].astype(BF16).astype(F32))
            mix_ref[place, cols] = part
            gated_ref[place, cols] = (part * opening).astype(BF16)
        lse_ref[0, a : a + 1, :] = peak * factor + jnp.log2(total)


def attend_bwd_kernel(
    blocks, rows, groups, kv_local,
    rank_ref, q_ref, k_ref, v_ref, g_ref, cos_ref, sin_ref, qg_ref, kg_ref, mix_ref, lse_ref, up_ref,
    grad_ref, qgain_ref, kgain_ref, keys, keys_t, vals, dkeys, dvals,
):
    rank = rank_ref[0]
    step = pl.program_id(0)
    factor = SCALE * LOG2E
    width = groups * HEAD

    @pl.when(step == 0)
    def _():
        qgain_ref[...] = jnp.zeros_like(qgain_ref)
        kgain_ref[...] = jnp.zeros_like(kgain_ref)

    for a in range(blocks):
        place = row_block(a, rank, rows)
        here = slice(a * rows, (a + 1) * rows)
        block = norm_turn(k_ref[place, :], kg_ref[...], cos_ref[place, :], sin_ref[place, :])
        keys[here, :] = block
        keys_t[:, here] = block.astype(F32).T.astype(BF16)
        vals[here, :] = v_ref[place, :].astype(BF16)
    mask = diagonal_mask(rows, groups)
    qgain = jnp.zeros((1, HEAD), F32)
    for a in reversed(range(blocks)):
        place = row_block(a, rank, rows)
        cosines, sines = cos_ref[place, :], sin_ref[place, :]
        queries, grads = [], []
        for h in range(groups):
            cols = slice(h * HEAD, (h + 1) * HEAD)
            queries.append(norm_turn(q_ref[place, cols], qg_ref[...], cosines, sines))
            upstream = up_ref[place, cols].astype(F32)
            opening = jax.nn.sigmoid(g_ref[place, cols].astype(BF16).astype(F32))
            opened = upstream * opening
            grads.append(opened.astype(BF16))
            grad_ref[
                place, pl.ds((kv_local * (groups + 2)) * HEAD + step * width + h * HEAD, HEAD)
            ] = (opened * mix_ref[place, cols] * (1.0 - opening)).astype(BF16)
        queries = jnp.concatenate(queries, axis=0)
        grads = jnp.concatenate(grads, axis=0)
        lse = lse_ref[0, a : a + 1, :]
        low, high = a * rows, (a + 1) * rows
        spans = [(low, high)] + ([(0, low)] if a else [])
        chances, grad_chances = [], []
        centre = jnp.zeros((1, groups * rows), F32)
        for start, stop in spans:
            part = jnp.exp2(mm(keys[start:stop, :], queries, NT) * factor - lse)
            if start == low:
                part = jnp.where(mask, part, 0.0)
            pull = mm(vals[start:stop, :], grads, NT)
            centre = centre + jnp.sum(part * pull, axis=0, keepdims=True)
            chances.append(part)
            grad_chances.append(pull)
        dq_t = jnp.zeros((HEAD, groups * rows), F32)
        for (start, stop), part, pull in zip(spans, chances, grad_chances):
            grad_products = (part * (pull - centre) * SCALE).astype(BF16)
            dval = mm(part.astype(BF16), grads)
            dkey = mm(grad_products, queries)
            if a == blocks - 1:
                dvals[start:stop, :] = dval
                dkeys[start:stop, :] = dkey
            else:
                dvals[start:stop, :] += dval
                dkeys[start:stop, :] += dkey
            dq_t = dq_t + mm(keys_t[:, start:stop], grad_products)
        dq = dq_t.T
        for h in range(groups):
            grad = dq[h * rows : (h + 1) * rows, :].astype(BF16).astype(F32)
            cols = slice(h * HEAD, (h + 1) * HEAD)
            raw, gain_part = norm_turn_back(q_ref[place, cols], qg_ref[...], grad, cosines, sines)
            grad_ref[place, pl.ds(step * width + h * HEAD, HEAD)] = raw.astype(BF16)
            qgain = qgain + gain_part
    kgain = jnp.zeros((1, HEAD), F32)
    for a in range(blocks):
        place = row_block(a, rank, rows)
        here = slice(a * rows, (a + 1) * rows)
        grad = dkeys[here, :].astype(BF16).astype(F32)
        raw, gain_part = norm_turn_back(
            k_ref[place, :], kg_ref[...], grad, cos_ref[place, :], sin_ref[place, :]
        )
        kgain = kgain + gain_part
        grad_ref[place, pl.ds(kv_local * width + step * HEAD, HEAD)] = raw.astype(BF16)
        grad_ref[place, pl.ds(kv_local * (width + HEAD) + step * HEAD, HEAD)] = dvals[
            here, :
        ].astype(BF16)
    qgain_ref[...] += qgain
    kgain_ref[...] += kgain


def attention_specs(length, groups, kv_local):
    width = groups * HEAD
    return [
        pl.BlockSpec((length, width), lambda g, r: (0, g)),
        pl.BlockSpec((length, HEAD), lambda g, r: (0, kv_local * groups + g)),
        pl.BlockSpec((length, HEAD), lambda g, r: (0, kv_local * (groups + 1) + g)),
        pl.BlockSpec((length, width), lambda g, r: (0, kv_local * (groups + 2) // groups + g)),
        pl.BlockSpec((length, HEAD), lambda g, r: (0, 0)),
        pl.BlockSpec((length, HEAD), lambda g, r: (0, 0)),
        pl.BlockSpec((1, HEAD), lambda g, r: (0, 0)),
        pl.BlockSpec((1, HEAD), lambda g, r: (0, 0)),
    ]


def attend_forward(rank, raw, cosines, sines, q_gain, k_gain, blocks, groups, kv_local):
    length = raw.shape[0]
    rows = length // blocks
    width = groups * HEAD
    flops = 4 * kv_local * groups * length * length * HEAD * (blocks + 1) // (2 * blocks)
    return pl.pallas_call(
        functools.partial(attend_fwd_kernel, blocks, rows, groups),
        grid_spec=pltpu.PrefetchScalarGridSpec(
            num_scalar_prefetch=1,
            grid=(kv_local,),
            in_specs=attention_specs(length, groups, kv_local),
            out_specs=[
                pl.BlockSpec((length, width), lambda g, r: (0, g)),
                pl.BlockSpec((length, width), lambda g, r: (0, g)),
                pl.BlockSpec((1, blocks, groups * rows), lambda g, r: (g, 0, 0)),
            ],
            scratch_shapes=[pltpu.VMEM((length, HEAD), BF16), pltpu.VMEM((HEAD, length), BF16)],
        ),
        out_shape=[
            jax.ShapeDtypeStruct((length, kv_local * width), BF16),
            jax.ShapeDtypeStruct((length, kv_local * width), F32),
            jax.ShapeDtypeStruct((kv_local, blocks, groups * rows), F32),
        ],
        compiler_params=pltpu.CompilerParams(
            dimension_semantics=("arbitrary",), vmem_limit_bytes=VMEM_LIMIT
        ),
        cost_estimate=pl.CostEstimate(
            flops=4 * flops,
            bytes_accessed=raw.size * 4 + length * kv_local * width * 6,
            transcendentals=kv_local * groups * length * length // 2,
        ),
        name="attend_forward",
    )(rank, raw, raw, raw, raw, cosines, sines, q_gain, k_gain)


def attend_backward(
    rank, raw, cosines, sines, q_gain, k_gain, mix, lse, upstream, blocks, groups, kv_local
):
    length = raw.shape[0]
    rows = length // blocks
    width = groups * HEAD
    flops = 10 * kv_local * groups * length * length * HEAD * (blocks + 1) // (2 * blocks)
    return pl.pallas_call(
        functools.partial(attend_bwd_kernel, blocks, rows, groups, kv_local),
        grid_spec=pltpu.PrefetchScalarGridSpec(
            num_scalar_prefetch=1,
            grid=(kv_local,),
            in_specs=attention_specs(length, groups, kv_local)
            + [
                pl.BlockSpec((length, width), lambda g, r: (0, g)),
                pl.BlockSpec((1, blocks, groups * rows), lambda g, r: (g, 0, 0)),
                pl.BlockSpec((length, width), lambda g, r: (0, g)),
            ],
            out_specs=[
                pl.BlockSpec(raw.shape, lambda g, r: (0, 0)),
                pl.BlockSpec((1, HEAD), lambda g, r: (0, 0)),
                pl.BlockSpec((1, HEAD), lambda g, r: (0, 0)),
            ],
            scratch_shapes=[
                pltpu.VMEM((length, HEAD), BF16),
                pltpu.VMEM((HEAD, length), BF16),
                pltpu.VMEM((length, HEAD), BF16),
                pltpu.VMEM((length, HEAD), F32),
                pltpu.VMEM((length, HEAD), F32),
            ],
        ),
        out_shape=[
            jax.ShapeDtypeStruct(raw.shape, BF16),
            jax.ShapeDtypeStruct((1, HEAD), F32),
            jax.ShapeDtypeStruct((1, HEAD), F32),
        ],
        compiler_params=pltpu.CompilerParams(
            dimension_semantics=("arbitrary",), vmem_limit_bytes=VMEM_LIMIT
        ),
        cost_estimate=pl.CostEstimate(
            flops=4 * flops,
            bytes_accessed=raw.size * 6 + length * kv_local * width * 6,
            transcendentals=kv_local * groups * length * length // 2,
        ),
        name="attend_backward",
    )(rank, raw, raw, raw, raw, cosines, sines, q_gain, k_gain, mix, lse, upstream)


def swap(values, bit, axis="sp"):
    return lax.ppermute(values, axis, [(i, i ^ bit) for i in range(lax.axis_size(axis))])


def gather_blocks(block):
    count = lax.axis_size("sp")
    if count != 4:
        return [block] + [swap(block, j) for j in range(1, count)]
    half = block.shape[0] // 2
    along_x, along_y = swap(block, 1), swap(block, 2)
    corner = jnp.concatenate([swap(along_y[:half], 1), swap(along_x[half:], 2)], axis=0)
    return [block, along_x, along_y, corner]


def scatter_sum(parts):
    count = lax.axis_size("sp")
    if count != 4:
        total = parts[0]
        for j in range(1, count):
            total = total + swap(parts[j].astype(BF16), j).astype(F32)
        return total
    half = parts[0].shape[0] // 2
    corner = parts[3].astype(BF16)
    from_x, from_y = swap(corner[:half], 1), swap(corner[half:], 2)
    to_y = jnp.concatenate([parts[2][:half] + from_x.astype(F32), parts[2][half:]], axis=0)
    to_x = jnp.concatenate([parts[1][:half], parts[1][half:] + from_y.astype(F32)], axis=0)
    return (
        parts[0]
        + swap(to_x.astype(BF16), 1).astype(F32)
        + swap(to_y.astype(BF16), 2).astype(F32)
    )


def row_parts(make, count, rows):
    if count != 4:
        whole = make(0, count * rows)
        return [whole[j * rows : (j + 1) * rows] for j in range(count)]
    corner = make(3 * rows, 4 * rows)
    middle = make(rows, 3 * rows)
    own = make(0, rows)
    return [own, middle[:rows], middle[rows:], corner]


def place_blocks(blocks, rank, axis):
    size = blocks[0].shape[axis]
    shape = list(blocks[0].shape)
    shape[axis] = size * len(blocks)
    whole = jnp.zeros(shape, blocks[0].dtype)
    for j, block in enumerate(blocks):
        whole = lax.dynamic_update_slice_in_dim(
            whole, block, jnp.bitwise_xor(rank, j) * size, axis
        )
    return whole


def sum_all(values):
    for axis in ("sp", "fsdp"):
        bit = 1
        while bit < lax.axis_size(axis):
            values = values + swap(values, bit, axis)
            bit *= 2
    return values


def rms_back(values, gain, grad):
    scale = lax.rsqrt(jnp.mean(values * values, axis=-1, keepdims=True) + EPS)
    pulled = grad * gain
    inner = jnp.mean(values * pulled, axis=-1, keepdims=True)
    return (
        scale * pulled - values * (scale * scale * scale * inner),
        jnp.sum(values * scale * grad, axis=0),
    )


def rms_low(values, gain):
    scale = lax.rsqrt(jnp.mean(values * values, axis=-1, keepdims=True) + EPS)
    return (values * scale * gain).astype(BF16)


def on_device(
    tokens, cotangent, positions, domain_ids, counts, loss_weight, domain_weights,
    q_weight, k_weight, v_weight, g_weight, o_weight, gate_weight, up_weight, down_weight,
    attn_gain, mlp_gain, q_gain, k_gain,
):
    count, shards = lax.axis_size("sp"), lax.axis_size("fsdp")
    rank, shard = lax.axis_index("sp"), lax.axis_index("fsdp")
    rank_ref = rank.astype(jnp.int32).reshape(1)
    _, rows, width = tokens.shape
    heads_local = q_weight.shape[1] // HEAD // count
    kv_local = k_weight.shape[1] // HEAD // count
    groups = heads_local // kv_local
    qcols, kcols = heads_local * HEAD, kv_local * HEAD
    dcols = width // count
    units = down_weight.shape[0] // count
    ffs = units * shards

    def columns(weight, size):
        return lax.dynamic_slice_in_dim(weight, rank * size, size, 1)

    def gather(weight):
        return lax.all_gather(weight, "fsdp", axis=0, tiled=True)

    def unit_columns(weight):
        spread = weight.reshape(weight.shape[0], shards, count, units)
        return lax.dynamic_slice_in_dim(spread, rank, 1, 2).reshape(weight.shape[0], ffs)

    attn_share = jnp.concatenate(
        [
            columns(q_weight, qcols), columns(k_weight, kcols), columns(v_weight, kcols),
            columns(g_weight, qcols), columns(o_weight, dcols),
        ],
        axis=1,
    )
    attn_full = gather(attn_share)
    in_cols = 2 * (qcols + kcols)
    w_in = attn_full[:, :in_cols]
    o_slices = attn_full[:, in_cols:].reshape(count, qcols, dcols)
    w_out = place_blocks(
        [
            swap(lax.dynamic_index_in_dim(o_slices, jnp.bitwise_xor(rank, j), 0, False), j)
            if j
            else lax.dynamic_index_in_dim(o_slices, rank, 0, False)
            for j in range(count)
        ],
        rank,
        1,
    )
    gateup = gather(jnp.concatenate([unit_columns(gate_weight), unit_columns(up_weight)], axis=1))
    w_gate, w_up = gateup[:, :ffs], gateup[:, ffs:]
    w_down = gather(lax.dynamic_slice_in_dim(down_weight, rank * units, units, 0))

    gains = lax.all_gather(
        jnp.concatenate([attn_gain, mlp_gain, q_gain, k_gain]), "fsdp", axis=0
    ).astype(F32)
    part = attn_gain.shape[0]
    first_gain = gains[:, :part].reshape(-1)
    second_gain = gains[:, part : 2 * part].reshape(-1)
    piece = q_gain.shape[0]
    query_gain = gains[:, 2 * part : 2 * part + piece].reshape(1, HEAD)
    key_gain = gains[:, 2 * part + piece :].reshape(1, HEAD)

    onehot = (domain_ids[:, None] == jnp.arange(domain_weights.shape[0], dtype=jnp.int32)).astype(F32)
    seq_scale = loss_weight * jnp.sum(onehot * domain_weights[None, :], axis=1) * SEQ_LEN
    seq_scale = (seq_scale / counts.astype(F32))[0]
    upstream = cotangent[0].astype(F32) * seq_scale
    inputs = tokens[0].astype(F32)
    tokens_all = jnp.concatenate(gather_blocks(tokens[0]), axis=0)
    places = jnp.concatenate([positions[0]] + [swap(positions[0], j) for j in range(1, count)])
    upstream_all = jnp.concatenate(gather_blocks(upstream.astype(BF16)), axis=0)

    inverse = ROPE_BASE ** (-(2.0 * jnp.arange(HALF, dtype=F32)) / HEAD)
    angles = places.astype(F32)[:, None] * inverse
    cosines, sines = jnp.cos(angles), jnp.sin(angles)
    cosines = jnp.concatenate([cosines, cosines], axis=1)
    sines = jnp.concatenate([-sines, sines], axis=1)

    first = rms_low(tokens_all.astype(F32), first_gain)
    raw = mm(first, w_in)
    gated, mix, lse = attend_forward(
        rank_ref, raw, cosines, sines, query_gain, key_gain, count, groups, kv_local
    )
    middle = inputs + scatter_sum(
        row_parts(lambda lo, hi: mm(gated[lo:hi], w_out), count, rows)
    )
    second = jnp.concatenate(gather_blocks(rms_low(middle, second_gain)), axis=0)

    gate_act = mm(second, w_gate)
    up_act = mm(second, w_up)
    opening = jax.nn.sigmoid(gate_act)
    silu = gate_act * opening
    hidden = (silu * up_act).astype(BF16)
    block_out = (
        middle + scatter_sum(row_parts(lambda lo, hi: mm(hidden[lo:hi], w_down), count, rows))
    ).astype(BF16)
    grad_hidden = mm(upstream_all, w_down, NT)
    grad_gate = (grad_hidden * up_act * opening * (1.0 + gate_act * (1.0 - opening))).astype(BF16)
    grad_up = (grad_hidden * silu).astype(BF16)
    grad_second = scatter_sum(
        row_parts(
            lambda lo, hi: mm(grad_gate[lo:hi], w_gate, NT) + mm(grad_up[lo:hi], w_up, NT),
            count,
            rows,
        )
    )
    pulled, second_gain_part = rms_back(middle, second_gain, grad_second)
    grad_middle = upstream + pulled

    grad_attn = jnp.concatenate(gather_blocks(grad_middle.astype(BF16)), axis=0)
    grad_gated = mm(grad_attn, w_out, NT).astype(BF16)
    grad_raw, query_gain_part, key_gain_part = attend_backward(
        rank_ref, raw, cosines, sines, query_gain, key_gain, mix, lse, grad_gated,
        count, groups, kv_local,
    )
    grad_first = scatter_sum(row_parts(lambda lo, hi: mm(grad_raw[lo:hi], w_in, NT), count, rows))
    pulled, first_gain_part = rms_back(inputs, first_gain, grad_first)
    input_grad = grad_middle + pulled

    def scatter(grad):
        return lax.psum_scatter(grad.astype(BF16), "fsdp", scatter_dimension=0, tiled=True)

    down_share = scatter(mm(hidden, upstream_all, TN))
    gateup_share = scatter(
        jnp.concatenate([mm(second, grad_gate, TN), mm(second, grad_up, TN)], axis=1).astype(BF16)
    )
    out_grad = mm(gated, grad_attn, TN).astype(BF16)
    out_slices = jnp.stack([out_grad[:, j * dcols : (j + 1) * dcols] for j in range(count)])
    out_grad = place_blocks(
        [
            swap(lax.dynamic_index_in_dim(out_slices, jnp.bitwise_xor(rank, j), 0, False), j)
            if j
            else lax.dynamic_index_in_dim(out_slices, rank, 0, False)
            for j in range(count)
        ],
        rank,
        0,
    )
    attn_shares = scatter(
        jnp.concatenate([mm(first, grad_raw, TN).astype(BF16), out_grad], axis=1)
    )

    down_grad = place_blocks(gather_blocks(down_share), rank, 0).astype(F32)
    gateup_blocks = gather_blocks(gateup_share)
    gateup_all = jnp.stack(gateup_blocks).reshape(count, -1, 2, shards, units)
    order = jnp.bitwise_xor(jnp.arange(count), rank)
    gateup_all = jnp.transpose(jnp.take(gateup_all, order, axis=0), (2, 1, 3, 0, 4)).reshape(
        2, gate_weight.shape[0], -1
    )
    attn_blocks = gather_blocks(attn_shares)

    def attn_grad(start, size):
        return place_blocks([b[:, start : start + size] for b in attn_blocks], rank, 1).astype(F32)

    total = sum_all(
        jnp.concatenate([first_gain_part, query_gain_part[0], key_gain_part[0], second_gain_part])
    )

    def own(values):
        size = values.shape[0] // shards
        return lax.dynamic_slice_in_dim(values, shard * size, size, 0)

    return (
        block_out[None],
        input_grad[None],
        attn_grad(0, qcols),
        attn_grad(qcols, kcols),
        attn_grad(qcols + kcols, kcols),
        attn_grad(qcols + 2 * kcols, qcols),
        attn_grad(in_cols, dcols),
        gateup_all[0].astype(F32),
        gateup_all[1].astype(F32),
        down_grad,
        own(total[:width]),
        own(total[width + 2 * HEAD :]),
        own(total[width : width + HEAD]),
        own(total[width + HEAD : width + 2 * HEAD]),
    )


def solution(mesh):
    both, over_fsdp = P("fsdp", "sp", None), P("fsdp", None)
    return jax.shard_map(
        on_device,
        mesh=mesh,
        in_specs=(both, both, P("fsdp", "sp"), P("fsdp"), P("fsdp"), P("fsdp"), P())
        + (over_fsdp,) * 8
        + (P("fsdp"),) * 4,
        out_specs=(both, both) + (over_fsdp,) * 8 + (P("fsdp"),) * 4,
        check_vma=False,
    )
```

time: 2570 us -> 867 us (0.34)
  waiting for transfers between devices: 1970 us -> 344 us
  matrix products: 303 us -> 170 us
  blocking collectives: 129 us -> 28.6 us
  local copies, waits for them, and re-layouts: 58.4 us -> 129 us
  starting transfers between devices: 25.4 us -> 59.9 us
  Pallas kernels: 0 us -> 30.7 us
    reduce_scatter x8 -> x3, waiting for transfers between devices: 939 us -> 54.9 us  [scatter(): lax.psum_scatter(grad.astype(BF16), 'fsdp', scatter_dimension=0, tiled=True)]
    all_gather x8 -> x3, waiting for transfers between devices: 819 us -> 36 us  [gather(): return lax.all_gather(weight, 'fsdp', axis=0, tiled=True)]
    ppermute x0 -> x58, waiting for transfers between devices: none -> 253 us  [swap(): lax.ppermute(values, axis, [(i, i ^ bit) for i in range(lax.axis_size(axi...]
    psum x1 -> x0, waiting for transfers between devices: 190 us -> none  [on_device(): lax.psum(shares[0].astype(jnp.bfloat16), 'sp').astype(jnp.float32)]
    dot_general x31 -> x25, matrix products: 303 us -> 170 us  [mm(): return lax.dot_general(left, right, dims, preferred_element_type=F32)]
    ppermute x0 -> x58, starting transfers between devices: none -> 59.7 us  [swap(): lax.ppermute(values, axis, [(i, i ^ bit) for i in range(lax.axis_size(axi...]
    all_to_all x4 -> x0, blocking collectives: 51.7 us -> none  [the longest x1 15.1 us: on_device(): lax.all_to_all(head_query, 'sp', split_axis=1, concat_axis=2, tiled=True)]
    slice x0 -> x54, local copies, waits for them, and re-layouts: none -> 39 us  [the longest x28 24.3 us: attn_grad(): b[:, start:start + size]]
  transfers between devices with their start and end apart: 23 -> 64, of which waited for: 18 -> 37; matrix products, arithmetic and copies ran while one was open for 11% -> 30% of each run, Pallas kernels for 0% -> 4%
where the time goes in v1:
time: 867 us; the launch traced here: 853 us
  waiting for transfers between devices  344 us (40%)
  matrix products  170 us (20%)
  local copies, waits for them, and re-layouts  129 us (15%)
  other arithmetic  71.6 us (8%)
  starting transfers between devices  59.9 us (7%)
  Pallas kernels  30.7 us (4%)
  blocking collectives  28.6 us (3%)
  between operations  19.3 us (2%)
    ppermute x58, waiting for transfers between devices, swap(): lax.ppermute(values, axis, [(i, i ^ bit) for i in range(lax.axis_size(axi...  253 us
    dot_general x25, matrix products, mm(): return lax.dot_general(left, right, dims, preferred_element_type=F32)  170 us
    ppermute x58, starting transfers between devices, swap(): lax.ppermute(values, axis, [(i, i ^ bit) for i in range(lax.axis_size(axi...  59.7 us
    reduce_scatter x3, waiting for transfers between devices, scatter(): lax.psum_scatter(grad.astype(BF16), 'fsdp', scatter_dimension=0, tiled=True)  54.9 us
    unnamed x138, local copies, waits for them, and re-layouts  44.1 us
    all_gather x3, waiting for transfers between devices, gather(): return lax.all_gather(weight, 'fsdp', axis=0, tiled=True)  36 us
    unnamed x1, blocking collectives  28.6 us
    slice x28, local copies, waits for them, and re-layouts, attn_grad(): b[:, start:start + size]  24.3 us
  transfers between devices with their start and end apart: 64, of which 37 were waited for; matrix products, arithmetic and copies ran while one was open for 30% of the time, Pallas kernels for 4%

profile of v1, /device:TPU:0, one launch (start us, length us, event | category | flops | bytes accessed | tf_op | source)
XLA Modules:
  0.0 853.4 jit_solution(5282300639597061394)
XLA Ops:
  36.9 28.6 %all-reduce = bf16[4352]{0:T(1024)(128)(2,1)S(1)} all-reduce(bf16[4352]{0:T(1024)(128)(2,1)S(1)} %dynamic-update-slice), channel_id=2, replica_groups=mesh['sp'=4,'fsdp'=8] {'fsdp'}, use_global_device_ids=true, to_apply=%add | all-reduce | flops 4352 | bytes 17408
  85.0 15.9 %all-gather.5.cloned.1.call-done = bf16[2048,2048]{1,0:T(8,128)(2,1)} async-done(((bf16[256,2048]{1,0:T(8,128)(2,1)}), bf16[2048,2048]{1,0:T(8,128)(2,1)}) %all-gather.5.cloned.1.call-update) | async-done | bytes 8388624 | tf_op jit(solution)/shard_map/all_gather | solution.py:398
  106.5 10.7 %fusion.26.q_ref.k_ref.v_ref.g_ref = f32[1024,1536]{1,0:T(8,128)} fusion(bf16[2048,2048]{1,0:T(8,128)(2,1)} %all-gather.5.cloned.1.call-done, bf16[1024,2048]{1,0:T(8,128)(2,1)S(1)} %copy-done.9, f32[2048]{0:T(1024)S(1)} %bitcast.108, f32[1024]{0:T(1024)S(1)} %add_rsqrt_fusion), kind=kOutput, calls=%fused_computation.46 | convolution fusion | flops 6450839552 | bytes 16789504 | tf_op jit(solution)/shard_map/dot_general | solution.py:26
  117.2 11.7 %attend_forward.1 = (bf16[1024,512]{1,0:T(8,128)(2,1)}, f32[1024,512]{1,0:T(8,128)}, f32[2,4,512]{2,1,0:T(4,128)}) custom-call(s32[1]{0:T(128)} %bitcast.1.rank_ref, f32[1024,1536]{1,0:T(8,128)} %fusion.26.q_ref.k_ref.v_ref.g_ref, f32[1024,1536]{1,0:T(8,128)} %fusion.26.q_ref.k_ref.v_ref.g_ref, f32[1024,1536]{1,0:T(8,128)} %fusion.26.q_ref.k_ref.v_ref.g_ref, ...), custom_call_target="tpu_custom_call" | custom-call | flops 5368709120 | bytes 9437184 | tf_op jit(solution)/shard_map/attend_forward/pallas_call | solution.py:220
  153.9 18.3 %collective-permute-done.11 = bf16[256,2048]{1,0:T(8,128)(2,1)S(1)} collective-permute-done((bf16[256,2048]{1,0:T(8,128)(2,1)S(1)}, bf16[256,2048]{1,0:T(8,128)(2,1)S(1)}, u32[]{:S(2)}, u32[]{:S(2)}) %collective-permute-start.11) | collective-permute-done | bytes 1048608 | tf_op jit(solution)/shard_map/ppermute | solution.py:299
  177.1 19.0 %collective-permute-done.23 = bf16[256,2048]{1,0:T(8,128)(2,1)S(1)} collective-permute-done((bf16[256,2048]{1,0:T(8,128)(2,1)S(1)}, bf16[256,2048]{1,0:T(8,128)(2,1)S(1)}, u32[]{:S(2)}, u32[]{:S(2)}) %collective-permute-start.23) | collective-permute-done | bytes 1048608 | tf_op jit(solution)/shard_map/ppermute | solution.py:299
  205.4 21.4 %collective-permute-done.25 = bf16[128,2048]{1,0:T(8,128)(2,1)S(1)} collective-permute-done((bf16[128,2048]{1,0:T(8,128)(2,1)S(1)}, bf16[128,2048]{1,0:T(8,128)(2,1)S(1)}, u32[]{:S(2)}, u32[]{:S(2)}) %collective-permute-start.25) | collective-permute-done | bytes 524320 | tf_op jit(solution)/shard_map/ppermute | solution.py:299
  230.4 11.7 %fusion.109 = f32[1024,1536]{1,0:T(8,128)} fusion(bf16[1024,2048]{1,0:T(8,128)(2,1)} %copy-done.24, bf16[1536,2048]{1,0:T(8,128)(2,1)} %all-gather.9.cloned.1.call-done), kind=kOutput, calls=%fused_computation.246 | convolution fusion | flops 6442450944 | bytes 16777216 | tf_op jit(solution)/shard_map/dot_general | solution.py:26
  242.1 11.2 %collective-permute-done.14 = bf16[256,2048]{1,0:T(8,128)(2,1)} collective-permute-done((bf16[256,2048]{1,0:T(8,128)(2,1)}, bf16[256,2048]{1,0:T(8,128)(2,1)}, u32[]{:S(2)}, u32[]{:S(2)}) %collective-permute-start.14) | collective-permute-done | bytes 1048608 | tf_op jit(solution)/shard_map/ppermute | solution.py:299
  264.5 20.1 %all-gather.7.cloned.1.call-done = bf16[2048,3072]{0,1:T(8,128)(2,1)} async-done(((bf16[256,3072]{0,1:T(8,128)(2,1)}), bf16[2048,3072]{0,1:T(8,128)(2,1)}) %all-gather.7.cloned.1.call-update) | async-done | bytes 12582928 | tf_op jit(solution)/shard_map/all_gather | solution.py:398
  284.6 11.7 %fusion.10 = f32[1024,1536]{1,0:T(8,128)} fusion(bf16[1024,2048]{1,0:T(8,128)(2,1)} %constant_dynamic-update-slice_fusion.5, bf16[2048,3072]{0,1:T(8,128)(2,1)} %all-gather.7.cloned.1.call-done), kind=kOutput, calls=%fused_computation.30 | convolution fusion | flops 6442450944 | bytes 16777216 | tf_op jit(solution)/shard_map/dot_general | solution.py:26
  296.3 28.5 %multiply_convert_fusion.1 = (bf16[1024,1536]{1,0:T(8,128)(2,1)}, bf16[1024,1536]{1,0:T(8,128)(2,1)}, bf16[1024,1536]{1,0:T(8,128)(2,1)S(1)}) fusion(f32[1024,1536]{1,0:T(8,128)} %fusion.109, f32[1024,1536]{1,0:T(8,128)} %fusion.10, bf16[1024,2048]{1,0:T(8,128)(2,1)} %constant_dynamic-update-slice_fusion.5, bf16[2048,3072]{0,1:T(8,128)(2,1)} %all-gather.7.cloned.1.call-done), kind=kOutput, calls=%fused_computation.15 | convolution fusion | flops 6466043904 | bytes 32505856 | tf_op jit(solution)/shard_map/dot_general | solution.py:26
  392.3 13.8 %collective-permute-done.19 = bf16[256,2048]{1,0:T(8,128)(2,1)S(1)} collective-permute-done((bf16[256,2048]{1,0:T(8,128)(2,1)S(1)}, bf16[256,2048]{1,0:T(8,128)(2,1)S(1)}, u32[]{:S(2)}, u32[]{:S(2)}) %collective-permute-start.19) | collective-permute-done | bytes 1048608 | tf_op jit(solution)/shard_map/ppermute | solution.py:299
  407.7 19.0 %collective-permute-done.27 = bf16[256,2048]{1,0:T(8,128)(2,1)S(1)} collective-permute-done((bf16[256,2048]{1,0:T(8,128)(2,1)S(1)}, bf16[256,2048]{1,0:T(8,128)(2,1)S(1)}, u32[]{:S(2)}, u32[]{:S(2)}) %collective-permute-start.27) | collective-permute-done | bytes 1048608 | tf_op jit(solution)/shard_map/ppermute | solution.py:299
  435.0 21.0 %collective-permute-done.31 = bf16[256,2048]{1,0:T(8,128)(2,1)S(1)} collective-permute-done((bf16[256,2048]{1,0:T(8,128)(2,1)S(1)}, bf16[256,2048]{1,0:T(8,128)(2,1)S(1)}, u32[]{:S(2)}, u32[]{:S(2)}) %collective-permute-start.31) | collective-permute-done | bytes 1048608 | tf_op jit(solution)/shard_map/ppermute | solution.py:299
  458.9 9.5 %collective-permute-done.32 = bf16[128,2048]{1,0:T(8,128)(2,1)S(1)} collective-permute-done((bf16[128,2048]{1,0:T(8,128)(2,1)S(1)}, bf16[128,2048]{1,0:T(8,128)(2,1)S(1)}, u32[]{:S(2)}, u32[]{:S(2)}) %collective-permute-start.32) | collective-permute-done | bytes 524320 | tf_op jit(solution)/shard_map/ppermute | solution.py:299
  486.9 19.0 %attend_backward.1 = (bf16[1024,1536]{1,0:T(8,128)(2,1)}, f32[1,128]{1,0:T(1,128)}, f32[1,128]{1,0:T(1,128)}) custom-call(s32[1]{0:T(128)} %bitcast.1.rank_ref, f32[1024,1536]{1,0:T(8,128)} %fusion.26.q_ref.k_ref.v_ref.g_ref, f32[1024,1536]{1,0:T(8,128)} %fusion.26.q_ref.k_ref.v_ref.g_ref, f32[1024,1536]{1,0:T(8,128)} %fusion.26.q_ref.k_ref.v_ref.g_ref, ...), custom_call_target="tpu_custom_call" | custom-call | flops 13421772800 | bytes 12582912 | tf_op jit(solution)/shard_map/attend_backward/pallas_call | solution.py:257
  505.9 11.1 %convolution_convert_fusion.3 = bf16[2048,1536]{0,1:T(8,128)(2,1)} fusion(bf16[1024,1536]{1,0:T(8,128)(2,1)} %get-tuple-element.23, bf16[1024,2048]{1,0:T(8,128)(2,1)S(1)} %copy-done.10, f32[2048]{0:T(1024)S(1)} %bitcast.109, f32[1024]{0:T(1024)S(1)} %copy-done.30), kind=kOutput, calls=%fused_computation.11 | convolution fusion | flops 6453985280 | bytes 13643776 | tf_op jit(solution)/shard_map/dot_general | solution.py:26
  528.8 9.8 %convolution_convert_fusion.1 = bf16[2048,1536]{0,1:T(8,128)(2,1)S(1)} fusion(bf16[1024,2048]{1,0:T(8,128)(2,1)} %constant_dynamic-update-slice_fusion.5, bf16[1024,1536]{1,0:T(8,128)(2,1)} %get-tuple-element.66), kind=kOutput, calls=%fused_computation.9 | convolution fusion | flops 6445596672 | bytes 13631488 | tf_op jit(solution)/shard_map/dot_general | solution.py:26
  548.1 14.9 %pad_maximum_fusion = bf16[2048,3072]{0,1:T(8,128)(2,1)} fusion(bf16[2048,1536]{0,1:T(8,128)(2,1)S(1)} %convolution_convert_fusion.1, bf16[2048,1536]{0,1:T(8,128)(2,1)S(1)} %convolution_convert_fusion.2), kind=kLoop, calls=%fused_computation.1 | loop fusion | flops 25165824 | bytes 25165824 | tf_op jit(solution)/shard_map/concatenate | solution.py:500
  583.4 18.1 %collective-permute-done.35 = bf16[256,2048]{1,0:T(8,128)(2,1)S(1)} collective-permute-done((bf16[256,2048]{1,0:T(8,128)(2,1)S(1)}, bf16[256,2048]{1,0:T(8,128)(2,1)S(1)}, u32[]{:S(2)}, u32[]{:S(2)}) %collective-permute-start.35) | collective-permute-done | bytes 1048608 | tf_op jit(solution)/shard_map/ppermute | solution.py:299
  660.1 15.5 %collective-permute-done.41 = bf16[256,2048]{0,1:T(8,128)(2,1)} collective-permute-done((bf16[256,2048]{0,1:T(8,128)(2,1)}, bf16[256,2048]{0,1:T(8,128)(2,1)}, u32[]{:S(2)}, u32[]{:S(2)}) %collective-permute-start.41) | collective-permute-done | bytes 1048608 | tf_op jit(solution)/shard_map/ppermute | solution.py:299
  692.1 54.9 %reduce-scatter.6.cloned.1.call-done = bf16[256,3072]{0,1:T(8,128)(2,1)} async-done(((bf16[2048,3072]{0,1:T(8,128)(2,1)}), bf16[256,3072]{0,1:T(8,128)(2,1)}) %reduce-scatter.6.cloned.1.call-update) | async-done | bytes 1572880 | tf_op jit(solution)/shard_map/reduce_scatter | solution.py:496
  767.3 14.0 %collective-permute-done.46 = bf16[256,3072]{0,1:T(8,128)(2,1)} collective-permute-done((bf16[256,3072]{0,1:T(8,128)(2,1)}, bf16[256,3072]{0,1:T(8,128)(2,1)}, u32[]{:S(2)}, u32[]{:S(2)}) %collective-permute-start.46) | collective-permute-done | bytes 1572896 | tf_op jit(solution)/shard_map/ppermute | solution.py:299
  (452 shorter events, 404.6 us)
Async XLA Ops:
  7.2 93.7 %all-gather.5.cloned.1.call-start = ((), (), s32[]{:S(2)}) async-start(), calls=%async_computation.3 | async-start | bytes 9437184 | tf_op jit(solution)/shard_map/all_gather | solution.py:398
  15.6 214.8 %all-gather.9.cloned.1.call-start = ((), (), s32[]{:S(2)}) async-start(), calls=%async_computation.5 | async-start | bytes 7077888 | tf_op jit(solution)/shard_map/all_gather | solution.py:398
  16.6 268.0 %all-gather.7.cloned.1.call-start = ((), (), s32[]{:S(2)}) async-start(), calls=%async_computation.4 | async-start | bytes 14155776 | tf_op jit(solution)/shard_map/all_gather | solution.py:398
  27.2 593.4 %reduce-scatter.8.cloned.1.call-start = ((), (), s32[]{:S(2)}) async-start(), calls=%async_computation.8 | async-start | bytes 7077888 | tf_op jit(solution)/shard_map/reduce_scatter | solution.py:496
  27.6 44.3 %collective-permute-start = (bf16[256,2048]{1,0:T(8,128)(2,1)S(1)}, bf16[256,2048]{1,0:T(8,128)(2,1)S(1)}, u32[]{:S(2)}, u32[]{:S(2)}) collective-permute-start(bf16[256,2048]{1,0:T(8,128)(2,1)S(1)} %bitcast.90), channel_id=1, source_target_pairs={{0,8},{8,0},{16,24},{24,16},{1,9},{9,1},{17,25},{25,17},{2,10},{10... | collective-permute-start | bytes 3145736 | tf_op jit(solution)/shard_map/ppermute | solution.py:299
  30.3 39.6 %collective-permute-start.1 = (bf16[256,2048]{1,0:T(8,128)(2,1)S(1)}, bf16[256,2048]{1,0:T(8,128)(2,1)S(1)}, u32[]{:S(2)}, u32[]{:S(2)}) collective-permute-start(bf16[256,2048]{1,0:T(8,128)(2,1)S(1)} %bitcast.91), channel_id=1, source_target_pairs={{0,16},{8,24},{16,0},{24,8},{1,17},{9,25},{17,1},{25,9},{2,18},{10... | collective-permute-start | bytes 3145736 | tf_op jit(solution)/shard_map/ppermute | solution.py:299
  31.9 36.1 %collective-permute-start.4 = (s32[256]{0:T(256)S(1)}, s32[256]{0:T(256)S(1)}, u32[]{:S(2)}, u32[]{:S(2)}) collective-permute-start(s32[256]{0:T(256)S(1)} %bitcast.116), channel_id=1, source_target_pairs={{0,8},{8,0},{16,24},{24,16},{1,9},{9,1},{17,25},{25,17},{2,10},{10... | collective-permute-start | bytes 3080 | tf_op jit(solution)/shard_map/ppermute | solution.py:299
  32.4 35.6 %collective-permute-start.5 = (s32[256]{0:T(256)S(1)}, s32[256]{0:T(256)S(1)}, u32[]{:S(2)}, u32[]{:S(2)}) collective-permute-start(s32[256]{0:T(256)S(1)} %bitcast.117), channel_id=1, source_target_pairs={{0,16},{8,24},{16,0},{24,8},{1,17},{9,25},{17,1},{25,9},{2,18},{10... | collective-permute-start | bytes 3080 | tf_op jit(solution)/shard_map/ppermute | solution.py:299
  32.4 35.6 %collective-permute-start.6 = (s32[256]{0:T(256)S(1)}, s32[256]{0:T(256)S(1)}, u32[]{:S(2)}, u32[]{:S(2)}) collective-permute-start(s32[256]{0:T(256)S(1)} %bitcast.118), channel_id=1, source_target_pairs={{0,24},{8,16},{16,8},{24,0},{1,25},{9,17},{17,9},{25,1},{2,26},{10... | collective-permute-start | bytes 3080 | tf_op jit(solution)/shard_map/ppermute | solution.py:299
  151.8 45.1 %collective-permute-start.22 = (bf16[256,2048]{1,0:T(8,128)(2,1)S(1)}, bf16[256,2048]{1,0:T(8,128)(2,1)S(1)}, u32[]{:S(2)}, u32[]{:S(2)}) collective-permute-start(bf16[256,2048]{1,0:T(8,128)(2,1)S(1)} %get-tuple-element.62), channel_id=1, source_target_pairs={{0,8},{8,0},{16,24},{24,16},{1,9},{9,1},{17,25},{25,17},{2,10},{10... | collective-permute-start | bytes 3145736 | tf_op jit(solution)/shard_map/ppermute | solution.py:299
  152.3 43.8 %collective-permute-start.23 = (bf16[256,2048]{1,0:T(8,128)(2,1)S(1)}, bf16[256,2048]{1,0:T(8,128)(2,1)S(1)}, u32[]{:S(2)}, u32[]{:S(2)}) collective-permute-start(bf16[256,2048]{1,0:T(8,128)(2,1)S(1)} %get-tuple-element.62), channel_id=1, source_target_pairs={{0,16},{8,24},{16,0},{24,8},{1,17},{9,25},{17,1},{25,9},{2,18},{10... | collective-permute-start | bytes 3145736 | tf_op jit(solution)/shard_map/ppermute | solution.py:299
  176.5 51.1 %collective-permute-start.15 = (bf16[256,2048]{1,0:T(8,128)(2,1)}, bf16[256,2048]{1,0:T(8,128)(2,1)S(1)}, u32[]{:S(2)}, u32[]{:S(2)}) collective-permute-start(bf16[256,2048]{1,0:T(8,128)(2,1)} %get-tuple-element.64), channel_id=1, source_target_pairs={{0,16},{8,24},{16,0},{24,8},{1,17},{9,25},{17,1},{25,9},{2,18},{10... | collective-permute-start | bytes 3145736 | tf_op jit(solution)/shard_map/ppermute | solution.py:299
  341.1 37.2 %collective-permute-start.18 = (bf16[128,2048]{1,0:T(8,128)(2,1)}, bf16[128,2048]{1,0:T(8,128)(2,1)}, u32[]{:S(2)}, u32[]{:S(2)}) collective-permute-start(bf16[128,2048]{1,0:T(8,128)(2,1)} %get-tuple-element.122), channel_id=1, source_target_pairs={{0,16},{8,24},{16,0},{24,8},{1,17},{9,25},{17,1},{25,9},{2,18},{10... | collective-permute-start | bytes 1572872 | tf_op jit(solution)/shard_map/ppermute | solution.py:299
  342.6 35.7 %collective-permute-start.20 = (bf16[128,2048]{1,0:T(8,128)(2,1)}, bf16[128,2048]{1,0:T(8,128)(2,1)}, u32[]{:S(2)}, u32[]{:S(2)}) collective-permute-start(bf16[128,2048]{1,0:T(8,128)(2,1)} %get-tuple-element.123), channel_id=1, source_target_pairs={{0,8},{8,0},{16,24},{24,16},{1,9},{9,1},{17,25},{25,17},{2,10},{10... | collective-permute-start | bytes 1572872 | tf_op jit(solution)/shard_map/ppermute | solution.py:299
  354.3 299.2 %reduce-scatter.4.cloned.1.call-start = ((), (), s32[]{:S(2)}) async-start(), calls=%async_computation.6 | async-start | bytes 9437184 | tf_op jit(solution)/shard_map/reduce_scatter | solution.py:496
  384.8 41.9 %collective-permute-start.27 = (bf16[256,2048]{1,0:T(8,128)(2,1)S(1)}, bf16[256,2048]{1,0:T(8,128)(2,1)S(1)}, u32[]{:S(2)}, u32[]{:S(2)}) collective-permute-start(bf16[256,2048]{1,0:T(8,128)(2,1)S(1)} %pad_maximum_fusion.10), channel_id=1, source_target_pairs={{0,8},{8,0},{16,24},{24,16},{1,9},{9,1},{17,25},{25,17},{2,10},{10... | collective-permute-start | bytes 3145736 | tf_op jit(solution)/shard_map/ppermute | solution.py:299
  385.5 42.5 %collective-permute-start.29 = (bf16[256,2048]{1,0:T(8,128)(2,1)S(1)}, bf16[256,2048]{1,0:T(8,128)(2,1)S(1)}, u32[]{:S(2)}, u32[]{:S(2)}) collective-permute-start(bf16[256,2048]{1,0:T(8,128)(2,1)S(1)} %pad_maximum_fusion.11), channel_id=1, source_target_pairs={{0,16},{8,24},{16,0},{24,8},{1,17},{9,25},{17,1},{25,9},{2,18},{10... | collective-permute-start | bytes 3145736 | tf_op jit(solution)/shard_map/ppermute | solution.py:299
  474.6 42.9 %collective-permute-start.38 = (bf16[512,512]{0,1:T(8,128)(2,1)}, bf16[512,512]{0,1:T(8,128)(2,1)}, u32[]{:S(2)}, u32[]{:S(2)}) collective-permute-start(bf16[512,512]{0,1:T(8,128)(2,1)} %bitcast.104), channel_id=1, source_target_pairs={{0,8},{8,0},{16,24},{24,16},{1,9},{9,1},{17,25},{25,17},{2,10},{10... | collective-permute-start | bytes 1572872 | tf_op jit(solution)/shard_map/ppermute | solution.py:299
  477.3 41.4 %collective-permute-start.39 = (bf16[512,512]{0,1:T(8,128)(2,1)}, bf16[512,512]{0,1:T(8,128)(2,1)}, u32[]{:S(2)}, u32[]{:S(2)}) collective-permute-start(bf16[512,512]{0,1:T(8,128)(2,1)} %bitcast.103), channel_id=1, source_target_pairs={{0,16},{8,24},{16,0},{24,8},{1,17},{9,25},{17,1},{25,9},{2,18},{10... | collective-permute-start | bytes 1572872 | tf_op jit(solution)/shard_map/ppermute | solution.py:299
  479.5 40.3 %collective-permute-start.40 = (bf16[512,512]{0,1:T(8,128)(2,1)}, bf16[512,512]{0,1:T(8,128)(2,1)}, u32[]{:S(2)}, u32[]{:S(2)}) collective-permute-start(bf16[512,512]{0,1:T(8,128)(2,1)} %bitcast.102), channel_id=1, source_target_pairs={{0,24},{8,16},{16,8},{24,0},{1,25},{9,17},{17,9},{25,1},{2,26},{10... | collective-permute-start | bytes 1572872 | tf_op jit(solution)/shard_map/ppermute | solution.py:299
  528.8 218.2 %reduce-scatter.6.cloned.1.call-start = ((), (), s32[]{:S(2)}) async-start(), calls=%async_computation.7 | async-start | bytes 14155776 | tf_op jit(solution)/shard_map/reduce_scatter | solution.py:496
  680.7 81.3 %collective-permute-start.43 = (bf16[128,2048]{0,1:T(8,128)(2,1)}, bf16[128,2048]{0,1:T(8,128)(2,1)}, u32[]{:S(2)}, u32[]{:S(2)}) collective-permute-start(bf16[128,2048]{0,1:T(8,128)(2,1)} %slice.456), channel_id=1, source_target_pairs={{0,8},{8,0},{16,24},{24,16},{1,9},{9,1},{17,25},{25,17},{2,10},{10... | collective-permute-start | bytes 1572872 | tf_op jit(solution)/shard_map/ppermute | solution.py:299
  683.0 80.1 %collective-permute-start.44 = (bf16[128,2048]{0,1:T(8,128)(2,1)}, bf16[128,2048]{0,1:T(8,128)(2,1)}, u32[]{:S(2)}, u32[]{:S(2)}) collective-permute-start(bf16[128,2048]{0,1:T(8,128)(2,1)} %slice.457), channel_id=1, source_target_pairs={{0,16},{8,24},{16,0},{24,8},{1,17},{9,25},{17,1},{25,9},{2,18},{10... | collective-permute-start | bytes 1572872 | tf_op jit(solution)/shard_map/ppermute | solution.py:299
  748.5 36.4 %collective-permute-start.45 = (bf16[256,3072]{0,1:T(8,128)(2,1)}, bf16[256,3072]{0,1:T(8,128)(2,1)}, u32[]{:S(2)}, u32[]{:S(2)}) collective-permute-start(bf16[256,3072]{0,1:T(8,128)(2,1)} %reduce-scatter.6.cloned.1.call-done), channel_id=1, source_target_pairs={{0,8},{8,0},{16,24},{24,16},{1,9},{9,1},{17,25},{25,17},{2,10},{10... | collective-permute-start | bytes 4718600 | tf_op jit(solution)/shard_map/ppermute | solution.py:299
  (95 other events, 1365.0 us)
Sparse Core Ops, SparseCore 0:
  15.7 85.1 all-gather.4
  103.1 63.4 all-gather.8
  168.8 115.7 all-gather.6
  354.4 67.9 reduce-scatter.7
  528.9 88.2 reduce-scatter.3
  619.4 127.5 reduce-scatter.5

commit v2 on v1

--- a/solution.py
+++ b/solution.py
@@ -295,47 +295,239 @@
     )(rank, raw, raw, raw, raw, cosines, sines, q_gain, k_gain, mix, lse, upstream)
 
 
+def middle_kernel(tokens_ref, own_ref, x_ref, y_ref, gain_ref, middle_ref, second_ref):
+    middle = tokens_ref[...].astype(F32) + own_ref[...]
+    middle = middle + x_ref[...].astype(F32) + y_ref[...].astype(F32)
+    scale = lax.rsqrt(jnp.mean(middle * middle, axis=-1, keepdims=True) + EPS)
+    middle_ref[...] = middle
+    second_ref[...] = (middle * scale * gain_ref[...]).astype(BF16)
+
+
+def norm_back_kernel(low, values_ref, base_ref, own_ref, x_ref, y_ref, gain_ref, grad_ref, part_ref, *low_ref):
+    values = values_ref[...].astype(F32)
+    grad = own_ref[...] + x_ref[...].astype(F32) + y_ref[...].astype(F32)
+    scale = lax.rsqrt(jnp.mean(values * values, axis=-1, keepdims=True) + EPS)
+    normed = values * scale
+    pulled = grad * gain_ref[...]
+    inner = jnp.mean(normed * pulled, axis=-1, keepdims=True)
+    total = base_ref[...] + scale * (pulled - normed * inner)
+    grad_ref[...] = total
+    if low:
+        low_ref[0][...] = total.astype(BF16)
+
+    @pl.when(pl.program_id(0) == 0)
+    def _():
+        part_ref[...] = jnp.zeros_like(part_ref)
+
+    part_ref[...] += jnp.sum(normed * grad, axis=0, keepdims=True)
+
+
+def row_call(kernel, name, arrays, gain, outs):
+    rows, width = arrays[0].shape
+    tile = rows // 4
+
+    def spec(shape):
+        if shape[0] == rows:
+            return pl.BlockSpec((tile, width), lambda i: (i, 0))
+        return pl.BlockSpec((1, width), lambda i: (0, 0))
+
+    return pl.pallas_call(
+        kernel,
+        grid=(4,),
+        in_specs=[spec(a.shape) for a in arrays] + [spec(gain.shape)],
+        out_specs=[spec(o.shape) for o in outs],
+        out_shape=outs,
+        compiler_params=pltpu.CompilerParams(
+            dimension_semantics=("arbitrary",), vmem_limit_bytes=VMEM_LIMIT
+        ),
+        cost_estimate=pl.CostEstimate(
+            flops=16 * rows * width, bytes_accessed=18 * rows * width, transcendentals=rows
+        ),
+        name=name,
+    )(*arrays, gain)
+
+
+def two_addends(came):
+    if len(came) == 2:
+        return came
+    return [sum(part.astype(F32) for part in came[:-1]), came[-1]]
+
+
+def middle_and_second(tokens, own, came, gain):
+    return row_call(
+        middle_kernel, "middle_and_second", [tokens, own, *two_addends(came)], gain[None],
+        [jax.ShapeDtypeStruct(own.shape, F32), jax.ShapeDtypeStruct(own.shape, BF16)],
+    )
+
+
+def norm_back(values, base, own, came, gain, low):
+    outs = [
+        jax.ShapeDtypeStruct(own.shape, F32), jax.ShapeDtypeStruct((1, own.shape[1]), F32),
+    ] + [jax.ShapeDtypeStruct(own.shape, BF16)] * low
+    return row_call(
+        functools.partial(norm_back_kernel, low), "norm_back",
+        [values, base, own, *two_addends(came)], gain[None], outs,
+    )
+
+
+def split_columns_kernel(count, sizes, rank_ref, *refs):
+    sources, outs = refs[:count], refs[count:]
+    block = jnp.bitwise_xor(pl.program_id(0), rank_ref[0])
+    for j in range(count):
+
+        @pl.when(block == j)
+        def _(j=j):
+            start = 0
+            for size, out in zip(sizes, outs):
+                out[...] = sources[j][:, start : start + size].astype(F32)
+                start += size
+
+
+def split_columns(rank, blocks, sizes):
+    count, rows = len(blocks), blocks[0].shape[0]
+    return pl.pallas_call(
+        functools.partial(split_columns_kernel, count, sizes),
+        grid_spec=pltpu.PrefetchScalarGridSpec(
+            num_scalar_prefetch=1,
+            grid=(count,),
+            in_specs=[pl.BlockSpec(b.shape, lambda a, r: (0, 0)) for b in blocks],
+            out_specs=[pl.BlockSpec((rows, size), lambda a, r: (0, a)) for size in sizes],
+        ),
+        out_shape=[jax.ShapeDtypeStruct((rows, count * size), F32) for size in sizes],
+        compiler_params=pltpu.CompilerParams(
+            dimension_semantics=("arbitrary",), vmem_limit_bytes=VMEM_LIMIT
+        ),
+        cost_estimate=pl.CostEstimate(
+            flops=0, bytes_accessed=6 * rows * count * sum(sizes), transcendentals=0
+        ),
+        name="split_columns",
+    )(rank, *blocks)
+
+
+def stack_rows_kernel(count, rank_ref, *refs):
+    block = jnp.bitwise_xor(pl.program_id(0), rank_ref[0])
+    for j in range(count):
+
+        @pl.when(block == j)
+        def _(j=j):
+            refs[count][...] = refs[j][...].astype(F32)
+
+
+def stack_rows(rank, blocks):
+    count, (rows, width) = len(blocks), blocks[0].shape
+    return pl.pallas_call(
+        functools.partial(stack_rows_kernel, count),
+        grid_spec=pltpu.PrefetchScalarGridSpec(
+            num_scalar_prefetch=1,
+            grid=(count,),
+            in_specs=[pl.BlockSpec(b.shape, lambda a, r: (0, 0)) for b in blocks],
+            out_specs=pl.BlockSpec((rows, width), lambda a, r: (a, 0)),
+        ),
+        out_shape=jax.ShapeDtypeStruct((count * rows, width), F32),
+        compiler_params=pltpu.CompilerParams(
+            dimension_semantics=("arbitrary",), vmem_limit_bytes=VMEM_LIMIT
+        ),
+        cost_estimate=pl.CostEstimate(
+            flops=0, bytes_accessed=6 * rows * count * width, transcendentals=0
+        ),
+        name="stack_rows",
+    )(rank, *blocks)
+
+
+def weave_units_kernel(count, shards, units, rank_ref, *refs):
+    sources, out, held = refs[:count], refs[count], refs[count + 1]
+    for j in range(count):
+        held[jnp.bitwise_xor(rank_ref[0], j)] = sources[j][...].astype(F32)
+    for a in range(count):
+        for f in range(shards):
+            start = (f * count + a) * units
+            out[:, start : start + units] = held[a, :, f * units : (f + 1) * units]
+
+
+def weave_units(rank, blocks, shards):
+    count, (rows, ffs) = len(blocks), blocks[0].shape
+    tile = rows // 4
+    return pl.pallas_call(
+        functools.partial(weave_units_kernel, count, shards, ffs // shards),
+        grid_spec=pltpu.PrefetchScalarGridSpec(
+            num_scalar_prefetch=1,
+            grid=(rows // tile,),
+            in_specs=[pl.BlockSpec((tile, ffs), lambda i, r: (i, 0)) for _ in blocks],
+            out_specs=pl.BlockSpec((tile, count * ffs), lambda i, r: (i, 0)),
+            scratch_shapes=[pltpu.VMEM((count, tile, ffs), F32)],
+        ),
+        out_shape=jax.ShapeDtypeStruct((rows, count * ffs), F32),
+        compiler_params=pltpu.CompilerParams(
+            dimension_semantics=("arbitrary",), vmem_limit_bytes=VMEM_LIMIT
+        ),
+        cost_estimate=pl.CostEstimate(
+            flops=0, bytes_accessed=6 * rows * count * ffs, transcendentals=0
+        ),
+        name="weave_units",
+    )(rank, *blocks)
+
+
 def swap(values, bit, axis="sp"):
     return lax.ppermute(values, axis, [(i, i ^ bit) for i in range(lax.axis_size(axis))])
 
 
+def sync(*values):
+    return lax.optimization_barrier(values)
+
+
+def gather_start(block):
+    return [block] + [swap(block, j) for j in range(1, lax.axis_size("sp"))][: 2 if lax.axis_size("sp") == 4 else None]
+
+
+def gather_turn(held):
+    if lax.axis_size("sp") != 4:
+        return held
+    half = held[0].shape[0] // 2
+    return held + [swap(held[2][:half], 1), swap(held[1][half:], 2)]
+
+
+def gather_end(held):
+    if lax.axis_size("sp") != 4:
+        return held
+    return held[:3] + [jnp.concatenate(held[3:], axis=0)]
+
+
 def gather_blocks(block):
+    return gather_end(gather_turn(gather_start(block)))
+
+
+def scatter_start(corner):
+    if lax.axis_size("sp") != 4:
+        return []
+    half = corner.shape[0] // 2
+    return [swap(corner[:half], 1), swap(corner[half:], 2)]
+
+
+def scatter_turn(others, came):
+    if lax.axis_size("sp") != 4:
+        return [swap(part.astype(BF16), j + 1) for j, part in enumerate(others)]
+    half = others[0].shape[0] // 2
+    to_x = jnp.concatenate([others[0][:half], others[0][half:] + came[1].astype(F32)], axis=0)
+    to_y = jnp.concatenate([others[1][:half] + came[0].astype(F32), others[1][half:]], axis=0)
+    return [swap(to_x.astype(BF16), 1), swap(to_y.astype(BF16), 2)]
+
+
+def scatter_end(own, came):
+    for part in came:
+        own = own + part.astype(F32)
+    return own
+
+
+def corner_rows(make, rows):
     count = lax.axis_size("sp")
-    if count != 4:
-        return [block] + [swap(block, j) for j in range(1, count)]
-    half = block.shape[0] // 2
-    along_x, along_y = swap(block, 1), swap(block, 2)
-    corner = jnp.concatenate([swap(along_y[:half], 1), swap(along_x[half:], 2)], axis=0)
-    return [block, along_x, along_y, corner]
-
-
-def scatter_sum(parts):
+    return make((count - 1) * rows, count * rows).astype(BF16) if count == 4 else None
+
+
+def other_rows(make, rows):
     count = lax.axis_size("sp")
-    if count != 4:
-        total = parts[0]
-        for j in range(1, count):
-            total = total + swap(parts[j].astype(BF16), j).astype(F32)
-        return total
-    half = parts[0].shape[0] // 2
-    corner = parts[3].astype(BF16)
-    from_x, from_y = swap(corner[:half], 1), swap(corner[half:], 2)
-    to_y = jnp.concatenate([parts[2][:half] + from_x.astype(F32), parts[2][half:]], axis=0)
-    to_x = jnp.concatenate([parts[1][:half], parts[1][half:] + from_y.astype(F32)], axis=0)
-    return (
-        parts[0]
-        + swap(to_x.astype(BF16), 1).astype(F32)
-        + swap(to_y.astype(BF16), 2).astype(F32)
-    )
-
-
-def row_parts(make, count, rows):
-    if count != 4:
-        whole = make(0, count * rows)
-        return [whole[j * rows : (j + 1) * rows] for j in range(count)]
-    corner = make(3 * rows, 4 * rows)
-    middle = make(rows, 3 * rows)
-    own = make(0, rows)
-    return [own, middle[:rows], middle[rows:], corner]
+    stop = 3 if count == 4 else count
+    whole = make(rows, stop * rows)
+    return [whole[j * rows : (j + 1) * rows] for j in range(stop - 1)]
 
 
 def place_blocks(blocks, rank, axis):
@@ -350,6 +542,43 @@
     return whole
 
 
+def halve_start(held, bit):
+    shard = lax.axis_index("fsdp")
+    mine = jnp.bitwise_and(lax.div(shard, jnp.int32(bit)), 1)
+    pairs = held.reshape(held.shape[0] // 2, 2, held.shape[1], held.shape[2])
+    sent = lax.dynamic_index_in_dim(pairs, 1 - mine, 1, False)
+    kept = lax.dynamic_index_in_dim(pairs, mine, 1, False)
+    return kept, swap(sent, bit, "fsdp")
+
+
+def halve_end(state):
+    return (state[0].astype(F32) + state[1].astype(F32)).astype(BF16)
+
+
+def halve_open(grad):
+    shards = lax.axis_size("fsdp")
+    return halve_start(grad.reshape(shards, grad.shape[0] // shards, grad.shape[1]), 1)
+
+
+def halve_next(state, bit):
+    return halve_start(halve_end(state), bit)
+
+
+def halve_close(state):
+    held = halve_end(state)
+    while held.shape[0] > 1:
+        held = halve_end(halve_start(held, lax.axis_size("fsdp") // held.shape[0]))
+    return held[0]
+
+
+def double_over(values, axis):
+    bit = 1
+    while bit < lax.axis_size(axis):
+        values = jnp.concatenate([values, swap(values, bit, axis)], axis=0)
+        bit *= 2
+    return values
+
+
 def sum_all(values):
     for axis in ("sp", "fsdp"):
         bit = 1
@@ -357,16 +586,6 @@
             values = values + swap(values, bit, axis)
             bit *= 2
     return values
-
-
-def rms_back(values, gain, grad):
-    scale = lax.rsqrt(jnp.mean(values * values, axis=-1, keepdims=True) + EPS)
-    pulled = grad * gain
-    inner = jnp.mean(values * pulled, axis=-1, keepdims=True)
-    return (
-        scale * pulled - values * (scale * scale * scale * inner),
-        jnp.sum(values * scale * grad, axis=0),
-    )
 
 
 def rms_low(values, gain):
@@ -401,135 +620,192 @@
         spread = weight.reshape(weight.shape[0], shards, count, units)
         return lax.dynamic_slice_in_dim(spread, rank, 1, 2).reshape(weight.shape[0], ffs)
 
-    attn_share = jnp.concatenate(
-        [
-            columns(q_weight, qcols), columns(k_weight, kcols), columns(v_weight, kcols),
-            columns(g_weight, qcols), columns(o_weight, dcols),
-        ],
-        axis=1,
-    )
-    attn_full = gather(attn_share)
+    def scatter(grad):
+        return lax.psum_scatter(grad, "fsdp", scatter_dimension=0, tiled=True)
+
+    tokens_held = gather_start(tokens[0])
+    places = double_over(positions[0][None], "sp").reshape(-1)
+    gains = double_over(jnp.concatenate([attn_gain, mlp_gain, q_gain, k_gain])[None], "fsdp")
+    attn_full = gather(
+        jnp.concatenate(
+            [
+                columns(q_weight, qcols), columns(k_weight, kcols), columns(v_weight, kcols),
+                columns(g_weight, qcols), columns(o_weight, dcols),
+            ],
+            axis=1,
+        )
+    )
     in_cols = 2 * (qcols + kcols)
-    w_in = attn_full[:, :in_cols]
-    o_slices = attn_full[:, in_cols:].reshape(count, qcols, dcols)
-    w_out = place_blocks(
-        [
-            swap(lax.dynamic_index_in_dim(o_slices, jnp.bitwise_xor(rank, j), 0, False), j)
-            if j
-            else lax.dynamic_index_in_dim(o_slices, rank, 0, False)
-            for j in range(count)
-        ],
-        rank,
-        1,
-    )
-    gateup = gather(jnp.concatenate([unit_columns(gate_weight), unit_columns(up_weight)], axis=1))
+    onehot = (domain_ids[:, None] == jnp.arange(domain_weights.shape[0], dtype=jnp.int32)).astype(F32)
+    seq_scale = loss_weight * jnp.sum(onehot * domain_weights[None, :], axis=1) * SEQ_LEN
+    seq_scale = (seq_scale / counts.astype(F32))[0]
+    upstream = cotangent[0].astype(F32) * seq_scale
+    tokens_held, places, gains = sync(tokens_held, places, gains)
+    tokens_held = gather_turn(tokens_held)
+    gateup_share = jnp.concatenate([unit_columns(gate_weight), unit_columns(up_weight)], axis=1)
+    tokens_held, upstream_low, gateup_share = sync(
+        tokens_held, upstream.astype(BF16), gateup_share
+    )
+    gateup = gather(gateup_share)
     w_gate, w_up = gateup[:, :ffs], gateup[:, ffs:]
-    w_down = gather(lax.dynamic_slice_in_dim(down_weight, rank * units, units, 0))
-
-    gains = lax.all_gather(
-        jnp.concatenate([attn_gain, mlp_gain, q_gain, k_gain]), "fsdp", axis=0
-    ).astype(F32)
+    upstream_held = gather_start(upstream_low)
+    tokens_all = jnp.concatenate(gather_end(tokens_held), axis=0)
+
+    order = jnp.bitwise_xor(jnp.arange(shards, dtype=jnp.int32), shard.astype(jnp.int32))
+    gains = jnp.take(gains, order, axis=0).astype(F32)
     part = attn_gain.shape[0]
     first_gain = gains[:, :part].reshape(-1)
     second_gain = gains[:, part : 2 * part].reshape(-1)
     piece = q_gain.shape[0]
     query_gain = gains[:, 2 * part : 2 * part + piece].reshape(1, HEAD)
     key_gain = gains[:, 2 * part + piece :].reshape(1, HEAD)
-
-    onehot = (domain_ids[:, None] == jnp.arange(domain_weights.shape[0], dtype=jnp.int32)).astype(F32)
-    seq_scale = loss_weight * jnp.sum(onehot * domain_weights[None, :], axis=1) * SEQ_LEN
-    seq_scale = (seq_scale / counts.astype(F32))[0]
-    upstream = cotangent[0].astype(F32) * seq_scale
-    inputs = tokens[0].astype(F32)
-    tokens_all = jnp.concatenate(gather_blocks(tokens[0]), axis=0)
-    places = jnp.concatenate([positions[0]] + [swap(positions[0], j) for j in range(1, count)])
-    upstream_all = jnp.concatenate(gather_blocks(upstream.astype(BF16)), axis=0)
-
     inverse = ROPE_BASE ** (-(2.0 * jnp.arange(HALF, dtype=F32)) / HEAD)
     angles = places.astype(F32)[:, None] * inverse
     cosines, sines = jnp.cos(angles), jnp.sin(angles)
     cosines = jnp.concatenate([cosines, cosines], axis=1)
     sines = jnp.concatenate([-sines, sines], axis=1)
-
     first = rms_low(tokens_all.astype(F32), first_gain)
+
+    upstream_held, first, cosines, sines = sync(upstream_held, first, cosines, sines)
+    upstream_held = gather_turn(upstream_held)
+    first, upstream_held = sync(first, upstream_held)
+    upstream_all = jnp.concatenate(gather_end(upstream_held), axis=0)
+    first, upstream_all = sync(first, upstream_all)
+
+    w_in = attn_full[:, :in_cols]
+    o_slices = attn_full[:, in_cols:].reshape(count, qcols, dcols)
+    o_blocks = [
+        lax.dynamic_index_in_dim(o_slices, jnp.bitwise_xor(rank, j), 0, False) for j in range(count)
+    ]
+    first, o_blocks = sync(first, o_blocks)
+    o_blocks = [swap(block, j) if j else block for j, block in enumerate(o_blocks)]
     raw = mm(first, w_in)
+    raw, o_blocks = sync(raw, o_blocks)
+    w_out = place_blocks(o_blocks, rank, 1)
     gated, mix, lse = attend_forward(
         rank_ref, raw, cosines, sines, query_gain, key_gain, count, groups, kv_local
     )
-    middle = inputs + scatter_sum(
-        row_parts(lambda lo, hi: mm(gated[lo:hi], w_out), count, rows)
-    )
-    second = jnp.concatenate(gather_blocks(rms_low(middle, second_gain)), axis=0)
+    down_share = lax.dynamic_slice_in_dim(down_weight, rank * units, units, 0)
+    down_share, gated = sync(down_share, gated)
+    w_down = gather(down_share)
+
+    def out_rows(lo, hi):
+        return mm(gated[lo:hi], w_out)
+
+    corner = scatter_start(corner_rows(out_rows, rows))
+    others = other_rows(out_rows, rows)
+    own_part = out_rows(0, rows)
+    middle, second = middle_and_second(
+        tokens[0], own_part, scatter_turn(others, corner), second_gain
+    )
+    second = jnp.concatenate(gather_blocks(second), axis=0)
 
     gate_act = mm(second, w_gate)
     up_act = mm(second, w_up)
     opening = jax.nn.sigmoid(gate_act)
     silu = gate_act * opening
     hidden = (silu * up_act).astype(BF16)
-    block_out = (
-        middle + scatter_sum(row_parts(lambda lo, hi: mm(hidden[lo:hi], w_down), count, rows))
-    ).astype(BF16)
-    grad_hidden = mm(upstream_all, w_down, NT)
+    down_grad, upstream_now = sync(mm(hidden, upstream_all, TN).astype(BF16), upstream_all)
+    down_share = scatter(down_grad)
+    grad_hidden = mm(upstream_now, w_down, NT)
     grad_gate = (grad_hidden * up_act * opening * (1.0 + gate_act * (1.0 - opening))).astype(BF16)
     grad_up = (grad_hidden * silu).astype(BF16)
-    grad_second = scatter_sum(
-        row_parts(
-            lambda lo, hi: mm(grad_gate[lo:hi], w_gate, NT) + mm(grad_up[lo:hi], w_up, NT),
-            count,
-            rows,
-        )
-    )
-    pulled, second_gain_part = rms_back(middle, second_gain, grad_second)
-    grad_middle = upstream + pulled
-
-    grad_attn = jnp.concatenate(gather_blocks(grad_middle.astype(BF16)), axis=0)
+
+    def second_rows(lo, hi):
+        return mm(grad_gate[lo:hi], w_gate, NT) + mm(grad_up[lo:hi], w_up, NT)
+
+    corner = scatter_start(corner_rows(second_rows, rows))
+    others = other_rows(second_rows, rows)
+    own_part = second_rows(0, rows)
+    own_part, corner, others, grad_gate, grad_up, second = sync(
+        own_part, corner, others, grad_gate, grad_up, second
+    )
+    came = scatter_turn(others, corner)
+    gateup_grad = mm(second, jnp.concatenate([grad_gate, grad_up], axis=1), TN).astype(BF16)
+    gateup_grad, came = sync(gateup_grad, came)
+    gateup_share = scatter(gateup_grad)
+    came, down_share = sync(came, down_share)
+    down_held = gather_start(down_share)
+    grad_middle, second_gain_part, grad_attn = norm_back(
+        middle, upstream, own_part, came, second_gain, True
+    )
+    grad_attn, hidden = sync(grad_attn, hidden)
+    grad_attn = gather_start(grad_attn)
+
+    def down_rows(lo, hi):
+        return mm(hidden[lo:hi], w_down)
+
+    corner = corner_rows(down_rows, rows)
+    others = other_rows(down_rows, rows)
+    own_part = down_rows(0, rows)
+    grad_attn, corner, others, own_part, down_held = sync(
+        grad_attn, corner, others, own_part, down_held
+    )
+    grad_attn = jnp.concatenate(gather_end(gather_turn(grad_attn)), axis=0)
+
     grad_gated = mm(grad_attn, w_out, NT).astype(BF16)
+    out_grad = mm(gated, grad_attn, TN).astype(BF16)
+    out_blocks = [
+        lax.dynamic_slice_in_dim(out_grad, jnp.bitwise_xor(rank, j) * dcols, dcols, 1)
+        for j in range(count)
+    ]
+    grad_gated, out_blocks = sync(grad_gated, out_blocks)
+    out_blocks = [swap(block, j) if j else block for j, block in enumerate(out_blocks)]
     grad_raw, query_gain_part, key_gain_part = attend_backward(
         rank_ref, raw, cosines, sines, query_gain, key_gain, mix, lse, grad_gated,
         count, groups, kv_local,
     )
-    grad_first = scatter_sum(row_parts(lambda lo, hi: mm(grad_raw[lo:hi], w_in, NT), count, rows))
-    pulled, first_gain_part = rms_back(inputs, first_gain, grad_first)
-    input_grad = grad_middle + pulled
-
-    def scatter(grad):
-        return lax.psum_scatter(grad.astype(BF16), "fsdp", scatter_dimension=0, tiled=True)
-
-    down_share = scatter(mm(hidden, upstream_all, TN))
-    gateup_share = scatter(
-        jnp.concatenate([mm(second, grad_gate, TN), mm(second, grad_up, TN)], axis=1).astype(BF16)
-    )
-    out_grad = mm(gated, grad_attn, TN).astype(BF16)
-    out_slices = jnp.stack([out_grad[:, j * dcols : (j + 1) * dcols] for j in range(count)])
-    out_grad = place_blocks(
-        [
-            swap(lax.dynamic_index_in_dim(out_slices, jnp.bitwise_xor(rank, j), 0, False), j)
-            if j
-            else lax.dynamic_index_in_dim(out_slices, rank, 0, False)
-            for j in range(count)
-        ],
-        rank,
-        0,
-    )
-    attn_shares = scatter(
-        jnp.concatenate([mm(first, grad_raw, TN).astype(BF16), out_grad], axis=1)
-    )
-
-    down_grad = place_blocks(gather_blocks(down_share), rank, 0).astype(F32)
-    gateup_blocks = gather_blocks(gateup_share)
-    gateup_all = jnp.stack(gateup_blocks).reshape(count, -1, 2, shards, units)
-    order = jnp.bitwise_xor(jnp.arange(count), rank)
-    gateup_all = jnp.transpose(jnp.take(gateup_all, order, axis=0), (2, 1, 3, 0, 4)).reshape(
-        2, gate_weight.shape[0], -1
-    )
-    attn_blocks = gather_blocks(attn_shares)
-
-    def attn_grad(start, size):
-        return place_blocks([b[:, start : start + size] for b in attn_blocks], rank, 1).astype(F32)
-
+    grad_raw, out_blocks, corner, down_held = sync(grad_raw, out_blocks, corner, down_held)
+    corner = scatter_start(corner)
+    down_held = gather_turn(down_held)
+    attn_grad = mm(first, grad_raw, TN).astype(BF16)
+    out_grad = place_blocks(out_blocks, rank, 0)
+    attn_grad, grad_raw, corner, down_held = sync(attn_grad, grad_raw, corner, down_held)
+    came = scatter_turn(others, corner)
+
+    def first_rows(lo, hi):
+        return mm(grad_raw[lo:hi], w_in, NT)
+
+    corner = corner_rows(first_rows, rows)
+    others = other_rows(first_rows, rows)
+    first_part = first_rows(0, rows)
+    down_grad = stack_rows(rank_ref, gather_end(down_held))
+    attn_grad, out_grad, corner, others, first_part = sync(
+        attn_grad, out_grad, corner, others, first_part
+    )
+    came, corner, down_grad, attn_grad, out_grad = sync(came, corner, down_grad, attn_grad, out_grad)
+    corner = scatter_start(corner)
+    gateup_share, attn_grad = sync(gateup_share, attn_grad)
+    attn_share = scatter(attn_grad)
+    gateup_held = gather_start(gateup_share)
+    out_grad, gateup_share = sync(out_grad, gateup_share)
+    out_share = scatter(out_grad)
+    block_out = (middle + scatter_end(own_part, came)).astype(BF16)
+    corner, block_out = sync(corner, block_out)
+    came = scatter_turn(others, corner)
+    came, gateup_held = sync(came, gateup_held)
+    gateup_held = gather_turn(gateup_held)
+    input_grad, first_gain_part = norm_back(
+        tokens[0], grad_middle, first_part, came, first_gain, False
+    )
+    attn_share, input_grad = sync(attn_share, input_grad)
+    attn_held = gather_start(attn_share)
     total = sum_all(
-        jnp.concatenate([first_gain_part, query_gain_part[0], key_gain_part[0], second_gain_part])
-    )
+        jnp.concatenate(
+            [first_gain_part, query_gain_part, key_gain_part, second_gain_part], axis=1
+        )[0]
+    )
+    gateup_held, attn_held = sync(gateup_held, attn_held)
+    attn_held = gather_turn(attn_held)
+    gateup_blocks = gather_end(gateup_held)
+    gate_grad = weave_units(rank_ref, [b[:, :ffs] for b in gateup_blocks], shards)
+    up_grad = weave_units(rank_ref, [b[:, ffs:] for b in gateup_blocks], shards)
+    out_share, gate_grad, up_grad = sync(out_share, gate_grad, up_grad)
+    out_held = gather_start(out_share)
+    out_held, attn_held = sync(out_held, attn_held)
+    out_held = gather_turn(out_held)
+    attn_grads = split_columns(rank_ref, gather_end(attn_held), (qcols, kcols, kcols, qcols))
+    (out_grad,) = split_columns(rank_ref, gather_end(out_held), (dcols,))
 
     def own(values):
         size = values.shape[0] // shards
@@ -538,13 +814,10 @@
     return (
         block_out[None],
         input_grad[None],
-        attn_grad(0, qcols),
-        attn_grad(qcols, kcols),
-        attn_grad(qcols + kcols, kcols),
-        attn_grad(qcols + 2 * kcols, qcols),
-        attn_grad(in_cols, dcols),
-        gateup_all[0].astype(F32),
-        gateup_all[1].astype(F32),
+        *attn_grads,
+        out_grad,
+        gate_grad,
+        up_grad,
         down_grad,
         own(total[:width]),
         own(total[width + 2 * HEAD :]),

time: 867 us -> 680 us (0.78)
  waiting for transfers between devices: 344 us -> 235 us
  other arithmetic: 71.6 us -> 29.4 us
  Pallas kernels: 30.7 us -> 72.7 us
  local copies, waits for them, and re-layouts: 129 us -> 87 us
  blocking collectives: 28.6 us -> 0 us
  matrix products: 170 us -> 152 us
  starting transfers between devices: 59.9 us -> 77.6 us
    reduce_scatter x3 -> x4, waiting for transfers between devices: 54.9 us -> 0.03 us  [scatter(): return lax.psum_scatter(grad, 'fsdp', scatter_dimension=0, tiled=True)]
    ppermute x58 -> x64, waiting for transfers between devices: 253 us -> 209 us  [swap(): lax.ppermute(values, axis, [(i, i ^ bit) for i in range(lax.axis_size(axi...]
    pallas_call x0 -> x8, Pallas kernels: none -> 41.7 us  [the longest x3 17.1 us: row_call(): pl.pallas_call(kernel, grid=(4,), in_specs=[spec(a.shape) for a in arrays...]
    unnamed x1 -> x0, blocking collectives: 28.6 us -> none
    dot_general x25 -> x24, matrix products: 170 us -> 152 us  [mm(): return lax.dot_general(left, right, dims, preferred_element_type=F32)]
    ppermute x58 -> x64, starting transfers between devices: 59.7 us -> 77.3 us  [swap(): lax.ppermute(values, axis, [(i, i ^ bit) for i in range(lax.axis_size(axi...]
    concatenate x13 -> x17, other arithmetic: 25 us -> 8.96 us  [the longest x3 3.72 us: gather_end(): return held[:3] + [jnp.concatenate(held[3:], axis=0)]]
    all_gather x3, waiting for transfers between devices: 36 us -> 26.1 us  [gather(): return lax.all_gather(weight, 'fsdp', axis=0, tiled=True)]
  transfers between devices with their start and end apart: 64 -> 71, of which waited for: 37 -> 38; matrix products, arithmetic and copies ran while one was open for 30% -> 38% of each run, Pallas kernels for 4% -> 10%
where the time goes in v2:
time: 680 us; the launch traced here: 672 us
  waiting for transfers between devices  235 us (35%)
  matrix products  152 us (22%)
  local copies, waits for them, and re-layouts  87 us (13%)
  starting transfers between devices  77.6 us (11%)
  Pallas kernels  72.7 us (11%)
  other arithmetic  29.4 us (4%)
  between operations  18 us (3%)
    ppermute x64, waiting for transfers between devices, swap(): lax.ppermute(values, axis, [(i, i ^ bit) for i in range(lax.axis_size(axi...  209 us
    dot_general x24, matrix products, mm(): return lax.dot_general(left, right, dims, preferred_element_type=F32)  152 us
    ppermute x64, starting transfers between devices, swap(): lax.ppermute(values, axis, [(i, i ^ bit) for i in range(lax.axis_size(axi...  77.3 us
    unnamed x148, local copies, waits for them, and re-layouts  40.7 us
    all_gather x3, waiting for transfers between devices, gather(): return lax.all_gather(weight, 'fsdp', axis=0, tiled=True)  26.1 us
    pallas_call x1, Pallas kernels, attend_backward(): pl.pallas_call(functools.partial(attend_bwd_kernel, blocks, rows, groups,...  19.6 us
    pallas_call x3, Pallas kernels, row_call(): pl.pallas_call(kernel, grid=(4,), in_specs=[spec(a.shape) for a in arrays...  17.1 us
  transfers between devices with their start and end apart: 71, of which 38 were waited for; matrix products, arithmetic and copies ran while one was open for 38% of the time, Pallas kernels for 10%

profile of v2, /device:TPU:0, one launch (start us, length us, event | category | flops | bytes accessed | tf_op | source)
XLA Modules:
  0.0 672.1 jit_solution(13694955317991977740)
XLA Ops:
  78.9 11.0 %collective-permute-done.9 = bf16[256,2048]{1,0:T(8,128)(2,1)S(1)} collective-permute-done((bf16[256,2048]{1,0:T(8,128)(2,1)S(1)}, bf16[256,2048]{1,0:T(8,128)(2,1)S(1)}, u32[]{:S(2)}, u32[]{:S(2)}) %collective-permute-start.9) | collective-permute-done | bytes 1048608 | tf_op jit(solution)/shard_map/ppermute | solution.py:471
  117.9 10.9 %fusion.29.q_ref.k_ref.v_ref.g_ref = f32[1024,1536]{1,0:T(8,128)} fusion(bf16[1024,2048]{1,0:T(8,128)(2,1)S(1)} %copy-done.13, bf16[2048,2048]{1,0:T(8,128)(2,1)} %all-gather.4.cloned.1.call-done), kind=kOutput, calls=%fused_computation.39 | convolution fusion | flops 6442450944 | bytes 16777216 | tf_op jit(solution)/shard_map/dot_general | solution.py:26
  132.5 11.4 %attend_forward.1 = (bf16[1024,512]{1,0:T(8,128)(2,1)}, f32[1024,512]{1,0:T(8,128)}, f32[2,4,512]{2,1,0:T(4,128)}) custom-call(s32[1]{0:T(128)} %bitcast.1.rank_ref, f32[1024,1536]{1,0:T(8,128)} %fusion.29.q_ref.k_ref.v_ref.g_ref, f32[1024,1536]{1,0:T(8,128)} %fusion.29.q_ref.k_ref.v_ref.g_ref, f32[1024,1536]{1,0:T(8,128)} %fusion.29.q_ref.k_ref.v_ref.g_ref, ...), custom_call_target="tpu_custom_call" | custom-call | flops 5368709120 | bytes 9437184 | tf_op jit(solution)/shard_map/attend_forward/pallas_call | solution.py:220
  154.3 5.8 collective-permute-done.18
  169.8 9.4 %collective-permute-done.17.x_ref = bf16[256,2048]{1,0:T(8,128)(2,1)S(1)} collective-permute-done((bf16[256,2048]{1,0:T(8,128)(2,1)S(1)}, bf16[256,2048]{1,0:T(8,128)(2,1)S(1)}, u32[]{:S(2)}, u32[]{:S(2)}) %collective-permute-start.17) | collective-permute-done | bytes 1048608 | tf_op jit(solution)/shard_map/ppermute | solution.py:471
  190.9 17.6 %collective-permute-done.21 = bf16[256,2048]{1,0:T(8,128)(2,1)S(1)} collective-permute-done((bf16[256,2048]{1,0:T(8,128)(2,1)}, bf16[256,2048]{1,0:T(8,128)(2,1)S(1)}, u32[]{:S(2)}, u32[]{:S(2)}) %collective-permute-start.21) | collective-permute-done | bytes 1048608 | tf_op jit(solution)/shard_map/ppermute | solution.py:471
  222.2 10.4 %fusion.21 = f32[1024,1536]{1,0:T(8,128)S(1)} fusion(bf16[1024,2048]{1,0:T(8,128)(2,1)} %constant_dynamic-update-slice_fusion.10, bf16[2048,3072]{0,1:T(8,128)(2,1)} %all-gather.6.cloned.1.call-done), kind=kOutput, calls=%fused_computation.31 | convolution fusion | flops 6442450944 | bytes 16777216 | tf_op jit(solution)/shard_map/dot_general | solution.py:26
  232.6 12.5 %multiply_convert_fusion.2 = (bf16[1024,1536]{1,0:T(8,128)(2,1)S(1)}, f32[1024,1536]{1,0:T(8,128)}) fusion(f32[1024,1536]{1,0:T(8,128)S(1)} %fusion.21, bf16[1024,2048]{1,0:T(8,128)(2,1)} %constant_dynamic-update-slice_fusion.10, bf16[2048,3072]{0,1:T(8,128)(2,1)S(1)} %copy-done.47), kind=kOutput, calls=%fused_computation.14 | convolution fusion | flops 6451888128 | bytes 26214400 | tf_op jit(solution)/shard_map/dot_general | solution.py:26
  245.0 12.0 %convolution_convert_fusion.2 = bf16[1536,2048]{1,0:T(8,128)(2,1)} fusion(bf16[1024,1536]{1,0:T(8,128)(2,1)S(1)} %get-tuple-element.221, bf16[1024,2048]{1,0:T(8,128)(2,1)} %constant_dynamic-update-slice_fusion.5), kind=kOutput, calls=%fused_computation.8 | convolution fusion | flops 6445596672 | bytes 13631488 | tf_op jit(solution)/shard_map/dot_general | solution.py:26
  257.1 26.1 %all-gather.8.cloned.1.call-done = bf16[1536,2048]{1,0:T(8,128)(2,1)} async-done(((bf16[192,2048]{1,0:T(8,128)(2,1)}), bf16[1536,2048]{1,0:T(8,128)(2,1)}) %all-gather.8.cloned.1.call-update) | async-done | bytes 6291472 | tf_op jit(solution)/shard_map/all_gather | solution.py:617
  283.2 14.7 %multiply_convert_fusion.1 = (bf16[1024,1536]{1,0:T(8,128)(2,1)S(1)}, bf16[1024,1536]{1,0:T(8,128)(2,1)S(1)}) fusion(f32[1024,1536]{1,0:T(8,128)} %copy-done.52, f32[1024,1536]{1,0:T(8,128)} %get-tuple-element.367, bf16[1024,2048]{1,0:T(8,128)(2,1)} %constant_dynamic-update-slice_fusion.5, bf16[1536,2048]{1,0:T(8,128)(2,1)} %all-gather.8.cloned.1.call-done), kind=kOutput, calls=%fused_computation.13 | convolution fusion | flops 6462898176 | bytes 29360128 | tf_op jit(solution)/shard_map/dot_general | solution.py:26
  329.9 18.7 %convolution_convert_fusion = bf16[2048,3072]{1,0:T(8,128)(2,1)} fusion(bf16[1024,2048]{1,0:T(8,128)(2,1)} %constant_dynamic-update-slice_fusion.10, bf16[1024,1536]{1,0:T(8,128)(2,1)S(1)} %get-tuple-element.209, bf16[1024,1536]{1,0:T(8,128)(2,1)S(1)} %get-tuple-element.208), kind=kOutput, calls=%fused_computation.1 | convolution fusion | flops 12903776256 | bytes 23068672 | tf_op jit(solution)/shard_map/dot_general | solution.py:26
  354.7 6.4 norm_back.2
  377.7 24.2 %collective-permute-done.30.refs_1_ = bf16[192,2048]{1,0:T(8,128)(2,1)S(1)} collective-permute-done((bf16[192,2048]{1,0:T(8,128)(2,1)S(1)}, bf16[192,2048]{1,0:T(8,128)(2,1)S(1)}, u32[]{:S(2)}, u32[]{:S(2)}) %collective-permute-start.30) | collective-permute-done | bytes 786464 | tf_op jit(solution)/shard_map/ppermute | solution.py:471
  406.4 8.0 %collective-permute-done.32 = bf16[128,2048]{1,0:T(8,128)(2,1)S(1)} collective-permute-done((bf16[128,2048]{1,0:T(8,128)(2,1)S(1)}, bf16[128,2048]{1,0:T(8,128)(2,1)S(1)}, u32[]{:S(2)}, u32[]{:S(2)}) %collective-permute-start.32) | collective-permute-done | bytes 524320 | tf_op jit(solution)/shard_map/ppermute | solution.py:471
  426.3 19.6 %attend_backward.1 = (bf16[1024,1536]{1,0:T(8,128)(2,1)}, f32[1,128]{1,0:T(1,128)}, f32[1,128]{1,0:T(1,128)}) custom-call(s32[1]{0:T(128)} %bitcast.1.rank_ref, f32[1024,1536]{1,0:T(8,128)} %fusion.29.q_ref.k_ref.v_ref.g_ref, f32[1024,1536]{1,0:T(8,128)} %fusion.29.q_ref.k_ref.v_ref.g_ref, f32[1024,1536]{1,0:T(8,128)} %fusion.29.q_ref.k_ref.v_ref.g_ref, ...), custom_call_target="tpu_custom_call" | custom-call | flops 13421772800 | bytes 12582912 | tf_op jit(solution)/shard_map/attend_backward/pallas_call | solution.py:257
  449.2 10.6 %convolution_convert_fusion.1 = bf16[2048,1536]{1,0:T(8,128)(2,1)} fusion(bf16[1024,2048]{1,0:T(8,128)(2,1)S(1)} %copy-done.14, bf16[1024,1536]{1,0:T(8,128)(2,1)} %get-tuple-element.252), kind=kOutput, calls=%fused_computation.7 | convolution fusion | flops 6445596672 | bytes 13631488 | tf_op jit(solution)/shard_map/dot_general | solution.py:26
  475.3 5.7 fusion.25
  506.4 7.3 %collective-permute-done.43 = bf16[128,2048]{1,0:T(8,128)(2,1)S(1)} collective-permute-done((bf16[128,2048]{1,0:T(8,128)(2,1)S(1)}, bf16[128,2048]{1,0:T(8,128)(2,1)S(1)}, u32[]{:S(2)}, u32[]{:S(2)}) %collective-permute-start.43) | collective-permute-done | bytes 524320 | tf_op jit(solution)/shard_map/ppermute | solution.py:471
  521.4 20.6 %collective-permute-done.45.x_ref = bf16[256,2048]{1,0:T(8,128)(2,1)} collective-permute-done((bf16[256,2048]{1,0:T(8,128)(2,1)}, bf16[256,2048]{1,0:T(8,128)(2,1)}, u32[]{:S(2)}, u32[]{:S(2)}) %collective-permute-start.45) | collective-permute-done | bytes 1048608 | tf_op jit(solution)/shard_map/ppermute | solution.py:471
  542.0 29.8 %collective-permute-done.46.y_ref = bf16[256,2048]{1,0:T(8,128)(2,1)} collective-permute-done((bf16[256,2048]{1,0:T(8,128)(2,1)}, bf16[256,2048]{1,0:T(8,128)(2,1)}, u32[]{:S(2)}, u32[]{:S(2)}) %collective-permute-start.46) | collective-permute-done | bytes 1048608 | tf_op jit(solution)/shard_map/ppermute | solution.py:471
  585.3 15.7 %collective-permute-done.59 = f32[4352]{0:T(1024)S(1)} collective-permute-done((f32[4352]{0:T(1024)S(1)}, f32[4352]{0:T(1024)S(1)}, u32[]{:S(2)}, u32[]{:S(2)}) %collective-permute-start.59) | collective-permute-done | bytes 17440 | tf_op jit(solution)/shard_map/ppermute | solution.py:471
  625.7 5.9 weave_units.2
  631.6 5.9 weave_units.3
  (422 shorter events, 334.0 us)
Async XLA Ops:
  7.2 105.3 %all-gather.4.cloned.1.call-start = ((), (), s32[]{:S(2)}) async-start(), calls=%async_computation.4 | async-start | bytes 9437184 | tf_op jit(solution)/shard_map/all_gather | solution.py:617
  15.6 206.6 %all-gather.6.cloned.1.call-start = ((), (), s32[]{:S(2)}) async-start(), calls=%async_computation.5 | async-start | bytes 14155776 | tf_op jit(solution)/shard_map/all_gather | solution.py:617
  15.6 33.1 %collective-permute-start = (bf16[256,2048]{1,0:T(8,128)(2,1)}, bf16[256,2048]{1,0:T(8,128)(2,1)}, u32[]{:S(2)}, u32[]{:S(2)}) collective-permute-start(bf16[256,2048]{1,0:T(8,128)(2,1)} %bitcast.61), channel_id=1, source_target_pairs={{0,8},{8,0},{16,24},{24,16},{1,9},{9,1},{17,25},{25,17},{2,10},{10... | collective-permute-start | bytes 3145736 | tf_op jit(solution)/shard_map/ppermute | solution.py:471
  18.6 30.1 %collective-permute-start.1 = (bf16[256,2048]{1,0:T(8,128)(2,1)}, bf16[256,2048]{1,0:T(8,128)(2,1)}, u32[]{:S(2)}, u32[]{:S(2)}) collective-permute-start(bf16[256,2048]{1,0:T(8,128)(2,1)} %bitcast.62), channel_id=1, source_target_pairs={{0,16},{8,24},{16,0},{24,8},{1,17},{9,25},{17,1},{25,9},{2,18},{10... | collective-permute-start | bytes 3145736 | tf_op jit(solution)/shard_map/ppermute | solution.py:471
  64.3 218.9 %all-gather.8.cloned.1.call-start = ((), (), s32[]{:S(2)}) async-start(), calls=%async_computation.6 | async-start | bytes 7077888 | tf_op jit(solution)/shard_map/all_gather | solution.py:617
  152.9 201.8 %reduce-scatter.5.cloned.1.call-start = ((), (), s32[]{:S(2)}) async-start(), calls=%async_computation.7 | async-start | bytes 7077888 | tf_op jit(solution)/shard_map/reduce_scatter | solution.py:624
  257.0 239.4 %reduce-scatter.7.cloned.1.call-start = ((), (), s32[]{:S(2)}) async-start(), calls=%async_computation.8 | async-start | bytes 14155776 | tf_op jit(solution)/shard_map/reduce_scatter | solution.py:624
  328.3 25.0 %collective-permute-start.26 = (bf16[256,2048]{1,0:T(8,128)(2,1)}, bf16[256,2048]{1,0:T(8,128)(2,1)}, u32[]{:S(2)}, u32[]{:S(2)}) collective-permute-start(bf16[256,2048]{1,0:T(8,128)(2,1)} %pad_maximum_fusion.3), channel_id=1, source_target_pairs={{0,8},{8,0},{16,24},{24,16},{1,9},{9,1},{17,25},{25,17},{2,10},{10... | collective-permute-start | bytes 3145736 | tf_op jit(solution)/shard_map/ppermute | solution.py:471
  329.2 24.6 %collective-permute-start.27 = (bf16[256,2048]{1,0:T(8,128)(2,1)S(1)}, bf16[256,2048]{1,0:T(8,128)(2,1)S(1)}, u32[]{:S(2)}, u32[]{:S(2)}) collective-permute-start(bf16[256,2048]{1,0:T(8,128)(2,1)S(1)} %pad_maximum_fusion.4), channel_id=1, source_target_pairs={{0,16},{8,24},{16,0},{24,8},{1,17},{9,25},{17,1},{25,9},{2,18},{10... | collective-permute-start | bytes 3145736 | tf_op jit(solution)/shard_map/ppermute | solution.py:471
  354.7 226.6 %reduce-scatter.9.cloned.1.call-start = ((), (), s32[]{:S(2)}) async-start(), calls=%async_computation.9 | async-start | bytes 7077888 | tf_op jit(solution)/shard_map/reduce_scatter | solution.py:624
  361.1 41.9 %collective-permute-start.28 = (bf16[256,2048]{1,0:T(8,128)(2,1)}, bf16[256,2048]{1,0:T(8,128)(2,1)S(1)}, u32[]{:S(2)}, u32[]{:S(2)}) collective-permute-start(bf16[256,2048]{1,0:T(8,128)(2,1)} %get-tuple-element.226), channel_id=1, source_target_pairs={{0,8},{8,0},{16,24},{24,16},{1,9},{9,1},{17,25},{25,17},{2,10},{10... | collective-permute-start | bytes 3145736 | tf_op jit(solution)/shard_map/ppermute | solution.py:471
  362.6 40.4 %collective-permute-start.29 = (bf16[256,2048]{1,0:T(8,128)(2,1)}, bf16[256,2048]{1,0:T(8,128)(2,1)S(1)}, u32[]{:S(2)}, u32[]{:S(2)}) collective-permute-start(bf16[256,2048]{1,0:T(8,128)(2,1)} %get-tuple-element.226), channel_id=1, source_target_pairs={{0,16},{8,24},{16,0},{24,8},{1,17},{9,25},{17,1},{25,9},{2,18},{10... | collective-permute-start | bytes 3145736 | tf_op jit(solution)/shard_map/ppermute | solution.py:471
  363.2 38.7 %collective-permute-start.30 = (bf16[192,2048]{1,0:T(8,128)(2,1)S(1)}, bf16[192,2048]{1,0:T(8,128)(2,1)S(1)}, u32[]{:S(2)}, u32[]{:S(2)}) collective-permute-start(bf16[192,2048]{1,0:T(8,128)(2,1)S(1)} %copy-done.34), channel_id=1, source_target_pairs={{0,8},{8,0},{16,24},{24,16},{1,9},{9,1},{17,25},{25,17},{2,10},{10... | collective-permute-start | bytes 2359304 | tf_op jit(solution)/shard_map/ppermute | solution.py:471
  363.8 39.2 %collective-permute-start.31 = (bf16[192,2048]{1,0:T(8,128)(2,1)S(1)}, bf16[192,2048]{1,0:T(8,128)(2,1)S(1)}, u32[]{:S(2)}, u32[]{:S(2)}) collective-permute-start(bf16[192,2048]{1,0:T(8,128)(2,1)S(1)} %copy-done.34), channel_id=1, source_target_pairs={{0,16},{8,24},{16,0},{24,8},{1,17},{9,25},{17,1},{25,9},{2,18},{10... | collective-permute-start | bytes 2359304 | tf_op jit(solution)/shard_map/ppermute | solution.py:471
  470.9 25.5 %collective-permute-start.41 = (bf16[256,2048]{1,0:T(8,128)(2,1)S(1)}, bf16[256,2048]{1,0:T(8,128)(2,1)}, u32[]{:S(2)}, u32[]{:S(2)}) collective-permute-start(bf16[256,2048]{1,0:T(8,128)(2,1)S(1)} %pad_maximum_fusion.5), channel_id=1, source_target_pairs={{0,8},{8,0},{16,24},{24,16},{1,9},{9,1},{17,25},{25,17},{2,10},{10... | collective-permute-start | bytes 3145736 | tf_op jit(solution)/shard_map/ppermute | solution.py:471
  497.4 140.2 %reduce-scatter.11.cloned.1.call-start = ((), (), s32[]{:S(2)}) async-start(), calls=%async_computation.10 | async-start | bytes 2359296 | tf_op jit(solution)/shard_map/reduce_scatter | solution.py:624
  515.6 26.4 %collective-permute-start.45 = (bf16[256,2048]{1,0:T(8,128)(2,1)}, bf16[256,2048]{1,0:T(8,128)(2,1)}, u32[]{:S(2)}, u32[]{:S(2)}) collective-permute-start(bf16[256,2048]{1,0:T(8,128)(2,1)} %pad_maximum_fusion.7), channel_id=1, source_target_pairs={{0,8},{8,0},{16,24},{24,16},{1,9},{9,1},{17,25},{25,17},{2,10},{10... | collective-permute-start | bytes 3145736 | tf_op jit(solution)/shard_map/ppermute | solution.py:471
  516.4 55.4 %collective-permute-start.47 = (bf16[256,3072]{1,0:T(8,128)(2,1)}, bf16[256,3072]{1,0:T(8,128)(2,1)S(1)}, u32[]{:S(2)}, u32[]{:S(2)}) collective-permute-start(bf16[256,3072]{1,0:T(8,128)(2,1)} %reduce-scatter.7.cloned.1.call-done), channel_id=1, source_target_pairs={{0,8},{8,0},{16,24},{24,16},{1,9},{9,1},{17,25},{25,17},{2,10},{10... | collective-permute-start | bytes 4718600 | tf_op jit(solution)/shard_map/ppermute | solution.py:471
  517.6 54.2 %collective-permute-start.48 = (bf16[256,3072]{1,0:T(8,128)(2,1)}, bf16[256,3072]{1,0:T(8,128)(2,1)S(1)}, u32[]{:S(2)}, u32[]{:S(2)}) collective-permute-start(bf16[256,3072]{1,0:T(8,128)(2,1)} %reduce-scatter.7.cloned.1.call-done), channel_id=1, source_target_pairs={{0,16},{8,24},{16,0},{24,8},{1,17},{9,25},{17,1},{25,9},{2,18},{10... | collective-permute-start | bytes 4718600 | tf_op jit(solution)/shard_map/ppermute | solution.py:471
  519.6 52.2 %collective-permute-start.46 = (bf16[256,2048]{1,0:T(8,128)(2,1)}, bf16[256,2048]{1,0:T(8,128)(2,1)}, u32[]{:S(2)}, u32[]{:S(2)}) collective-permute-start(bf16[256,2048]{1,0:T(8,128)(2,1)} %pad_maximum_fusion.8), channel_id=1, source_target_pairs={{0,16},{8,24},{16,0},{24,8},{1,17},{9,25},{17,1},{25,9},{2,18},{10... | collective-permute-start | bytes 3145736 | tf_op jit(solution)/shard_map/ppermute | solution.py:471
  572.7 44.2 %collective-permute-start.49 = (bf16[128,3072]{1,0:T(8,128)(2,1)}, bf16[128,3072]{1,0:T(8,128)(2,1)}, u32[]{:S(2)}, u32[]{:S(2)}) collective-permute-start(bf16[128,3072]{1,0:T(8,128)(2,1)} %slice.320), channel_id=1, source_target_pairs={{0,8},{8,0},{16,24},{24,16},{1,9},{9,1},{17,25},{25,17},{2,10},{10... | collective-permute-start | bytes 2359304 | tf_op jit(solution)/shard_map/ppermute | solution.py:471
  574.8 42.1 %collective-permute-start.50 = (bf16[128,3072]{1,0:T(8,128)(2,1)}, bf16[128,3072]{1,0:T(8,128)(2,1)}, u32[]{:S(2)}, u32[]{:S(2)}) collective-permute-start(bf16[128,3072]{1,0:T(8,128)(2,1)} %slice.321), channel_id=1, source_target_pairs={{0,16},{8,24},{16,0},{24,8},{1,17},{9,25},{17,1},{25,9},{2,18},{10... | collective-permute-start | bytes 2359304 | tf_op jit(solution)/shard_map/ppermute | solution.py:471
  581.3 35.6 %collective-permute-start.51 = (bf16[256,1536]{1,0:T(8,128)(2,1)}, bf16[256,1536]{1,0:T(8,128)(2,1)}, u32[]{:S(2)}, u32[]{:S(2)}) collective-permute-start(bf16[256,1536]{1,0:T(8,128)(2,1)} %reduce-scatter.9.cloned.1.call-done.refs_0_), channel_id=1, source_target_pairs={{0,8},{8,0},{16,24},{24,16},{1,9},{9,1},{17,25},{25,17},{2,10},{10... | collective-permute-start | bytes 2359304 | tf_op jit(solution)/shard_map/ppermute | solution.py:471
  582.2 34.8 %collective-permute-start.52 = (bf16[256,1536]{1,0:T(8,128)(2,1)}, bf16[256,1536]{1,0:T(8,128)(2,1)}, u32[]{:S(2)}, u32[]{:S(2)}) collective-permute-start(bf16[256,1536]{1,0:T(8,128)(2,1)} %reduce-scatter.9.cloned.1.call-done.refs_0_), channel_id=1, source_target_pairs={{0,16},{8,24},{16,0},{24,8},{1,17},{9,25},{17,1},{25,9},{2,18},{10... | collective-permute-start | bytes 2359304 | tf_op jit(solution)/shard_map/ppermute | solution.py:471
  (108 other events, 1301.5 us)
Sparse Core Ops, SparseCore 0:
  15.7 84.9 all-gather.3
  102.9 115.6 all-gather.5
  220.2 62.9 all-gather.7
  285.3 68.4 reduce-scatter.4
  356.0 127.5 reduce-scatter.6
  496.6 70.4 reduce-scatter.8
  569.4 33.9 reduce-scatter.10

commit v3 on v2

--- a/solution.py
+++ b/solution.py
@@ -303,7 +303,7 @@
     second_ref[...] = (middle * scale * gain_ref[...]).astype(BF16)
 
 
-def norm_back_kernel(low, values_ref, base_ref, own_ref, x_ref, y_ref, gain_ref, grad_ref, part_ref, *low_ref):
+def norm_back_kernel(low, values_ref, base_ref, own_ref, x_ref, y_ref, gain_ref, grad_ref, *low_ref):
     values = values_ref[...].astype(F32)
     grad = own_ref[...] + x_ref[...].astype(F32) + y_ref[...].astype(F32)
     scale = lax.rsqrt(jnp.mean(values * values, axis=-1, keepdims=True) + EPS)
@@ -315,12 +315,6 @@
     if low:
         low_ref[0][...] = total.astype(BF16)
 
-    @pl.when(pl.program_id(0) == 0)
-    def _():
-        part_ref[...] = jnp.zeros_like(part_ref)
-
-    part_ref[...] += jnp.sum(normed * grad, axis=0, keepdims=True)
-
 
 def row_call(kernel, name, arrays, gain, outs):
     rows, width = arrays[0].shape
@@ -361,39 +355,71 @@
 
 
 def norm_back(values, base, own, came, gain, low):
-    outs = [
-        jax.ShapeDtypeStruct(own.shape, F32), jax.ShapeDtypeStruct((1, own.shape[1]), F32),
-    ] + [jax.ShapeDtypeStruct(own.shape, BF16)] * low
+    outs = [jax.ShapeDtypeStruct(own.shape, F32)] + [jax.ShapeDtypeStruct(own.shape, BF16)] * low
     return row_call(
         functools.partial(norm_back_kernel, low), "norm_back",
         [values, base, own, *two_addends(came)], gain[None], outs,
     )
 
 
-def split_columns_kernel(count, sizes, rank_ref, *refs):
-    sources, outs = refs[:count], refs[count:]
+def flat_specs(pieces, spec):
+    return [spec(piece) for block in pieces for piece in block]
+
+
+def grouped(refs, counts):
+    blocks, start = [], 0
+    for count in counts:
+        blocks.append(refs[start : start + count])
+        start += count
+    return blocks, refs[start:]
+
+
+def split_columns_kernel(counts, sizes, weighed, rank_ref, *refs):
+    sources, refs = grouped(refs, counts)
+    weights, outs, sums = refs[:weighed], refs[weighed : weighed + len(sizes)], refs[-1]
     block = jnp.bitwise_xor(pl.program_id(0), rank_ref[0])
-    for j in range(count):
+    for j, pieces in enumerate(sources):
 
         @pl.when(block == j)
-        def _(j=j):
-            start = 0
-            for size, out in zip(sizes, outs):
-                out[...] = sources[j][:, start : start + size].astype(F32)
-                start += size
-
-
-def split_columns(rank, blocks, sizes):
-    count, rows = len(blocks), blocks[0].shape[0]
+        def _(pieces=pieces):
+            top = 0
+            for piece in pieces:
+                start, stop = 0, top + piece.shape[0]
+                for size, out in zip(sizes, outs):
+                    out[top:stop, :] = piece[:, start : start + size].astype(F32)
+                    start += size
+                top = stop
+
+    if weighed:
+        part = sum(
+            jnp.sum(out[...] * weight[...].astype(F32), axis=1, keepdims=True)
+            for out, weight in zip(outs, weights)
+        )
+
+        @pl.when(pl.program_id(0) == 0)
+        def _():
+            sums[...] = jnp.zeros_like(sums)
+
+        sums[...] += part
+
+
+def split_columns(rank, pieces, sizes, weights=()):
+    count, rows = len(pieces), pieces[0][0].shape[0]
+    group_specs = [pl.BlockSpec((rows, size), lambda a, r: (0, a)) for size in sizes]
+    sum_specs = [pl.BlockSpec((rows, 1), lambda a, r: (0, 0))] if weights else []
     return pl.pallas_call(
-        functools.partial(split_columns_kernel, count, sizes),
+        functools.partial(
+            split_columns_kernel, [len(block) for block in pieces], sizes, len(weights)
+        ),
         grid_spec=pltpu.PrefetchScalarGridSpec(
             num_scalar_prefetch=1,
             grid=(count,),
-            in_specs=[pl.BlockSpec(b.shape, lambda a, r: (0, 0)) for b in blocks],
-            out_specs=[pl.BlockSpec((rows, size), lambda a, r: (0, a)) for size in sizes],
-        ),
-        out_shape=[jax.ShapeDtypeStruct((rows, count * size), F32) for size in sizes],
+            in_specs=flat_specs(pieces, lambda p: pl.BlockSpec(p.shape, lambda a, r: (0, 0)))
+            + group_specs[: len(weights)],
+            out_specs=group_specs + sum_specs,
+        ),
+        out_shape=[jax.ShapeDtypeStruct((rows, count * size), F32) for size in sizes]
+        + [jax.ShapeDtypeStruct((rows, 1), F32)] * len(sum_specs),
         compiler_params=pltpu.CompilerParams(
             dimension_semantics=("arbitrary",), vmem_limit_bytes=VMEM_LIMIT
         ),
@@ -401,26 +427,30 @@
             flops=0, bytes_accessed=6 * rows * count * sum(sizes), transcendentals=0
         ),
         name="split_columns",
-    )(rank, *blocks)
-
-
-def stack_rows_kernel(count, rank_ref, *refs):
+    )(rank, *sum(pieces, []), *weights)
+
+
+def stack_rows_kernel(counts, rank_ref, *refs):
+    sources, (out,) = grouped(refs, counts)
     block = jnp.bitwise_xor(pl.program_id(0), rank_ref[0])
-    for j in range(count):
+    for j, pieces in enumerate(sources):
 
         @pl.when(block == j)
-        def _(j=j):
-            refs[count][...] = refs[j][...].astype(F32)
-
-
-def stack_rows(rank, blocks):
-    count, (rows, width) = len(blocks), blocks[0].shape
+        def _(pieces=pieces):
+            top = 0
+            for piece in pieces:
+                out[top : top + piece.shape[0], :] = piece[...].astype(F32)
+                top += piece.shape[0]
+
+
+def stack_rows(rank, pieces):
+    count, (rows, width) = len(pieces), pieces[0][0].shape
     return pl.pallas_call(
-        functools.partial(stack_rows_kernel, count),
+        functools.partial(stack_rows_kernel, [len(block) for block in pieces]),
         grid_spec=pltpu.PrefetchScalarGridSpec(
             num_scalar_prefetch=1,
             grid=(count,),
-            in_specs=[pl.BlockSpec(b.shape, lambda a, r: (0, 0)) for b in blocks],
+            in_specs=flat_specs(pieces, lambda p: pl.BlockSpec(p.shape, lambda a, r: (0, 0))),
             out_specs=pl.BlockSpec((rows, width), lambda a, r: (a, 0)),
         ),
         out_shape=jax.ShapeDtypeStruct((count * rows, width), F32),
@@ -431,40 +461,71 @@
             flops=0, bytes_accessed=6 * rows * count * width, transcendentals=0
         ),
         name="stack_rows",
-    )(rank, *blocks)
-
-
-def weave_units_kernel(count, shards, units, rank_ref, *refs):
-    sources, out, held = refs[:count], refs[count], refs[count + 1]
-    for j in range(count):
-        held[jnp.bitwise_xor(rank_ref[0], j)] = sources[j][...].astype(F32)
+    )(rank, *sum(pieces, []))
+
+
+def weave_units_kernel(counts, steps, shards, units, rank_ref, *refs):
+    sources, (weight, out, sums, held) = grouped(refs, counts)
+    step = pl.program_id(0)
+    for j, pieces in enumerate(sources):
+        place = jnp.bitwise_xor(rank_ref[0], j)
+        if len(pieces) == 1:
+            held[place] = pieces[0][...].astype(F32)
+            continue
+        share = steps // len(pieces)
+        for k, piece in enumerate(pieces):
+
+            @pl.when((step >= k * share) & (step < (k + 1) * share))
+            def _(piece=piece, place=place):
+                held[place] = piece[...].astype(F32)
+
+    count = len(counts)
     for a in range(count):
         for f in range(shards):
             start = (f * count + a) * units
             out[:, start : start + units] = held[a, :, f * units : (f + 1) * units]
-
-
-def weave_units(rank, blocks, shards):
-    count, (rows, ffs) = len(blocks), blocks[0].shape
-    tile = rows // 4
+    sums[...] = jnp.sum(out[...] * weight[...].astype(F32), axis=1, keepdims=True)
+
+
+def weave_units(rank, pieces, group, weight, shards):
+    count, (rows, width) = len(pieces), pieces[0][0].shape
+    ffs, steps = width // 2, 4
+    tile = rows // steps
+
+    def spec(block, k):
+        share = steps // len(block)
+
+        def place(i, r):
+            return (jnp.clip(i - k * share, 0, share - 1), group)
+
+        return pl.BlockSpec((tile, ffs), place)
+
     return pl.pallas_call(
-        functools.partial(weave_units_kernel, count, shards, ffs // shards),
+        functools.partial(
+            weave_units_kernel, [len(block) for block in pieces], steps, shards, ffs // shards
+        ),
         grid_spec=pltpu.PrefetchScalarGridSpec(
             num_scalar_prefetch=1,
-            grid=(rows // tile,),
-            in_specs=[pl.BlockSpec((tile, ffs), lambda i, r: (i, 0)) for _ in blocks],
-            out_specs=pl.BlockSpec((tile, count * ffs), lambda i, r: (i, 0)),
+            grid=(steps,),
+            in_specs=[spec(block, k) for block in pieces for k in range(len(block))]
+            + [pl.BlockSpec((tile, count * ffs), lambda i, r: (i, 0))],
+            out_specs=[
+                pl.BlockSpec((tile, count * ffs), lambda i, r: (i, 0)),
+                pl.BlockSpec((tile, 1), lambda i, r: (i, 0)),
+            ],
             scratch_shapes=[pltpu.VMEM((count, tile, ffs), F32)],
         ),
-        out_shape=jax.ShapeDtypeStruct((rows, count * ffs), F32),
+        out_shape=[
+            jax.ShapeDtypeStruct((rows, count * ffs), F32), jax.ShapeDtypeStruct((rows, 1), F32),
+        ],
         compiler_params=pltpu.CompilerParams(
             dimension_semantics=("arbitrary",), vmem_limit_bytes=VMEM_LIMIT
         ),
         cost_estimate=pl.CostEstimate(
-            flops=0, bytes_accessed=6 * rows * count * ffs, transcendentals=0
+            flops=0, bytes_accessed=8 * rows * count * ffs, transcendentals=0
         ),
         name="weave_units",
-    )(rank, *blocks)
+    )(rank, *sum(pieces, []), weight)
 
 
 def swap(values, bit, axis="sp"):
@@ -494,6 +555,12 @@
 
 def gather_blocks(block):
     return gather_end(gather_turn(gather_start(block)))
+
+
+def gather_pieces(held):
+    if lax.axis_size("sp") != 4:
+        return [[block] for block in held]
+    return [[block] for block in held[:3]] + [held[3:]]
 
 
 def scatter_start(corner):
@@ -579,12 +646,17 @@
     return values
 
 
-def sum_all(values):
-    for axis in ("sp", "fsdp"):
-        bit = 1
-        while bit < lax.axis_size(axis):
-            values = values + swap(values, bit, axis)
-            bit *= 2
+def sum_steps():
+    return [
+        (axis, 1 << k)
+        for axis in ("sp", "fsdp")
+        for k in range((lax.axis_size(axis) - 1).bit_length())
+    ]
+
+
+def sum_over(values, steps):
+    for axis, bit in steps:
+        values = values + swap(values, bit, axis)
     return values
 
 
@@ -705,11 +777,29 @@
     opening = jax.nn.sigmoid(gate_act)
     silu = gate_act * opening
     hidden = (silu * up_act).astype(BF16)
-    down_grad, upstream_now = sync(mm(hidden, upstream_all, TN).astype(BF16), upstream_all)
+    down_grad, hidden, upstream_now = sync(
+        mm(hidden, upstream_all, TN).astype(BF16), hidden, upstream_all
+    )
     down_share = scatter(down_grad)
+
+    def down_rows(lo, hi):
+        return mm(hidden[lo:hi], w_down)
+
+    block_corner = corner_rows(down_rows, rows)
+    block_others = other_rows(down_rows, rows)
+    block_part = down_rows(0, rows)
+    block_corner, block_others, block_part, upstream_now = sync(
+        block_corner, block_others, block_part, upstream_now
+    )
+    block_corner = scatter_start(block_corner)
     grad_hidden = mm(upstream_now, w_down, NT)
     grad_gate = (grad_hidden * up_act * opening * (1.0 + gate_act * (1.0 - opening))).astype(BF16)
     grad_up = (grad_hidden * silu).astype(BF16)
+    grad_gate, grad_up, block_corner = sync(grad_gate, grad_up, block_corner)
+    block_came = scatter_turn(block_others, block_corner)
+    gateup_grad = mm(second, jnp.concatenate([grad_gate, grad_up], axis=1), TN).astype(BF16)
+    gateup_grad, grad_gate, grad_up, block_came = sync(gateup_grad, grad_gate, grad_up, block_came)
+    gateup_share = scatter(gateup_grad)
 
     def second_rows(lo, hi):
         return mm(grad_gate[lo:hi], w_gate, NT) + mm(grad_up[lo:hi], w_up, NT)
@@ -717,30 +807,12 @@
     corner = scatter_start(corner_rows(second_rows, rows))
     others = other_rows(second_rows, rows)
     own_part = second_rows(0, rows)
-    own_part, corner, others, grad_gate, grad_up, second = sync(
-        own_part, corner, others, grad_gate, grad_up, second
-    )
+    own_part, corner, others = sync(own_part, corner, others)
     came = scatter_turn(others, corner)
-    gateup_grad = mm(second, jnp.concatenate([grad_gate, grad_up], axis=1), TN).astype(BF16)
-    gateup_grad, came = sync(gateup_grad, came)
-    gateup_share = scatter(gateup_grad)
-    came, down_share = sync(came, down_share)
-    down_held = gather_start(down_share)
-    grad_middle, second_gain_part, grad_attn = norm_back(
-        middle, upstream, own_part, came, second_gain, True
-    )
-    grad_attn, hidden = sync(grad_attn, hidden)
+    block_out = (middle + scatter_end(block_part, block_came)).astype(BF16)
+    came, block_out = sync(came, block_out)
+    grad_middle, grad_attn = norm_back(middle, upstream, own_part, came, second_gain, True)
     grad_attn = gather_start(grad_attn)
-
-    def down_rows(lo, hi):
-        return mm(hidden[lo:hi], w_down)
-
-    corner = corner_rows(down_rows, rows)
-    others = other_rows(down_rows, rows)
-    own_part = down_rows(0, rows)
-    grad_attn, corner, others, own_part, down_held = sync(
-        grad_attn, corner, others, own_part, down_held
-    )
     grad_attn = jnp.concatenate(gather_end(gather_turn(grad_attn)), axis=0)
 
     grad_gated = mm(grad_attn, w_out, NT).astype(BF16)
@@ -749,63 +821,66 @@
         lax.dynamic_slice_in_dim(out_grad, jnp.bitwise_xor(rank, j) * dcols, dcols, 1)
         for j in range(count)
     ]
-    grad_gated, out_blocks = sync(grad_gated, out_blocks)
+    grad_gated, out_blocks, down_share = sync(grad_gated, out_blocks, down_share)
     out_blocks = [swap(block, j) if j else block for j, block in enumerate(out_blocks)]
+    down_held = gather_start(down_share)
     grad_raw, query_gain_part, key_gain_part = attend_backward(
         rank_ref, raw, cosines, sines, query_gain, key_gain, mix, lse, grad_gated,
         count, groups, kv_local,
     )
-    grad_raw, out_blocks, corner, down_held = sync(grad_raw, out_blocks, corner, down_held)
-    corner = scatter_start(corner)
-    down_held = gather_turn(down_held)
+    steps = sum_steps()
+    gain_sums = jnp.concatenate([query_gain_part, key_gain_part], axis=1)
     attn_grad = mm(first, grad_raw, TN).astype(BF16)
-    out_grad = place_blocks(out_blocks, rank, 0)
-    attn_grad, grad_raw, corner, down_held = sync(attn_grad, grad_raw, corner, down_held)
-    came = scatter_turn(others, corner)
+    attn_grad, grad_raw, gain_sums, out_blocks = sync(attn_grad, grad_raw, gain_sums, out_blocks)
 
     def first_rows(lo, hi):
         return mm(grad_raw[lo:hi], w_in, NT)
 
     corner = corner_rows(first_rows, rows)
+    corner, grad_raw, attn_grad, gain_sums = sync(corner, grad_raw, attn_grad, gain_sums)
+    corner = scatter_start(corner)
+    gain_sums = sum_over(gain_sums, steps[:1])
     others = other_rows(first_rows, rows)
     first_part = first_rows(0, rows)
-    down_grad = stack_rows(rank_ref, gather_end(down_held))
-    attn_grad, out_grad, corner, others, first_part = sync(
-        attn_grad, out_grad, corner, others, first_part
-    )
-    came, corner, down_grad, attn_grad, out_grad = sync(came, corner, down_grad, attn_grad, out_grad)
-    corner = scatter_start(corner)
-    gateup_share, attn_grad = sync(gateup_share, attn_grad)
+    out_grad = place_blocks(out_blocks, rank, 0)
+    attn_grad, out_grad, others, first_part, corner, down_held, gain_sums = sync(
+        attn_grad, out_grad, others, first_part, corner, down_held, gain_sums
+    )
+    came = scatter_turn(others, corner)
+    gateup_share, attn_grad, out_grad = sync(gateup_share, attn_grad, out_grad)
     attn_share = scatter(attn_grad)
+    out_share = scatter(out_grad)
     gateup_held = gather_start(gateup_share)
-    out_grad, gateup_share = sync(out_grad, gateup_share)
-    out_share = scatter(out_grad)
-    block_out = (middle + scatter_end(own_part, came)).astype(BF16)
-    corner, block_out = sync(corner, block_out)
-    came = scatter_turn(others, corner)
-    came, gateup_held = sync(came, gateup_held)
+    gain_sums = sum_over(gain_sums, steps[1:2])
+    came, gain_sums, gateup_held = sync(came, gain_sums, gateup_held)
     gateup_held = gather_turn(gateup_held)
-    input_grad, first_gain_part = norm_back(
-        tokens[0], grad_middle, first_part, came, first_gain, False
-    )
-    attn_share, input_grad = sync(attn_share, input_grad)
+    down_held = gather_turn(down_held)
+    (input_grad,) = norm_back(tokens[0], grad_middle, first_part, came, first_gain, False)
+    gateup_held, gain_sums, input_grad, attn_share, down_held = sync(
+        gateup_held, gain_sums, input_grad, attn_share, down_held
+    )
     attn_held = gather_start(attn_share)
-    total = sum_all(
-        jnp.concatenate(
-            [first_gain_part, query_gain_part, key_gain_part, second_gain_part], axis=1
-        )[0]
-    )
-    gateup_held, attn_held = sync(gateup_held, attn_held)
+    gain_sums = sum_over(gain_sums, steps[2:3])
+    gateup_pieces = gather_pieces(gateup_held)
+    gate_grad, gate_sums = weave_units(rank_ref, gateup_pieces, 0, gate_weight, shards)
+    attn_held, out_share, gate_grad, gain_sums = sync(attn_held, out_share, gate_grad, gain_sums)
     attn_held = gather_turn(attn_held)
-    gateup_blocks = gather_end(gateup_held)
-    gate_grad = weave_units(rank_ref, [b[:, :ffs] for b in gateup_blocks], shards)
-    up_grad = weave_units(rank_ref, [b[:, ffs:] for b in gateup_blocks], shards)
-    out_share, gate_grad, up_grad = sync(out_share, gate_grad, up_grad)
     out_held = gather_start(out_share)
-    out_held, attn_held = sync(out_held, attn_held)
+    gain_sums = sum_over(gain_sums, steps[3:4])
+    down_grad = stack_rows(rank_ref, gather_pieces(down_held))
+    up_grad, up_sums = weave_units(rank_ref, gateup_pieces, 1, up_weight, shards)
+    attn_held, out_held, gain_sums, up_grad, down_grad = sync(
+        attn_held, out_held, gain_sums, up_grad, down_grad
+    )
     out_held = gather_turn(out_held)
-    attn_grads = split_columns(rank_ref, gather_end(attn_held), (qcols, kcols, kcols, qcols))
-    (out_grad,) = split_columns(rank_ref, gather_end(out_held), (dcols,))
+    gain_sums = sum_over(gain_sums, steps[4:])
+    *attn_grads, in_sums = split_columns(
+        rank_ref, gather_pieces(attn_held), (qcols, kcols, kcols, qcols),
+        (q_weight, k_weight, v_weight, g_weight),
+    )
+    (out_grad,) = split_columns(rank_ref, gather_pieces(out_held), (dcols,))
+    attn_gain_grad = in_sums[:, 0] / attn_gain.astype(F32)
+    mlp_gain_grad = (gate_sums + up_sums)[:, 0] / mlp_gain.astype(F32)
 
     def own(values):
         size = values.shape[0] // shards
@@ -819,10 +894,10 @@
         gate_grad,
         up_grad,
         down_grad,
-        own(total[:width]),
-        own(total[width + 2 * HEAD :]),
-        own(total[width : width + HEAD]),
-        own(total[width + HEAD : width + 2 * HEAD]),
+        attn_gain_grad,
+        mlp_gain_grad,
+        own(gain_sums[0, :HEAD]),
+        own(gain_sums[0, HEAD:]),
     )
 
 

time: 680 us -> 656 us (0.965)
  starting transfers between devices: 77.6 us -> 68.6 us
  local copies, waits for them, and re-layouts: 87 us -> 78.1 us
    ppermute x64, starting transfers between devices: 77.3 us -> 67.7 us  [swap(): lax.ppermute(values, axis, [(i, i ^ bit) for i in range(lax.axis_size(axi...]
    ppermute x64, waiting for transfers between devices: 209 us -> 201 us  [swap(): lax.ppermute(values, axis, [(i, i ^ bit) for i in range(lax.axis_size(axi...]
    unnamed x148 -> x151, local copies, waits for them, and re-layouts: 40.7 us -> 45.8 us
  transfers between devices with their start and end apart: 71 -> 71, of which waited for: 38 -> 31; matrix products, arithmetic and copies ran while one was open for 38% -> 36% of each run, Pallas kernels for 10% -> 11%
where the time goes in v3:
time: 656 us; the launch traced here: 648 us
  waiting for transfers between devices  229 us (35%)
  matrix products  150 us (23%)
  local copies, waits for them, and re-layouts  78.1 us (12%)
  Pallas kernels  76.7 us (12%)
  starting transfers between devices  68.6 us (10%)
  other arithmetic  26.5 us (4%)
  between operations  18.6 us (3%)
    ppermute x64, waiting for transfers between devices, swap(): lax.ppermute(values, axis, [(i, i ^ bit) for i in range(lax.axis_size(axi...  201 us
    dot_general x24, matrix products, mm(): return lax.dot_general(left, right, dims, preferred_element_type=F32)  150 us
    ppermute x64, starting transfers between devices, swap(): lax.ppermute(values, axis, [(i, i ^ bit) for i in range(lax.axis_size(axi...  67.7 us
    unnamed x151, local copies, waits for them, and re-layouts  45.8 us
    all_gather x3, waiting for transfers between devices, gather(): return lax.all_gather(weight, 'fsdp', axis=0, tiled=True)  22.7 us
    pallas_call x1, Pallas kernels, attend_backward(): pl.pallas_call(functools.partial(attend_bwd_kernel, blocks, rows, groups,...  19 us
    pallas_call x3, Pallas kernels, row_call(): pl.pallas_call(kernel, grid=(4,), in_specs=[spec(a.shape) for a in arrays...  17.5 us
    pallas_call x2, Pallas kernels, weave_units(): pl.pallas_call(functools.partial(weave_units_kernel, [len(block) for bloc...  14.1 us
  transfers between devices with their start and end apart: 71, of which 31 were waited for; matrix products, arithmetic and copies ran while one was open for 36% of the time, Pallas kernels for 11%

profile of v3, /device:TPU:0, one launch (start us, length us, event | category | flops | bytes accessed | tf_op | source)
XLA Modules:
  0.0 647.7 jit_solution(757221626028537754)
XLA Ops:
  80.0 9.5 %collective-permute-done.10 = bf16[256,2048]{1,0:T(8,128)(2,1)S(1)} collective-permute-done((bf16[256,2048]{1,0:T(8,128)(2,1)S(1)}, bf16[256,2048]{1,0:T(8,128)(2,1)S(1)}, u32[]{:S(2)}, u32[]{:S(2)}) %collective-permute-start.10) | collective-permute-done | bytes 1048608 | tf_op jit(solution)/shard_map/ppermute | solution.py:532
  96.7 6.3 collective-permute-done.11
  118.6 10.6 %fusion.29.q_ref.k_ref.v_ref.g_ref = f32[1024,1536]{1,0:T(8,128)} fusion(bf16[1024,2048]{1,0:T(8,128)(2,1)S(1)} %copy-done.12, bf16[2048,2048]{1,0:T(8,128)(2,1)} %all-gather.4.cloned.1.call-done), kind=kOutput, calls=%fused_computation.39 | convolution fusion | flops 6442450944 | bytes 16777216 | tf_op jit(solution)/shard_map/dot_general | solution.py:26
  132.6 11.4 %attend_forward.1 = (bf16[1024,512]{1,0:T(8,128)(2,1)}, f32[1024,512]{1,0:T(8,128)}, f32[2,4,512]{2,1,0:T(4,128)}) custom-call(s32[1]{0:T(128)} %bitcast.1.rank_ref, f32[1024,1536]{1,0:T(8,128)} %fusion.29.q_ref.k_ref.v_ref.g_ref, f32[1024,1536]{1,0:T(8,128)} %fusion.29.q_ref.k_ref.v_ref.g_ref, f32[1024,1536]{1,0:T(8,128)} %fusion.29.q_ref.k_ref.v_ref.g_ref, ...), custom_call_target="tpu_custom_call" | custom-call | flops 5368709120 | bytes 9437184 | tf_op jit(solution)/shard_map/attend_forward/pallas_call | solution.py:220
  154.0 8.2 %collective-permute-done.18 = bf16[128,2048]{1,0:T(8,128)(2,1)} collective-permute-done((bf16[128,2048]{1,0:T(8,128)(2,1)}, bf16[128,2048]{1,0:T(8,128)(2,1)}, u32[]{:S(2)}, u32[]{:S(2)}) %collective-permute-start.18) | collective-permute-done | bytes 524320 | tf_op jit(solution)/shard_map/ppermute | solution.py:532
  170.9 9.8 %collective-permute-done.17.x_ref = bf16[256,2048]{1,0:T(8,128)(2,1)S(1)} collective-permute-done((bf16[256,2048]{1,0:T(8,128)(2,1)S(1)}, bf16[256,2048]{1,0:T(8,128)(2,1)S(1)}, u32[]{:S(2)}, u32[]{:S(2)}) %collective-permute-start.17) | collective-permute-done | bytes 1048608 | tf_op jit(solution)/shard_map/ppermute | solution.py:532
  192.0 20.0 %collective-permute-done.21 = bf16[256,2048]{1,0:T(8,128)(2,1)S(1)} collective-permute-done((bf16[256,2048]{1,0:T(8,128)(2,1)}, bf16[256,2048]{1,0:T(8,128)(2,1)S(1)}, u32[]{:S(2)}, u32[]{:S(2)}) %collective-permute-start.21) | collective-permute-done | bytes 1048608 | tf_op jit(solution)/shard_map/ppermute | solution.py:532
  224.6 11.1 %fusion.21 = f32[1024,1536]{1,0:T(8,128)S(1)} fusion(bf16[1024,2048]{1,0:T(8,128)(2,1)} %constant_dynamic-update-slice_fusion.10, bf16[2048,3072]{0,1:T(8,128)(2,1)} %all-gather.6.cloned.1.call-done), kind=kOutput, calls=%fused_computation.31 | convolution fusion | flops 6442450944 | bytes 16777216 | tf_op jit(solution)/shard_map/dot_general | solution.py:26
  235.7 12.5 %multiply_convert_fusion.2 = (bf16[1024,1536]{1,0:T(8,128)(2,1)S(1)}, f32[1024,1536]{1,0:T(8,128)}) fusion(f32[1024,1536]{1,0:T(8,128)S(1)} %fusion.21, bf16[1024,2048]{1,0:T(8,128)(2,1)} %constant_dynamic-update-slice_fusion.10, bf16[2048,3072]{0,1:T(8,128)(2,1)S(1)} %copy-done.46), kind=kOutput, calls=%fused_computation.14 | convolution fusion | flops 6451888128 | bytes 26214400 | tf_op jit(solution)/shard_map/dot_general | solution.py:26
  248.1 12.1 %convolution_convert_fusion.2 = bf16[1536,2048]{1,0:T(8,128)(2,1)} fusion(bf16[1024,1536]{1,0:T(8,128)(2,1)S(1)} %get-tuple-element.202, bf16[1024,2048]{1,0:T(8,128)(2,1)} %constant_dynamic-update-slice_fusion.5), kind=kOutput, calls=%fused_computation.8 | convolution fusion | flops 6445596672 | bytes 13631488 | tf_op jit(solution)/shard_map/dot_general | solution.py:26
  260.5 22.7 %all-gather.8.cloned.1.call-done = bf16[1536,2048]{1,0:T(8,128)(2,1)} async-done(((bf16[192,2048]{1,0:T(8,128)(2,1)}), bf16[1536,2048]{1,0:T(8,128)(2,1)}) %all-gather.8.cloned.1.call-update) | async-done | bytes 6291472 | tf_op jit(solution)/shard_map/all_gather | solution.py:689
  299.6 14.4 %multiply_convert_fusion = (bf16[1024,1536]{1,0:T(8,128)(2,1)}, bf16[1024,1536]{1,0:T(8,128)(2,1)}) fusion(f32[1024,1536]{1,0:T(8,128)} %copy-done.56, f32[1024,1536]{1,0:T(8,128)} %get-tuple-element.355, bf16[1024,2048]{1,0:T(8,128)(2,1)} %constant_dynamic-update-slice_fusion.5, bf16[1536,2048]{1,0:T(8,128)(2,1)S(1)} %copy-done.47), kind=kOutput, calls=%fused_computation.12 | convolution fusion | flops 6462898176 | bytes 29360128 | tf_op jit(solution)/shard_map/dot_general | solution.py:26
  317.4 18.8 %convolution_convert_fusion = bf16[2048,3072]{1,0:T(8,128)(2,1)} fusion(bf16[1024,2048]{1,0:T(8,128)(2,1)} %constant_dynamic-update-slice_fusion.10, bf16[1024,1536]{1,0:T(8,128)(2,1)S(1)} %copy-done.51, bf16[1024,1536]{1,0:T(8,128)(2,1)S(1)} %copy-done.49), kind=kOutput, calls=%fused_computation.1 | convolution fusion | flops 12903776256 | bytes 23068672 | tf_op jit(solution)/shard_map/dot_general | solution.py:26
  372.2 18.0 %collective-permute-done.31.y_ref = bf16[256,2048]{1,0:T(8,128)(2,1)S(1)} collective-permute-done((bf16[256,2048]{1,0:T(8,128)(2,1)S(1)}, bf16[256,2048]{1,0:T(8,128)(2,1)S(1)}, u32[]{:S(2)}, u32[]{:S(2)}) %collective-permute-start.31) | collective-permute-done | bytes 1048608 | tf_op jit(solution)/shard_map/ppermute | solution.py:532
  391.7 6.4 norm_back.2
  401.0 19.5 %collective-permute-done.33 = bf16[256,2048]{1,0:T(8,128)(2,1)S(1)} collective-permute-done((bf16[256,2048]{1,0:T(8,128)(2,1)}, bf16[256,2048]{1,0:T(8,128)(2,1)S(1)}, u32[]{:S(2)}, u32[]{:S(2)}) %collective-permute-start.33) | collective-permute-done | bytes 1048608 | tf_op jit(solution)/shard_map/ppermute | solution.py:532
  424.7 8.0 %collective-permute-done.34 = bf16[128,2048]{1,0:T(8,128)(2,1)S(1)} collective-permute-done((bf16[128,2048]{1,0:T(8,128)(2,1)S(1)}, bf16[128,2048]{1,0:T(8,128)(2,1)S(1)}, u32[]{:S(2)}, u32[]{:S(2)}) %collective-permute-start.34) | collective-permute-done | bytes 524320 | tf_op jit(solution)/shard_map/ppermute | solution.py:532
  446.6 19.0 %attend_backward.1 = (bf16[1024,1536]{1,0:T(8,128)(2,1)}, f32[1,128]{1,0:T(1,128)}, f32[1,128]{1,0:T(1,128)}) custom-call(s32[1]{0:T(128)} %bitcast.1.rank_ref, f32[1024,1536]{1,0:T(8,128)} %fusion.29.q_ref.k_ref.v_ref.g_ref, f32[1024,1536]{1,0:T(8,128)} %fusion.29.q_ref.k_ref.v_ref.g_ref, f32[1024,1536]{1,0:T(8,128)} %fusion.29.q_ref.k_ref.v_ref.g_ref, ...), custom_call_target="tpu_custom_call" | custom-call | flops 13421772800 | bytes 12582912 | tf_op jit(solution)/shard_map/attend_backward/pallas_call | solution.py:257
  465.7 10.7 %convolution_convert_fusion.1 = bf16[2048,1536]{1,0:T(8,128)(2,1)} fusion(bf16[1024,2048]{1,0:T(8,128)(2,1)S(1)} %copy-done.13, bf16[1024,1536]{1,0:T(8,128)(2,1)} %get-tuple-element.247), kind=kOutput, calls=%fused_computation.7 | convolution fusion | flops 6445596672 | bytes 13631488 | tf_op jit(solution)/shard_map/dot_general | solution.py:26
  513.2 47.6 %collective-permute-done.46 = f32[1,256]{1,0:T(1,128)S(1)} collective-permute-done((f32[1,256]{1,0:T(1,128)S(1)}, f32[1,256]{1,0:T(1,128)S(1)}, u32[]{:S(2)}, u32[]{:S(2)}) %collective-permute-start.46) | collective-permute-done | bytes 1056 | tf_op jit(solution)/shard_map/ppermute | solution.py:532
  578.2 10.4 %collective-permute-done.51.refs_3_ = bf16[96,2048]{1,0:T(8,128)(2,1)S(1)} collective-permute-done((bf16[96,2048]{1,0:T(8,128)(2,1)}, bf16[96,2048]{1,0:T(8,128)(2,1)S(1)}, u32[]{:S(2)}, u32[]{:S(2)}) %collective-permute-start.51) | collective-permute-done | bytes 393248 | tf_op jit(solution)/shard_map/ppermute | solution.py:532
  593.1 7.1 %weave_units.2 = (f32[256,6144]{1,0:T(8,128)}, f32[256,1]{1,0:T(8,128)}) custom-call(s32[1]{0:T(128)} %bitcast.1.rank_ref, bf16[256,3072]{1,0:T(8,128)(2,1)} %reduce-scatter.7.cloned.1.call-done.refs_0_, bf16[256,3072]{1,0:T(8,128)(2,1)} %copy-done.5, bf16[256,3072]{1,0:T(8,128)(2,1)} %copy-done.4, bf16[128,3072]{1,0:T(8,128)(2,1)} %collective-permute-done.49.refs_3_, ...), custom_call_target="tpu_custom_call" | custom-call | bytes 12582912 | tf_op jit(solution)/shard_map/weave_units/pallas_call | solution.py:503
  608.6 7.1 %weave_units.3 = (f32[256,6144]{1,0:T(8,128)}, f32[256,1]{1,0:T(8,128)}) custom-call(s32[1]{0:T(128)} %bitcast.1.rank_ref, bf16[256,3072]{1,0:T(8,128)(2,1)} %reduce-scatter.7.cloned.1.call-done.refs_0_, bf16[256,3072]{1,0:T(8,128)(2,1)} %copy-done.5, bf16[256,3072]{1,0:T(8,128)(2,1)} %copy-done.4, bf16[128,3072]{1,0:T(8,128)(2,1)} %collective-permute-done.49.refs_3_, ...), custom_call_target="tpu_custom_call" | custom-call | bytes 12582912 | tf_op jit(solution)/shard_map/weave_units/pallas_call | solution.py:503
  627.8 6.7 %split_columns.2 = (f32[256,2048]{1,0:T(8,128)}, f32[256,1024]{1,0:T(8,128)}, f32[256,1024]{1,0:T(8,128)}, f32[256,2048]{1,0:T(8,128)}, f32[256,1]{1,0:T(8,128)}) custom-call(s32[1]{0:T(128)} %bitcast.1.rank_ref, bf16[256,1536]{1,0:T(8,128)(2,1)} %reduce-scatter.9.cloned.1.call-done.refs_0_, bf16[256,1536]{1,0:T(8,128)(2,1)} %copy-done.19, ...), custom_call_target="tpu_custom_call" | custom-call | bytes 9437184 | tf_op jit(solution)/shard_map/split_columns/pallas_call | solution.py:410
  (417 shorter events, 301.2 us)
Async XLA Ops:
  7.2 106.1 %all-gather.4.cloned.1.call-start = ((), (), s32[]{:S(2)}) async-start(), calls=%async_computation.4 | async-start | bytes 9437184 | tf_op jit(solution)/shard_map/all_gather | solution.py:689
  15.6 209.0 %all-gather.6.cloned.1.call-start = ((), (), s32[]{:S(2)}) async-start(), calls=%async_computation.5 | async-start | bytes 14155776 | tf_op jit(solution)/shard_map/all_gather | solution.py:689
  15.6 35.6 %collective-permute-start.1 = (bf16[256,2048]{1,0:T(8,128)(2,1)}, bf16[256,2048]{1,0:T(8,128)(2,1)}, u32[]{:S(2)}, u32[]{:S(2)}) collective-permute-start(bf16[256,2048]{1,0:T(8,128)(2,1)} %bitcast.65), channel_id=1, source_target_pairs={{0,16},{8,24},{16,0},{24,8},{1,17},{9,25},{17,1},{25,9},{2,18},{10... | collective-permute-start | bytes 3145736 | tf_op jit(solution)/shard_map/ppermute | solution.py:532
  18.7 32.6 %collective-permute-start = (bf16[256,2048]{1,0:T(8,128)(2,1)}, bf16[256,2048]{1,0:T(8,128)(2,1)}, u32[]{:S(2)}, u32[]{:S(2)}) collective-permute-start(bf16[256,2048]{1,0:T(8,128)(2,1)} %bitcast.66), channel_id=1, source_target_pairs={{0,8},{8,0},{16,24},{24,16},{1,9},{9,1},{17,25},{25,17},{2,10},{10... | collective-permute-start | bytes 3145736 | tf_op jit(solution)/shard_map/ppermute | solution.py:532
  64.5 218.7 %all-gather.8.cloned.1.call-start = ((), (), s32[]{:S(2)}) async-start(), calls=%async_computation.6 | async-start | bytes 7077888 | tf_op jit(solution)/shard_map/all_gather | solution.py:689
  152.6 288.4 %reduce-scatter.5.cloned.1.call-start = ((), (), s32[]{:S(2)}) async-start(), calls=%async_computation.7 | async-start | bytes 7077888 | tf_op jit(solution)/shard_map/reduce_scatter | solution.py:696
  260.2 239.6 %reduce-scatter.7.cloned.1.call-start = ((), (), s32[]{:S(2)}) async-start(), calls=%async_computation.8 | async-start | bytes 14155776 | tf_op jit(solution)/shard_map/reduce_scatter | solution.py:696
  315.3 25.0 %collective-permute-start.27 = (bf16[256,2048]{1,0:T(8,128)(2,1)}, bf16[256,2048]{1,0:T(8,128)(2,1)}, u32[]{:S(2)}, u32[]{:S(2)}) collective-permute-start(bf16[256,2048]{1,0:T(8,128)(2,1)} %pad_maximum_fusion.4), channel_id=1, source_target_pairs={{0,16},{8,24},{16,0},{24,8},{1,17},{9,25},{17,1},{25,9},{2,18},{10... | collective-permute-start | bytes 3145736 | tf_op jit(solution)/shard_map/ppermute | solution.py:532
  316.2 24.6 %collective-permute-start.26 = (bf16[256,2048]{1,0:T(8,128)(2,1)S(1)}, bf16[256,2048]{1,0:T(8,128)(2,1)S(1)}, u32[]{:S(2)}, u32[]{:S(2)}) collective-permute-start(bf16[256,2048]{1,0:T(8,128)(2,1)S(1)} %pad_maximum_fusion.3), channel_id=1, source_target_pairs={{0,8},{8,0},{16,24},{24,16},{1,9},{9,1},{17,25},{25,17},{2,10},{10... | collective-permute-start | bytes 3145736 | tf_op jit(solution)/shard_map/ppermute | solution.py:532
  341.7 247.8 %reduce-scatter.9.cloned.1.call-start = ((), (), s32[]{:S(2)}) async-start(), calls=%async_computation.9 | async-start | bytes 7077888 | tf_op jit(solution)/shard_map/reduce_scatter | solution.py:696
  399.6 24.0 %collective-permute-start.32 = (bf16[256,2048]{1,0:T(8,128)(2,1)}, bf16[256,2048]{1,0:T(8,128)(2,1)S(1)}, u32[]{:S(2)}, u32[]{:S(2)}) collective-permute-start(bf16[256,2048]{1,0:T(8,128)(2,1)} %get-tuple-element.229), channel_id=1, source_target_pairs={{0,8},{8,0},{16,24},{24,16},{1,9},{9,1},{17,25},{25,17},{2,10},{10... | collective-permute-start | bytes 3145736 | tf_op jit(solution)/shard_map/ppermute | solution.py:532
  441.0 58.7 %collective-permute-start.42 = (bf16[192,2048]{1,0:T(8,128)(2,1)}, bf16[192,2048]{1,0:T(8,128)(2,1)}, u32[]{:S(2)}, u32[]{:S(2)}) collective-permute-start(bf16[192,2048]{1,0:T(8,128)(2,1)} %reduce-scatter.5.cloned.1.call-done.refs_0_), channel_id=1, source_target_pairs={{0,16},{8,24},{16,0},{24,8},{1,17},{9,25},{17,1},{25,9},{2,18},{10... | collective-permute-start | bytes 2359304 | tf_op jit(solution)/shard_map/ppermute | solution.py:532
  442.2 57.6 %collective-permute-start.41 = (bf16[192,2048]{1,0:T(8,128)(2,1)}, bf16[192,2048]{1,0:T(8,128)(2,1)}, u32[]{:S(2)}, u32[]{:S(2)}) collective-permute-start(bf16[192,2048]{1,0:T(8,128)(2,1)} %reduce-scatter.5.cloned.1.call-done.refs_0_), channel_id=1, source_target_pairs={{0,8},{8,0},{16,24},{24,16},{1,9},{9,1},{17,25},{25,17},{2,10},{10... | collective-permute-start | bytes 2359304 | tf_op jit(solution)/shard_map/ppermute | solution.py:532
  443.1 33.4 %collective-permute-start.36 = (bf16[512,512]{1,0:T(8,128)(2,1)}, bf16[512,512]{1,0:T(8,128)(2,1)S(1)}, u32[]{:S(2)}, u32[]{:S(2)}) collective-permute-start(bf16[512,512]{1,0:T(8,128)(2,1)} %get-tuple-element.236), channel_id=1, source_target_pairs={{0,8},{8,0},{16,24},{24,16},{1,9},{9,1},{17,25},{25,17},{2,10},{10... | collective-permute-start | bytes 1572872 | tf_op jit(solution)/shard_map/ppermute | solution.py:532
  444.2 32.3 %collective-permute-start.37 = (bf16[512,512]{1,0:T(8,128)(2,1)}, bf16[512,512]{1,0:T(8,128)(2,1)S(1)}, u32[]{:S(2)}, u32[]{:S(2)}) collective-permute-start(bf16[512,512]{1,0:T(8,128)(2,1)} %get-tuple-element.237), channel_id=1, source_target_pairs={{0,16},{8,24},{16,0},{24,8},{1,17},{9,25},{17,1},{25,9},{2,18},{10... | collective-permute-start | bytes 1572872 | tf_op jit(solution)/shard_map/ppermute | solution.py:532
  445.1 36.7 %collective-permute-start.38 = (bf16[512,512]{1,0:T(8,128)(2,1)}, bf16[512,512]{1,0:T(8,128)(2,1)S(1)}, u32[]{:S(2)}, u32[]{:S(2)}) collective-permute-start(bf16[512,512]{1,0:T(8,128)(2,1)} %get-tuple-element.238), channel_id=1, source_target_pairs={{0,24},{8,16},{16,8},{24,0},{1,25},{9,17},{17,9},{25,1},{2,26},{10... | collective-permute-start | bytes 1572872 | tf_op jit(solution)/shard_map/ppermute | solution.py:532
  499.8 105.7 %reduce-scatter.11.cloned.1.call-start = ((), (), s32[]{:S(2)}) async-start(), calls=%async_computation.10 | async-start | bytes 2359296 | tf_op jit(solution)/shard_map/reduce_scatter | solution.py:696
  505.8 55.0 %collective-permute-start.45 = (bf16[256,2048]{1,0:T(8,128)(2,1)S(1)}, bf16[256,2048]{1,0:T(8,128)(2,1)S(1)}, u32[]{:S(2)}, u32[]{:S(2)}) collective-permute-start(bf16[256,2048]{1,0:T(8,128)(2,1)S(1)} %pad_maximum_fusion.8), channel_id=1, source_target_pairs={{0,16},{8,24},{16,0},{24,8},{1,17},{9,25},{17,1},{25,9},{2,18},{10... | collective-permute-start | bytes 3145736 | tf_op jit(solution)/shard_map/ppermute | solution.py:532
  507.8 56.9 %collective-permute-start.48 = (bf16[256,3072]{1,0:T(8,128)(2,1)S(1)}, bf16[256,3072]{1,0:T(8,128)(2,1)S(1)}, u32[]{:S(2)}, u32[]{:S(2)}) collective-permute-start(bf16[256,3072]{1,0:T(8,128)(2,1)S(1)} %copy-done.10), channel_id=1, source_target_pairs={{0,16},{8,24},{16,0},{24,8},{1,17},{9,25},{17,1},{25,9},{2,18},{10... | collective-permute-start | bytes 4718600 | tf_op jit(solution)/shard_map/ppermute | solution.py:532
  507.9 56.7 %collective-permute-start.47 = (bf16[256,3072]{1,0:T(8,128)(2,1)S(1)}, bf16[256,3072]{1,0:T(8,128)(2,1)S(1)}, u32[]{:S(2)}, u32[]{:S(2)}) collective-permute-start(bf16[256,3072]{1,0:T(8,128)(2,1)S(1)} %copy-done.10), channel_id=1, source_target_pairs={{0,8},{8,0},{16,24},{24,16},{1,9},{9,1},{17,25},{25,17},{2,10},{10... | collective-permute-start | bytes 4718600 | tf_op jit(solution)/shard_map/ppermute | solution.py:532
  510.0 54.6 %collective-permute-start.44 = (bf16[256,2048]{1,0:T(8,128)(2,1)S(1)}, bf16[256,2048]{1,0:T(8,128)(2,1)S(1)}, u32[]{:S(2)}, u32[]{:S(2)}) collective-permute-start(bf16[256,2048]{1,0:T(8,128)(2,1)S(1)} %pad_maximum_fusion.7), channel_id=1, source_target_pairs={{0,8},{8,0},{16,24},{24,16},{1,9},{9,1},{17,25},{25,17},{2,10},{10... | collective-permute-start | bytes 3145736 | tf_op jit(solution)/shard_map/ppermute | solution.py:532
  511.3 49.5 %collective-permute-start.46 = (f32[1,256]{1,0:T(1,128)S(1)}, f32[1,256]{1,0:T(1,128)S(1)}, u32[]{:S(2)}, u32[]{:S(2)}) collective-permute-start(f32[1,256]{1,0:T(1,128)S(1)} %add.177), channel_id=1, source_target_pairs={{0,16},{8,24},{16,0},{24,8},{1,17},{9,25},{17,1},{25,9},{2,18},{10... | collective-permute-start | bytes 3080 | tf_op jit(solution)/shard_map/ppermute | solution.py:532
  564.8 23.8 %collective-permute-start.49 = (bf16[128,3072]{1,0:T(8,128)(2,1)S(1)}, bf16[128,3072]{1,0:T(8,128)(2,1)}, u32[]{:S(2)}, u32[]{:S(2)}) collective-permute-start(bf16[128,3072]{1,0:T(8,128)(2,1)S(1)} %slice.288), channel_id=1, source_target_pairs={{0,8},{8,0},{16,24},{24,16},{1,9},{9,1},{17,25},{25,17},{2,10},{10... | collective-permute-start | bytes 2359304 | tf_op jit(solution)/shard_map/ppermute | solution.py:532
  565.7 23.8 %collective-permute-start.50 = (bf16[128,3072]{1,0:T(8,128)(2,1)S(1)}, bf16[128,3072]{1,0:T(8,128)(2,1)}, u32[]{:S(2)}, u32[]{:S(2)}) collective-permute-start(bf16[128,3072]{1,0:T(8,128)(2,1)S(1)} %slice.289), channel_id=1, source_target_pairs={{0,16},{8,24},{16,0},{24,8},{1,17},{9,25},{17,1},{25,9},{2,18},{10... | collective-permute-start | bytes 2359304 | tf_op jit(solution)/shard_map/ppermute | solution.py:532
  (110 other events, 1236.0 us)
Sparse Core Ops, SparseCore 0:
  15.7 84.9 all-gather.3
  102.9 115.6 all-gather.5
  220.2 62.9 all-gather.7
  285.3 68.4 reduce-scatter.4
  356.0 127.5 reduce-scatter.6
  499.9 68.6 reduce-scatter.8
  571.5 34.0 reduce-scatter.10

commit v4 on v3

--- a/solution.py
+++ b/solution.py
@@ -528,6 +528,35 @@
     )(rank, *sum(pieces, []), weight)
 
 
+def column_shares_kernel(rank_ref, *refs):
+    start = 0
+    for ref in refs[:-1]:
+        refs[-1][:, start : start + ref.shape[1]] = ref[...]
+        start += ref.shape[1]
+
+
+def column_shares(rank, weights, sizes):
+    rows, width = weights[0].shape[0], sum(sizes)
+    tile = rows // 2
+    return pl.pallas_call(
+        column_shares_kernel,
+        grid_spec=pltpu.PrefetchScalarGridSpec(
+            num_scalar_prefetch=1,
+            grid=(2,),
+            in_specs=[pl.BlockSpec((tile, size), lambda i, r: (i, r[0])) for size in sizes],
+            out_specs=pl.BlockSpec((tile, width), lambda i, r: (i, 0)),
+        ),
+        out_shape=jax.ShapeDtypeStruct((rows, width), weights[0].dtype),
+        compiler_params=pltpu.CompilerParams(
+            dimension_semantics=("arbitrary",), vmem_limit_bytes=VMEM_LIMIT
+        ),
+        cost_estimate=pl.CostEstimate(
+            flops=0, bytes_accessed=4 * rows * width, transcendentals=0
+        ),
+        name="column_shares",
+    )(rank, *weights)
+
+
 def swap(values, bit, axis="sp"):
     return lax.ppermute(values, axis, [(i, i ^ bit) for i in range(lax.axis_size(axis))])
 
@@ -682,9 +711,6 @@
     units = down_weight.shape[0] // count
     ffs = units * shards
 
-    def columns(weight, size):
-        return lax.dynamic_slice_in_dim(weight, rank * size, size, 1)
-
     def gather(weight):
         return lax.all_gather(weight, "fsdp", axis=0, tiled=True)
 
@@ -699,12 +725,9 @@
     places = double_over(positions[0][None], "sp").reshape(-1)
     gains = double_over(jnp.concatenate([attn_gain, mlp_gain, q_gain, k_gain])[None], "fsdp")
     attn_full = gather(
-        jnp.concatenate(
-            [
-                columns(q_weight, qcols), columns(k_weight, kcols), columns(v_weight, kcols),
-                columns(g_weight, qcols), columns(o_weight, dcols),
-            ],
-            axis=1,
+        column_shares(
+            rank_ref, (q_weight, k_weight, v_weight, g_weight, o_weight),
+            (qcols, kcols, kcols, qcols, dcols),
         )
     )
     in_cols = 2 * (qcols + kcols)
@@ -863,15 +886,15 @@
     gain_sums = sum_over(gain_sums, steps[2:3])
     gateup_pieces = gather_pieces(gateup_held)
     gate_grad, gate_sums = weave_units(rank_ref, gateup_pieces, 0, gate_weight, shards)
-    attn_held, out_share, gate_grad, gain_sums = sync(attn_held, out_share, gate_grad, gain_sums)
+    down_grad = stack_rows(rank_ref, gather_pieces(down_held))
+    attn_held, out_share, gate_grad, gain_sums, down_grad = sync(
+        attn_held, out_share, gate_grad, gain_sums, down_grad
+    )
     attn_held = gather_turn(attn_held)
     out_held = gather_start(out_share)
     gain_sums = sum_over(gain_sums, steps[3:4])
-    down_grad = stack_rows(rank_ref, gather_pieces(down_held))
     up_grad, up_sums = weave_units(rank_ref, gateup_pieces, 1, up_weight, shards)
-    attn_held, out_held, gain_sums, up_grad, down_grad = sync(
-        attn_held, out_held, gain_sums, up_grad, down_grad
-    )
+    attn_held, out_held, gain_sums, up_grad = sync(attn_held, out_held, gain_sums, up_grad)
     out_held = gather_turn(out_held)
     gain_sums = sum_over(gain_sums, steps[4:])
     *attn_grads, in_sums = split_columns(

time: 656 us -> 649 us (0.989)
  local copies, waits for them, and re-layouts: 78.1 us -> 69.3 us
    unnamed x151 -> x155, local copies, waits for them, and re-layouts: 45.8 us -> 38.7 us
  transfers between devices with their start and end apart: 71 -> 71, of which waited for: 31 -> 33; matrix products, arithmetic and copies ran while one was open for 36% -> 36% of each run, Pallas kernels for 11% -> 12%
where the time goes in v4:
time: 649 us; the launch traced here: 641 us
  waiting for transfers between devices  227 us (35%)
  matrix products  149 us (23%)
  Pallas kernels  79.1 us (12%)
  starting transfers between devices  72.4 us (11%)
  local copies, waits for them, and re-layouts  69.3 us (11%)
  other arithmetic  25.7 us (4%)
  between operations  18.6 us (3%)
    ppermute x64, waiting for transfers between devices, swap(): lax.ppermute(values, axis, [(i, i ^ bit) for i in range(lax.axis_size(axi...  200 us
    dot_general x24, matrix products, mm(): return lax.dot_general(left, right, dims, preferred_element_type=F32)  149 us
    ppermute x64, starting transfers between devices, swap(): lax.ppermute(values, axis, [(i, i ^ bit) for i in range(lax.axis_size(axi...  71.6 us
    unnamed x155, local copies, waits for them, and re-layouts  38.7 us
    all_gather x3, waiting for transfers between devices, gather(): return lax.all_gather(weight, 'fsdp', axis=0, tiled=True)  25.9 us
    pallas_call x1, Pallas kernels, attend_backward(): pl.pallas_call(functools.partial(attend_bwd_kernel, blocks, rows, groups,...  19 us
    pallas_call x3, Pallas kernels, row_call(): pl.pallas_call(kernel, grid=(4,), in_specs=[spec(a.shape) for a in arrays...  17.6 us
    pallas_call x2, Pallas kernels, weave_units(): pl.pallas_call(functools.partial(weave_units_kernel, [len(block) for bloc...  14.1 us
  transfers between devices with their start and end apart: 71, of which 33 were waited for; matrix products, arithmetic and copies ran while one was open for 36% of the time, Pallas kernels for 12%

profile of v4, /device:TPU:0, one launch (start us, length us, event | category | flops | bytes accessed | tf_op | source)
XLA Modules:
  0.0 641.1 jit_solution(14085650669786735085)
XLA Ops:
  73.5 10.5 %collective-permute-done.10 = bf16[256,2048]{1,0:T(8,128)(2,1)S(1)} collective-permute-done((bf16[256,2048]{1,0:T(8,128)(2,1)S(1)}, bf16[256,2048]{1,0:T(8,128)(2,1)S(1)}, u32[]{:S(2)}, u32[]{:S(2)}) %collective-permute-start.10) | collective-permute-done | bytes 1048608 | tf_op jit(solution)/shard_map/ppermute | solution.py:561
  112.2 10.6 %fusion.29.q_ref.k_ref.v_ref.g_ref = f32[1024,1536]{1,0:T(8,128)} fusion(bf16[1024,2048]{1,0:T(8,128)(2,1)S(1)} %copy-done.12, bf16[2048,2048]{1,0:T(8,128)(2,1)} %all-gather.4.cloned.1.call-done), kind=kOutput, calls=%fused_computation.39 | convolution fusion | flops 6442450944 | bytes 16777216 | tf_op jit(solution)/shard_map/dot_general | solution.py:26
  122.9 6.0 collective-permute-done.14
  128.8 11.4 %attend_forward.1 = (bf16[1024,512]{1,0:T(8,128)(2,1)}, f32[1024,512]{1,0:T(8,128)}, f32[2,4,512]{2,1,0:T(4,128)}) custom-call(s32[1]{0:T(128)} %bitcast.1.rank_ref, f32[1024,1536]{1,0:T(8,128)} %fusion.29.q_ref.k_ref.v_ref.g_ref, f32[1024,1536]{1,0:T(8,128)} %fusion.29.q_ref.k_ref.v_ref.g_ref, f32[1024,1536]{1,0:T(8,128)} %fusion.29.q_ref.k_ref.v_ref.g_ref, ...), custom_call_target="tpu_custom_call" | custom-call | flops 5368709120 | bytes 9437184 | tf_op jit(solution)/shard_map/attend_forward/pallas_call | solution.py:220
  163.8 11.3 %collective-permute-done.17.x_ref = bf16[256,2048]{1,0:T(8,128)(2,1)S(1)} collective-permute-done((bf16[256,2048]{1,0:T(8,128)(2,1)S(1)}, bf16[256,2048]{1,0:T(8,128)(2,1)S(1)}, u32[]{:S(2)}, u32[]{:S(2)}) %collective-permute-start.17) | collective-permute-done | bytes 1048608 | tf_op jit(solution)/shard_map/ppermute | solution.py:561
  184.2 17.4 %collective-permute-done.21 = bf16[256,2048]{1,0:T(8,128)(2,1)S(1)} collective-permute-done((bf16[256,2048]{1,0:T(8,128)(2,1)}, bf16[256,2048]{1,0:T(8,128)(2,1)S(1)}, u32[]{:S(2)}, u32[]{:S(2)}) %collective-permute-start.21) | collective-permute-done | bytes 1048608 | tf_op jit(solution)/shard_map/ppermute | solution.py:561
  216.7 10.4 %fusion.21 = f32[1024,1536]{1,0:T(8,128)S(1)} fusion(bf16[1024,2048]{1,0:T(8,128)(2,1)} %constant_dynamic-update-slice_fusion.10, bf16[2048,3072]{0,1:T(8,128)(2,1)} %all-gather.6.cloned.1.call-done), kind=kOutput, calls=%fused_computation.31 | convolution fusion | flops 6442450944 | bytes 16777216 | tf_op jit(solution)/shard_map/dot_general | solution.py:26
  227.1 12.5 %multiply_convert_fusion.2 = (bf16[1024,1536]{1,0:T(8,128)(2,1)S(1)}, f32[1024,1536]{1,0:T(8,128)}) fusion(f32[1024,1536]{1,0:T(8,128)S(1)} %fusion.21, bf16[1024,2048]{1,0:T(8,128)(2,1)} %constant_dynamic-update-slice_fusion.10, bf16[2048,3072]{0,1:T(8,128)(2,1)S(1)} %copy-done.50), kind=kOutput, calls=%fused_computation.14 | convolution fusion | flops 6451888128 | bytes 26214400 | tf_op jit(solution)/shard_map/dot_general | solution.py:26
  239.6 12.0 %convolution_convert_fusion.2 = bf16[1536,2048]{1,0:T(8,128)(2,1)} fusion(bf16[1024,1536]{1,0:T(8,128)(2,1)S(1)} %get-tuple-element.202, bf16[1024,2048]{1,0:T(8,128)(2,1)} %constant_dynamic-update-slice_fusion.5), kind=kOutput, calls=%fused_computation.8 | convolution fusion | flops 6445596672 | bytes 13631488 | tf_op jit(solution)/shard_map/dot_general | solution.py:26
  251.8 25.9 %all-gather.8.cloned.1.call-done = bf16[1536,2048]{1,0:T(8,128)(2,1)} async-done(((bf16[192,2048]{1,0:T(8,128)(2,1)}), bf16[1536,2048]{1,0:T(8,128)(2,1)}) %all-gather.8.cloned.1.call-update) | async-done | bytes 6291472 | tf_op jit(solution)/shard_map/all_gather | solution.py:715
  294.1 14.4 %multiply_convert_fusion = (bf16[1024,1536]{1,0:T(8,128)(2,1)}, bf16[1024,1536]{1,0:T(8,128)(2,1)}) fusion(f32[1024,1536]{1,0:T(8,128)} %copy-done.60, f32[1024,1536]{1,0:T(8,128)} %get-tuple-element.355, bf16[1024,2048]{1,0:T(8,128)(2,1)} %constant_dynamic-update-slice_fusion.5, bf16[1536,2048]{1,0:T(8,128)(2,1)S(1)} %copy-done.51), kind=kOutput, calls=%fused_computation.12 | convolution fusion | flops 6462898176 | bytes 29360128 | tf_op jit(solution)/shard_map/dot_general | solution.py:26
  312.0 18.7 %convolution_convert_fusion = bf16[2048,3072]{1,0:T(8,128)(2,1)} fusion(bf16[1024,2048]{1,0:T(8,128)(2,1)} %constant_dynamic-update-slice_fusion.10, bf16[1024,1536]{1,0:T(8,128)(2,1)S(1)} %copy-done.55, bf16[1024,1536]{1,0:T(8,128)(2,1)S(1)} %copy-done.53), kind=kOutput, calls=%fused_computation.1 | convolution fusion | flops 12903776256 | bytes 23068672 | tf_op jit(solution)/shard_map/dot_general | solution.py:26
  366.8 17.9 %collective-permute-done.31.y_ref = bf16[256,2048]{1,0:T(8,128)(2,1)S(1)} collective-permute-done((bf16[256,2048]{1,0:T(8,128)(2,1)S(1)}, bf16[256,2048]{1,0:T(8,128)(2,1)S(1)}, u32[]{:S(2)}, u32[]{:S(2)}) %collective-permute-start.31) | collective-permute-done | bytes 1048608 | tf_op jit(solution)/shard_map/ppermute | solution.py:561
  386.2 6.4 norm_back.2
  395.6 19.4 %collective-permute-done.33 = bf16[256,2048]{1,0:T(8,128)(2,1)S(1)} collective-permute-done((bf16[256,2048]{1,0:T(8,128)(2,1)}, bf16[256,2048]{1,0:T(8,128)(2,1)S(1)}, u32[]{:S(2)}, u32[]{:S(2)}) %collective-permute-start.33) | collective-permute-done | bytes 1048608 | tf_op jit(solution)/shard_map/ppermute | solution.py:561
  419.3 8.0 %collective-permute-done.34 = bf16[128,2048]{1,0:T(8,128)(2,1)S(1)} collective-permute-done((bf16[128,2048]{1,0:T(8,128)(2,1)S(1)}, bf16[128,2048]{1,0:T(8,128)(2,1)S(1)}, u32[]{:S(2)}, u32[]{:S(2)}) %collective-permute-start.34) | collective-permute-done | bytes 524320 | tf_op jit(solution)/shard_map/ppermute | solution.py:561
  441.2 19.0 %attend_backward.1 = (bf16[1024,1536]{1,0:T(8,128)(2,1)}, f32[1,128]{1,0:T(1,128)}, f32[1,128]{1,0:T(1,128)}) custom-call(s32[1]{0:T(128)} %bitcast.1.rank_ref, f32[1024,1536]{1,0:T(8,128)} %fusion.29.q_ref.k_ref.v_ref.g_ref, f32[1024,1536]{1,0:T(8,128)} %fusion.29.q_ref.k_ref.v_ref.g_ref, f32[1024,1536]{1,0:T(8,128)} %fusion.29.q_ref.k_ref.v_ref.g_ref, ...), custom_call_target="tpu_custom_call" | custom-call | flops 13421772800 | bytes 12582912 | tf_op jit(solution)/shard_map/attend_backward/pallas_call | solution.py:257
  460.2 10.7 %convolution_convert_fusion.1 = bf16[2048,1536]{1,0:T(8,128)(2,1)} fusion(bf16[1024,2048]{1,0:T(8,128)(2,1)S(1)} %copy-done.13, bf16[1024,1536]{1,0:T(8,128)(2,1)} %get-tuple-element.247), kind=kOutput, calls=%fused_computation.7 | convolution fusion | flops 6445596672 | bytes 13631488 | tf_op jit(solution)/shard_map/dot_general | solution.py:26
  507.7 47.6 %collective-permute-done.46 = f32[1,256]{1,0:T(1,128)S(1)} collective-permute-done((f32[1,256]{1,0:T(1,128)S(1)}, f32[1,256]{1,0:T(1,128)S(1)}, u32[]{:S(2)}, u32[]{:S(2)}) %collective-permute-start.46) | collective-permute-done | bytes 1056 | tf_op jit(solution)/shard_map/ppermute | solution.py:561
  566.9 5.9 norm_back.3
  572.9 10.4 %collective-permute-done.51.refs_3_ = bf16[96,2048]{1,0:T(8,128)(2,1)S(1)} collective-permute-done((bf16[96,2048]{1,0:T(8,128)(2,1)}, bf16[96,2048]{1,0:T(8,128)(2,1)S(1)}, u32[]{:S(2)}, u32[]{:S(2)}) %collective-permute-start.51) | collective-permute-done | bytes 393248 | tf_op jit(solution)/shard_map/ppermute | solution.py:561
  592.6 7.0 %weave_units.2 = (f32[256,6144]{1,0:T(8,128)}, f32[256,1]{1,0:T(8,128)}) custom-call(s32[1]{0:T(128)} %bitcast.1.rank_ref, bf16[256,3072]{1,0:T(8,128)(2,1)} %reduce-scatter.7.cloned.1.call-done.refs_0_, bf16[256,3072]{1,0:T(8,128)(2,1)} %copy-done.5, bf16[256,3072]{1,0:T(8,128)(2,1)} %copy-done.4, bf16[128,3072]{1,0:T(8,128)(2,1)} %collective-permute-done.49.refs_3_, ...), custom_call_target="tpu_custom_call" | custom-call | bytes 12582912 | tf_op jit(solution)/shard_map/weave_units/pallas_call | solution.py:503
  603.3 7.1 %weave_units.3 = (f32[256,6144]{1,0:T(8,128)}, f32[256,1]{1,0:T(8,128)}) custom-call(s32[1]{0:T(128)} %bitcast.1.rank_ref, bf16[256,3072]{1,0:T(8,128)(2,1)} %reduce-scatter.7.cloned.1.call-done.refs_0_, bf16[256,3072]{1,0:T(8,128)(2,1)} %copy-done.5, bf16[256,3072]{1,0:T(8,128)(2,1)} %copy-done.4, bf16[128,3072]{1,0:T(8,128)(2,1)} %collective-permute-done.49.refs_3_, ...), custom_call_target="tpu_custom_call" | custom-call | bytes 12582912 | tf_op jit(solution)/shard_map/weave_units/pallas_call | solution.py:503
  621.2 6.7 %split_columns.2 = (f32[256,2048]{1,0:T(8,128)}, f32[256,1024]{1,0:T(8,128)}, f32[256,1024]{1,0:T(8,128)}, f32[256,2048]{1,0:T(8,128)}, f32[256,1]{1,0:T(8,128)}) custom-call(s32[1]{0:T(128)} %bitcast.1.rank_ref, bf16[256,1536]{1,0:T(8,128)(2,1)} %reduce-scatter.9.cloned.1.call-done.refs_0_, bf16[256,1536]{1,0:T(8,128)(2,1)} %copy-done.19, ...), custom_call_target="tpu_custom_call" | custom-call | bytes 9437184 | tf_op jit(solution)/shard_map/split_columns/pallas_call | solution.py:410
  (421 shorter events, 295.1 us)
Async XLA Ops:
  7.3 99.6 %all-gather.4.cloned.1.call-start = ((), (), s32[]{:S(2)}) async-start(), calls=%async_computation.4 | async-start | bytes 9437184 | tf_op jit(solution)/shard_map/all_gather | solution.py:715
  9.6 207.1 %all-gather.6.cloned.1.call-start = ((), (), s32[]{:S(2)}) async-start(), calls=%async_computation.5 | async-start | bytes 14155776 | tf_op jit(solution)/shard_map/all_gather | solution.py:715
  9.7 33.1 %collective-permute-start.1 = (bf16[256,2048]{1,0:T(8,128)(2,1)}, bf16[256,2048]{1,0:T(8,128)(2,1)}, u32[]{:S(2)}, u32[]{:S(2)}) collective-permute-start(bf16[256,2048]{1,0:T(8,128)(2,1)} %bitcast.65), channel_id=1, source_target_pairs={{0,16},{8,24},{16,0},{24,8},{1,17},{9,25},{17,1},{25,9},{2,18},{10... | collective-permute-start | bytes 3145736 | tf_op jit(solution)/shard_map/ppermute | solution.py:561
  12.7 30.1 %collective-permute-start = (bf16[256,2048]{1,0:T(8,128)(2,1)}, bf16[256,2048]{1,0:T(8,128)(2,1)}, u32[]{:S(2)}, u32[]{:S(2)}) collective-permute-start(bf16[256,2048]{1,0:T(8,128)(2,1)} %bitcast.66), channel_id=1, source_target_pairs={{0,8},{8,0},{16,24},{24,16},{1,9},{9,1},{17,25},{25,17},{2,10},{10... | collective-permute-start | bytes 3145736 | tf_op jit(solution)/shard_map/ppermute | solution.py:561
  58.0 219.7 %all-gather.8.cloned.1.call-start = ((), (), s32[]{:S(2)}) async-start(), calls=%async_computation.6 | async-start | bytes 7077888 | tf_op jit(solution)/shard_map/all_gather | solution.py:715
  149.1 286.6 %reduce-scatter.5.cloned.1.call-start = ((), (), s32[]{:S(2)}) async-start(), calls=%async_computation.7 | async-start | bytes 7077888 | tf_op jit(solution)/shard_map/reduce_scatter | solution.py:722
  251.6 242.7 %reduce-scatter.7.cloned.1.call-start = ((), (), s32[]{:S(2)}) async-start(), calls=%async_computation.8 | async-start | bytes 14155776 | tf_op jit(solution)/shard_map/reduce_scatter | solution.py:722
  310.0 25.0 %collective-permute-start.27 = (bf16[256,2048]{1,0:T(8,128)(2,1)}, bf16[256,2048]{1,0:T(8,128)(2,1)}, u32[]{:S(2)}, u32[]{:S(2)}) collective-permute-start(bf16[256,2048]{1,0:T(8,128)(2,1)} %pad_maximum_fusion.4), channel_id=1, source_target_pairs={{0,16},{8,24},{16,0},{24,8},{1,17},{9,25},{17,1},{25,9},{2,18},{10... | collective-permute-start | bytes 3145736 | tf_op jit(solution)/shard_map/ppermute | solution.py:561
  310.8 24.5 %collective-permute-start.26 = (bf16[256,2048]{1,0:T(8,128)(2,1)S(1)}, bf16[256,2048]{1,0:T(8,128)(2,1)S(1)}, u32[]{:S(2)}, u32[]{:S(2)}) collective-permute-start(bf16[256,2048]{1,0:T(8,128)(2,1)S(1)} %pad_maximum_fusion.3), channel_id=1, source_target_pairs={{0,8},{8,0},{16,24},{24,16},{1,9},{9,1},{17,25},{25,17},{2,10},{10... | collective-permute-start | bytes 3145736 | tf_op jit(solution)/shard_map/ppermute | solution.py:561
  336.3 247.7 %reduce-scatter.9.cloned.1.call-start = ((), (), s32[]{:S(2)}) async-start(), calls=%async_computation.9 | async-start | bytes 7077888 | tf_op jit(solution)/shard_map/reduce_scatter | solution.py:722
  394.2 24.0 %collective-permute-start.32 = (bf16[256,2048]{1,0:T(8,128)(2,1)}, bf16[256,2048]{1,0:T(8,128)(2,1)S(1)}, u32[]{:S(2)}, u32[]{:S(2)}) collective-permute-start(bf16[256,2048]{1,0:T(8,128)(2,1)} %get-tuple-element.229), channel_id=1, source_target_pairs={{0,8},{8,0},{16,24},{24,16},{1,9},{9,1},{17,25},{25,17},{2,10},{10... | collective-permute-start | bytes 3145736 | tf_op jit(solution)/shard_map/ppermute | solution.py:561
  435.6 58.7 %collective-permute-start.42 = (bf16[192,2048]{1,0:T(8,128)(2,1)}, bf16[192,2048]{1,0:T(8,128)(2,1)}, u32[]{:S(2)}, u32[]{:S(2)}) collective-permute-start(bf16[192,2048]{1,0:T(8,128)(2,1)} %reduce-scatter.5.cloned.1.call-done.refs_0_), channel_id=1, source_target_pairs={{0,16},{8,24},{16,0},{24,8},{1,17},{9,25},{17,1},{25,9},{2,18},{10... | collective-permute-start | bytes 2359304 | tf_op jit(solution)/shard_map/ppermute | solution.py:561
  436.8 57.5 %collective-permute-start.41 = (bf16[192,2048]{1,0:T(8,128)(2,1)}, bf16[192,2048]{1,0:T(8,128)(2,1)}, u32[]{:S(2)}, u32[]{:S(2)}) collective-permute-start(bf16[192,2048]{1,0:T(8,128)(2,1)} %reduce-scatter.5.cloned.1.call-done.refs_0_), channel_id=1, source_target_pairs={{0,8},{8,0},{16,24},{24,16},{1,9},{9,1},{17,25},{25,17},{2,10},{10... | collective-permute-start | bytes 2359304 | tf_op jit(solution)/shard_map/ppermute | solution.py:561
  437.7 33.4 %collective-permute-start.36 = (bf16[512,512]{1,0:T(8,128)(2,1)}, bf16[512,512]{1,0:T(8,128)(2,1)S(1)}, u32[]{:S(2)}, u32[]{:S(2)}) collective-permute-start(bf16[512,512]{1,0:T(8,128)(2,1)} %get-tuple-element.236), channel_id=1, source_target_pairs={{0,8},{8,0},{16,24},{24,16},{1,9},{9,1},{17,25},{25,17},{2,10},{10... | collective-permute-start | bytes 1572872 | tf_op jit(solution)/shard_map/ppermute | solution.py:561
  438.8 32.2 %collective-permute-start.37 = (bf16[512,512]{1,0:T(8,128)(2,1)}, bf16[512,512]{1,0:T(8,128)(2,1)S(1)}, u32[]{:S(2)}, u32[]{:S(2)}) collective-permute-start(bf16[512,512]{1,0:T(8,128)(2,1)} %get-tuple-element.237), channel_id=1, source_target_pairs={{0,16},{8,24},{16,0},{24,8},{1,17},{9,25},{17,1},{25,9},{2,18},{10... | collective-permute-start | bytes 1572872 | tf_op jit(solution)/shard_map/ppermute | solution.py:561
  439.7 36.7 %collective-permute-start.38 = (bf16[512,512]{1,0:T(8,128)(2,1)}, bf16[512,512]{1,0:T(8,128)(2,1)S(1)}, u32[]{:S(2)}, u32[]{:S(2)}) collective-permute-start(bf16[512,512]{1,0:T(8,128)(2,1)} %get-tuple-element.238), channel_id=1, source_target_pairs={{0,24},{8,16},{16,8},{24,0},{1,25},{9,17},{17,9},{25,1},{2,26},{10... | collective-permute-start | bytes 1572872 | tf_op jit(solution)/shard_map/ppermute | solution.py:561
  494.4 105.8 %reduce-scatter.11.cloned.1.call-start = ((), (), s32[]{:S(2)}) async-start(), calls=%async_computation.10 | async-start | bytes 2359296 | tf_op jit(solution)/shard_map/reduce_scatter | solution.py:722
  500.4 55.0 %collective-permute-start.45 = (bf16[256,2048]{1,0:T(8,128)(2,1)S(1)}, bf16[256,2048]{1,0:T(8,128)(2,1)S(1)}, u32[]{:S(2)}, u32[]{:S(2)}) collective-permute-start(bf16[256,2048]{1,0:T(8,128)(2,1)S(1)} %pad_maximum_fusion.8), channel_id=1, source_target_pairs={{0,16},{8,24},{16,0},{24,8},{1,17},{9,25},{17,1},{25,9},{2,18},{10... | collective-permute-start | bytes 3145736 | tf_op jit(solution)/shard_map/ppermute | solution.py:561
  502.3 56.9 %collective-permute-start.48 = (bf16[256,3072]{1,0:T(8,128)(2,1)S(1)}, bf16[256,3072]{1,0:T(8,128)(2,1)S(1)}, u32[]{:S(2)}, u32[]{:S(2)}) collective-permute-start(bf16[256,3072]{1,0:T(8,128)(2,1)S(1)} %copy-done.10), channel_id=1, source_target_pairs={{0,16},{8,24},{16,0},{24,8},{1,17},{9,25},{17,1},{25,9},{2,18},{10... | collective-permute-start | bytes 4718600 | tf_op jit(solution)/shard_map/ppermute | solution.py:561
  502.4 56.7 %collective-permute-start.47 = (bf16[256,3072]{1,0:T(8,128)(2,1)S(1)}, bf16[256,3072]{1,0:T(8,128)(2,1)S(1)}, u32[]{:S(2)}, u32[]{:S(2)}) collective-permute-start(bf16[256,3072]{1,0:T(8,128)(2,1)S(1)} %copy-done.10), channel_id=1, source_target_pairs={{0,8},{8,0},{16,24},{24,16},{1,9},{9,1},{17,25},{25,17},{2,10},{10... | collective-permute-start | bytes 4718600 | tf_op jit(solution)/shard_map/ppermute | solution.py:561
  504.7 54.5 %collective-permute-start.44 = (bf16[256,2048]{1,0:T(8,128)(2,1)S(1)}, bf16[256,2048]{1,0:T(8,128)(2,1)S(1)}, u32[]{:S(2)}, u32[]{:S(2)}) collective-permute-start(bf16[256,2048]{1,0:T(8,128)(2,1)S(1)} %pad_maximum_fusion.7), channel_id=1, source_target_pairs={{0,8},{8,0},{16,24},{24,16},{1,9},{9,1},{17,25},{25,17},{2,10},{10... | collective-permute-start | bytes 3145736 | tf_op jit(solution)/shard_map/ppermute | solution.py:561
  505.8 49.5 %collective-permute-start.46 = (f32[1,256]{1,0:T(1,128)S(1)}, f32[1,256]{1,0:T(1,128)S(1)}, u32[]{:S(2)}, u32[]{:S(2)}) collective-permute-start(f32[1,256]{1,0:T(1,128)S(1)} %add.169), channel_id=1, source_target_pairs={{0,16},{8,24},{16,0},{24,8},{1,17},{9,25},{17,1},{25,9},{2,18},{10... | collective-permute-start | bytes 3080 | tf_op jit(solution)/shard_map/ppermute | solution.py:561
  559.3 23.9 %collective-permute-start.49 = (bf16[128,3072]{1,0:T(8,128)(2,1)S(1)}, bf16[128,3072]{1,0:T(8,128)(2,1)}, u32[]{:S(2)}, u32[]{:S(2)}) collective-permute-start(bf16[128,3072]{1,0:T(8,128)(2,1)S(1)} %slice.288), channel_id=1, source_target_pairs={{0,8},{8,0},{16,24},{24,16},{1,9},{9,1},{17,25},{25,17},{2,10},{10... | collective-permute-start | bytes 2359304 | tf_op jit(solution)/shard_map/ppermute | solution.py:561
  560.3 23.7 %collective-permute-start.50 = (bf16[128,3072]{1,0:T(8,128)(2,1)S(1)}, bf16[128,3072]{1,0:T(8,128)(2,1)}, u32[]{:S(2)}, u32[]{:S(2)}) collective-permute-start(bf16[128,3072]{1,0:T(8,128)(2,1)S(1)} %slice.289), channel_id=1, source_target_pairs={{0,16},{8,24},{16,0},{24,8},{1,17},{9,25},{17,1},{25,9},{2,18},{10... | collective-permute-start | bytes 2359304 | tf_op jit(solution)/shard_map/ppermute | solution.py:561
  (114 other events, 1254.8 us)
Sparse Core Ops, SparseCore 0:
  10.3 84.9 all-gather.3
  97.4 115.6 all-gather.5
  214.7 62.9 all-gather.7
  279.9 68.4 reduce-scatter.4
  350.5 127.5 reduce-scatter.6
  494.5 68.7 reduce-scatter.8
  566.1 33.9 reduce-scatter.10

commit v5 on v4

--- a/solution.py
+++ b/solution.py
@@ -318,7 +318,7 @@
 
 def row_call(kernel, name, arrays, gain, outs):
     rows, width = arrays[0].shape
-    tile = rows // 4
+    tile = rows // 2
 
     def spec(shape):
         if shape[0] == rows:
@@ -327,7 +327,7 @@
 
     return pl.pallas_call(
         kernel,
-        grid=(4,),
+        grid=(2,),
         in_specs=[spec(a.shape) for a in arrays] + [spec(gain.shape)],
         out_specs=[spec(o.shape) for o in outs],
         out_shape=outs,
@@ -489,7 +489,7 @@
 
 def weave_units(rank, pieces, group, weight, shards):
     count, (rows, width) = len(pieces), pieces[0][0].shape
-    ffs, steps = width // 2, 4
+    ffs, steps = width // 2, 2
     tile = rows // steps
 
     def spec(block, k):
@@ -602,10 +602,42 @@
 def scatter_turn(others, came):
     if lax.axis_size("sp") != 4:
         return [swap(part.astype(BF16), j + 1) for j, part in enumerate(others)]
-    half = others[0].shape[0] // 2
-    to_x = jnp.concatenate([others[0][:half], others[0][half:] + came[1].astype(F32)], axis=0)
-    to_y = jnp.concatenate([others[1][:half] + came[0].astype(F32), others[1][half:]], axis=0)
-    return [swap(to_x.astype(BF16), 1), swap(to_y.astype(BF16), 2)]
+    to_x, to_y = add_corner(others, came)
+    return [swap(to_x, 1), swap(to_y, 2)]
+
+
+def add_corner_kernel(whole_ref, from_x_ref, from_y_ref, to_x_ref, to_y_ref):
+    half = from_x_ref.shape[0]
+
+    @pl.when(pl.program_id(0) == 0)
+    def _():
+        to_x_ref[:half, :] = whole_ref[:half, :].astype(BF16)
+        to_x_ref[half:, :] = (whole_ref[half:, :] + from_y_ref[...].astype(F32)).astype(BF16)
+
+    @pl.when(pl.program_id(0) == 1)
+    def _():
+        to_y_ref[:half, :] = (whole_ref[:half, :] + from_x_ref[...].astype(F32)).astype(BF16)
+        to_y_ref[half:, :] = whole_ref[half:, :].astype(BF16)
+
+
+def add_corner(whole, came):
+    rows, width = whole.shape[0] // 2, whole.shape[1]
+    half = pl.BlockSpec((rows // 2, width), lambda i: (0, 0))
+    out = pl.BlockSpec((rows, width), lambda i: (0, 0))
+    return pl.pallas_call(
+        add_corner_kernel,
+        grid=(2,),
+        in_specs=[pl.BlockSpec((rows, width), lambda i: (i, 0)), half, half],
+        out_specs=[out, out],
+        out_shape=[jax.ShapeDtypeStruct((rows, width), BF16)] * 2,
+        compiler_params=pltpu.CompilerParams(
+            dimension_semantics=("arbitrary",), vmem_limit_bytes=32 * 1024 * 1024
+        ),
+        cost_estimate=pl.CostEstimate(
+            flops=rows * width, bytes_accessed=14 * rows * width, transcendentals=0
+        ),
+        name="add_corner",
+    )(whole, *came)
 
 
 def scatter_end(own, came):
@@ -623,6 +655,8 @@
     count = lax.axis_size("sp")
     stop = 3 if count == 4 else count
     whole = make(rows, stop * rows)
+    if count == 4:
+        return whole
     return [whole[j * rows : (j + 1) * rows] for j in range(stop - 1)]
 
 
@@ -854,13 +888,15 @@
     steps = sum_steps()
     gain_sums = jnp.concatenate([query_gain_part, key_gain_part], axis=1)
     attn_grad = mm(first, grad_raw, TN).astype(BF16)
-    attn_grad, grad_raw, gain_sums, out_blocks = sync(attn_grad, grad_raw, gain_sums, out_blocks)
+    attn_grad, grad_raw, gain_sums = sync(attn_grad, grad_raw, gain_sums)
 
     def first_rows(lo, hi):
         return mm(grad_raw[lo:hi], w_in, NT)
 
     corner = corner_rows(first_rows, rows)
-    corner, grad_raw, attn_grad, gain_sums = sync(corner, grad_raw, attn_grad, gain_sums)
+    corner, grad_raw, attn_grad, gain_sums, out_blocks = sync(
+        corner, grad_raw, attn_grad, gain_sums, out_blocks
+    )
     corner = scatter_start(corner)
     gain_sums = sum_over(gain_sums, steps[:1])
     others = other_rows(first_rows, rows)

time: 649 us -> 642 us (0.989)
  waiting for transfers between devices: 227 us -> 236 us
    slice x10 -> x0, local copies, waits for them, and re-layouts: 7.34 us -> none  [the longest x3 3.05 us: other_rows(): return [whole[j * rows:(j + 1) * rows] for j in range(stop - 1)]]
    unnamed x155 -> x159, local copies, waits for them, and re-layouts: 38.7 us -> 41.1 us
    pallas_call x3 -> x7, Pallas kernels: 17.6 us -> 16.2 us  [the longest x3 14.5 us: row_call(): pl.pallas_call(kernel, grid=(2,), in_specs=[spec(a.shape) for a in arrays...]
  transfers between devices with their start and end apart: 71 -> 71, of which waited for: 33 -> 33; matrix products, arithmetic and copies ran while one was open for 36% -> 35% of each run, Pallas kernels for 12% -> 11%
where the time goes in v5:
time: 642 us; the launch traced here: 634 us
  waiting for transfers between devices  236 us (37%)
  matrix products  150 us (23%)
  Pallas kernels  76.4 us (12%)
  starting transfers between devices  70 us (11%)
  local copies, waits for them, and re-layouts  63.7 us (10%)
  other arithmetic  19.4 us (3%)
  between operations  18.1 us (3%)
    ppermute x64, waiting for transfers between devices, swap(): lax.ppermute(values, axis, [(i, i ^ bit) for i in range(lax.axis_size(axi...  202 us
    dot_general x24, matrix products, mm(): return lax.dot_general(left, right, dims, preferred_element_type=F32)  150 us
    ppermute x64, starting transfers between devices, swap(): lax.ppermute(values, axis, [(i, i ^ bit) for i in range(lax.axis_size(axi...  69.1 us
    unnamed x159, local copies, waits for them, and re-layouts  41.1 us
    all_gather x3, waiting for transfers between devices, gather(): return lax.all_gather(weight, 'fsdp', axis=0, tiled=True)  27.4 us
    pallas_call x1, Pallas kernels, attend_backward(): pl.pallas_call(functools.partial(attend_bwd_kernel, blocks, rows, groups,...  19.6 us
    pallas_call x3, Pallas kernels, row_call(): pl.pallas_call(kernel, grid=(2,), in_specs=[spec(a.shape) for a in arrays...  14.5 us
  transfers between devices with their start and end apart: 71, of which 33 were waited for; matrix products, arithmetic and copies ran while one was open for 35% of the time, Pallas kernels for 11%

profile of v5, /device:TPU:0, one launch (start us, length us, event | category | flops | bytes accessed | tf_op | source)
XLA Modules:
  0.0 634.1 jit_solution(1572820270116192451)
XLA Ops:
  73.5 10.5 %collective-permute-done.10 = bf16[256,2048]{1,0:T(8,128)(2,1)S(1)} collective-permute-done((bf16[256,2048]{1,0:T(8,128)(2,1)S(1)}, bf16[256,2048]{1,0:T(8,128)(2,1)S(1)}, u32[]{:S(2)}, u32[]{:S(2)}) %collective-permute-start.10) | collective-permute-done | bytes 1048608 | tf_op jit(solution)/shard_map/ppermute | solution.py:561
  112.2 10.9 %fusion.29.q_ref.k_ref.v_ref.g_ref = f32[1024,1536]{1,0:T(8,128)} fusion(bf16[1024,2048]{1,0:T(8,128)(2,1)S(1)} %copy-done.11, bf16[2048,2048]{1,0:T(8,128)(2,1)} %all-gather.4.cloned.1.call-done), kind=kOutput, calls=%fused_computation.39 | convolution fusion | flops 6442450944 | bytes 16777216 | tf_op jit(solution)/shard_map/dot_general | solution.py:26
  128.9 11.8 %attend_forward.1 = (bf16[1024,512]{1,0:T(8,128)(2,1)}, f32[1024,512]{1,0:T(8,128)}, f32[2,4,512]{2,1,0:T(4,128)}) custom-call(s32[1]{0:T(128)} %bitcast.1.rank_ref, f32[1024,1536]{1,0:T(8,128)} %fusion.29.q_ref.k_ref.v_ref.g_ref, f32[1024,1536]{1,0:T(8,128)} %fusion.29.q_ref.k_ref.v_ref.g_ref, f32[1024,1536]{1,0:T(8,128)} %fusion.29.q_ref.k_ref.v_ref.g_ref, ...), custom_call_target="tpu_custom_call" | custom-call | flops 5368709120 | bytes 9437184 | tf_op jit(solution)/shard_map/attend_forward/pallas_call | solution.py:220
  146.2 9.8 %collective-permute-done.17.from_y_ref = bf16[128,2048]{1,0:T(8,128)(2,1)S(1)} collective-permute-done((bf16[128,2048]{1,0:T(8,128)(2,1)S(1)}, bf16[128,2048]{1,0:T(8,128)(2,1)S(1)}, u32[]{:S(2)}, u32[]{:S(2)}) %collective-permute-start.17) | collective-permute-done | bytes 524320 | tf_op jit(solution)/shard_map/ppermute | solution.py:561
  163.7 12.2 %collective-permute-done.18.x_ref = bf16[256,2048]{1,0:T(8,128)(2,1)S(1)} collective-permute-done((bf16[256,2048]{1,0:T(8,128)(2,1)S(1)}, bf16[256,2048]{1,0:T(8,128)(2,1)S(1)}, u32[]{:S(2)}, u32[]{:S(2)}) %collective-permute-start.18) | collective-permute-done | bytes 1048608 | tf_op jit(solution)/shard_map/ppermute | solution.py:561
  183.1 18.4 %collective-permute-done.21 = bf16[256,2048]{1,0:T(8,128)(2,1)S(1)} collective-permute-done((bf16[256,2048]{1,0:T(8,128)(2,1)}, bf16[256,2048]{1,0:T(8,128)(2,1)S(1)}, u32[]{:S(2)}, u32[]{:S(2)}) %collective-permute-start.21) | collective-permute-done | bytes 1048608 | tf_op jit(solution)/shard_map/ppermute | solution.py:561
  215.0 10.2 %fusion.21 = f32[1024,1536]{1,0:T(8,128)S(1)} fusion(bf16[1024,2048]{1,0:T(8,128)(2,1)} %constant_dynamic-update-slice_fusion.10, bf16[2048,3072]{0,1:T(8,128)(2,1)} %all-gather.6.cloned.1.call-done), kind=kOutput, calls=%fused_computation.31 | convolution fusion | flops 6442450944 | bytes 16777216 | tf_op jit(solution)/shard_map/dot_general | solution.py:26
  225.3 12.5 %multiply_convert_fusion.2 = (bf16[1024,1536]{1,0:T(8,128)(2,1)S(1)}, f32[1024,1536]{1,0:T(8,128)}) fusion(f32[1024,1536]{1,0:T(8,128)S(1)} %fusion.21, bf16[1024,2048]{1,0:T(8,128)(2,1)} %constant_dynamic-update-slice_fusion.10, bf16[2048,3072]{0,1:T(8,128)(2,1)S(1)} %copy-done.53), kind=kOutput, calls=%fused_computation.14 | convolution fusion | flops 6451888128 | bytes 26214400 | tf_op jit(solution)/shard_map/dot_general | solution.py:26
  237.7 12.1 %convolution_convert_fusion.2 = bf16[1536,2048]{1,0:T(8,128)(2,1)} fusion(bf16[1024,1536]{1,0:T(8,128)(2,1)S(1)} %get-tuple-element.209, bf16[1024,2048]{1,0:T(8,128)(2,1)} %constant_dynamic-update-slice_fusion.5), kind=kOutput, calls=%fused_computation.8 | convolution fusion | flops 6445596672 | bytes 13631488 | tf_op jit(solution)/shard_map/dot_general | solution.py:26
  250.3 27.4 %all-gather.8.cloned.1.call-done = bf16[1536,2048]{1,0:T(8,128)(2,1)} async-done(((bf16[192,2048]{1,0:T(8,128)(2,1)}), bf16[1536,2048]{1,0:T(8,128)(2,1)}) %all-gather.8.cloned.1.call-update) | async-done | bytes 6291472 | tf_op jit(solution)/shard_map/all_gather | solution.py:749
  293.8 14.4 %multiply_convert_fusion = (bf16[1024,1536]{1,0:T(8,128)(2,1)}, bf16[1024,1536]{1,0:T(8,128)(2,1)}) fusion(f32[1024,1536]{1,0:T(8,128)} %copy-done.62, f32[1024,1536]{1,0:T(8,128)} %get-tuple-element.353, bf16[1024,2048]{1,0:T(8,128)(2,1)} %constant_dynamic-update-slice_fusion.5, bf16[1536,2048]{1,0:T(8,128)(2,1)S(1)} %copy-done.54), kind=kOutput, calls=%fused_computation.12 | convolution fusion | flops 6462898176 | bytes 29360128 | tf_op jit(solution)/shard_map/dot_general | solution.py:26
  310.1 18.7 %convolution_convert_fusion = bf16[2048,3072]{1,0:T(8,128)(2,1)} fusion(bf16[1024,2048]{1,0:T(8,128)(2,1)} %constant_dynamic-update-slice_fusion.10, bf16[1024,1536]{1,0:T(8,128)(2,1)} %get-tuple-element.222, bf16[1024,1536]{1,0:T(8,128)(2,1)S(1)} %copy-done.56), kind=kOutput, calls=%fused_computation.1 | convolution fusion | flops 12903776256 | bytes 23068672 | tf_op jit(solution)/shard_map/dot_general | solution.py:26
  364.2 17.8 %collective-permute-done.30.x_ref = bf16[256,2048]{1,0:T(8,128)(2,1)S(1)} collective-permute-done((bf16[256,2048]{1,0:T(8,128)(2,1)S(1)}, bf16[256,2048]{1,0:T(8,128)(2,1)S(1)}, u32[]{:S(2)}, u32[]{:S(2)}) %collective-permute-start.30) | collective-permute-done | bytes 1048608 | tf_op jit(solution)/shard_map/ppermute | solution.py:561
  391.7 19.5 %collective-permute-done.33 = bf16[256,2048]{1,0:T(8,128)(2,1)S(1)} collective-permute-done((bf16[256,2048]{1,0:T(8,128)(2,1)}, bf16[256,2048]{1,0:T(8,128)(2,1)S(1)}, u32[]{:S(2)}, u32[]{:S(2)}) %collective-permute-start.33) | collective-permute-done | bytes 1048608 | tf_op jit(solution)/shard_map/ppermute | solution.py:561
  415.6 8.1 %collective-permute-done.34 = bf16[128,2048]{1,0:T(8,128)(2,1)S(1)} collective-permute-done((bf16[128,2048]{1,0:T(8,128)(2,1)S(1)}, bf16[128,2048]{1,0:T(8,128)(2,1)S(1)}, u32[]{:S(2)}, u32[]{:S(2)}) %collective-permute-start.34) | collective-permute-done | bytes 524320 | tf_op jit(solution)/shard_map/ppermute | solution.py:561
  437.7 19.6 %attend_backward.1 = (bf16[1024,1536]{1,0:T(8,128)(2,1)}, f32[1,128]{1,0:T(1,128)}, f32[1,128]{1,0:T(1,128)}) custom-call(s32[1]{0:T(128)} %bitcast.1.rank_ref, f32[1024,1536]{1,0:T(8,128)} %fusion.29.q_ref.k_ref.v_ref.g_ref, f32[1024,1536]{1,0:T(8,128)} %fusion.29.q_ref.k_ref.v_ref.g_ref, f32[1024,1536]{1,0:T(8,128)} %fusion.29.q_ref.k_ref.v_ref.g_ref, ...), custom_call_target="tpu_custom_call" | custom-call | flops 13421772800 | bytes 12582912 | tf_op jit(solution)/shard_map/attend_backward/pallas_call | solution.py:257
  458.0 10.5 %convolution_convert_fusion.1 = bf16[2048,1536]{1,0:T(8,128)(2,1)} fusion(bf16[1024,2048]{1,0:T(8,128)(2,1)S(1)} %copy-done.12, bf16[1024,1536]{1,0:T(8,128)(2,1)} %get-tuple-element.256), kind=kOutput, calls=%fused_computation.7 | convolution fusion | flops 6445596672 | bytes 13631488 | tf_op jit(solution)/shard_map/dot_general | solution.py:26
  479.4 8.2 %fusion.25.whole_ref = f32[512,2048]{1,0:T(8,128)} fusion(bf16[2048,2048]{1,0:T(8,128)(2,1)} %all-gather.4.cloned.1.call-done, bf16[1024,1536]{1,0:T(8,128)(2,1)S(1)} %copy-done.59), kind=kOutput, calls=%fused_computation.35 | convolution fusion | flops 3221225472 | bytes 12058624 | tf_op jit(solution)/shard_map/dot_general | solution.py:26
  500.2 46.7 %collective-permute-done.46 = f32[1,256]{1,0:T(1,128)S(1)} collective-permute-done((f32[1,256]{1,0:T(1,128)S(1)}, f32[1,256]{1,0:T(1,128)S(1)}, u32[]{:S(2)}, u32[]{:S(2)}) %collective-permute-start.46) | collective-permute-done | bytes 1056 | tf_op jit(solution)/shard_map/ppermute | solution.py:561
  561.9 12.2 %collective-permute-done.51.refs_3_ = bf16[96,2048]{1,0:T(8,128)(2,1)S(1)} collective-permute-done((bf16[96,2048]{1,0:T(8,128)(2,1)S(1)}, bf16[96,2048]{1,0:T(8,128)(2,1)S(1)}, u32[]{:S(2)}, u32[]{:S(2)}) %collective-permute-start.51) | collective-permute-done | bytes 393248 | tf_op jit(solution)/shard_map/ppermute | solution.py:561
  582.5 5.9 weave_units.2
  588.5 6.5 %reduce-scatter.11.cloned.1.call-done.refs_0_ = bf16[256,512]{1,0:T(8,128)(2,1)} async-done(((bf16[2048,512]{1,0:T(8,128)(2,1)}), bf16[256,512]{1,0:T(8,128)(2,1)}) %reduce-scatter.11.cloned.1.call-update) | async-done | bytes 262160 | tf_op jit(solution)/shard_map/reduce_scatter | solution.py:756
  598.1 5.9 weave_units.3
  614.5 6.7 %split_columns.2 = (f32[256,2048]{1,0:T(8,128)}, f32[256,1024]{1,0:T(8,128)}, f32[256,1024]{1,0:T(8,128)}, f32[256,2048]{1,0:T(8,128)}, f32[256,1]{1,0:T(8,128)}) custom-call(s32[1]{0:T(128)} %bitcast.1.rank_ref, bf16[256,1536]{1,0:T(8,128)(2,1)} %reduce-scatter.9.cloned.1.call-done.refs_0_, bf16[256,1536]{1,0:T(8,128)(2,1)} %copy-done.21, ...), custom_call_target="tpu_custom_call" | custom-call | bytes 9437184 | tf_op jit(solution)/shard_map/split_columns/pallas_call | solution.py:410
  (404 shorter events, 279.5 us)
Async XLA Ops:
  7.3 99.6 %all-gather.4.cloned.1.call-start = ((), (), s32[]{:S(2)}) async-start(), calls=%async_computation.4 | async-start | bytes 9437184 | tf_op jit(solution)/shard_map/all_gather | solution.py:749
  9.6 205.4 %all-gather.6.cloned.1.call-start = ((), (), s32[]{:S(2)}) async-start(), calls=%async_computation.5 | async-start | bytes 14155776 | tf_op jit(solution)/shard_map/all_gather | solution.py:749
  9.7 33.1 %collective-permute-start.1 = (bf16[256,2048]{1,0:T(8,128)(2,1)}, bf16[256,2048]{1,0:T(8,128)(2,1)}, u32[]{:S(2)}, u32[]{:S(2)}) collective-permute-start(bf16[256,2048]{1,0:T(8,128)(2,1)} %bitcast.65), channel_id=1, source_target_pairs={{0,16},{8,24},{16,0},{24,8},{1,17},{9,25},{17,1},{25,9},{2,18},{10... | collective-permute-start | bytes 3145736 | tf_op jit(solution)/shard_map/ppermute | solution.py:561
  12.7 30.1 %collective-permute-start = (bf16[256,2048]{1,0:T(8,128)(2,1)}, bf16[256,2048]{1,0:T(8,128)(2,1)}, u32[]{:S(2)}, u32[]{:S(2)}) collective-permute-start(bf16[256,2048]{1,0:T(8,128)(2,1)} %bitcast.66), channel_id=1, source_target_pairs={{0,8},{8,0},{16,24},{24,16},{1,9},{9,1},{17,25},{25,17},{2,10},{10... | collective-permute-start | bytes 3145736 | tf_op jit(solution)/shard_map/ppermute | solution.py:561
  58.0 219.7 %all-gather.8.cloned.1.call-start = ((), (), s32[]{:S(2)}) async-start(), calls=%async_computation.6 | async-start | bytes 7077888 | tf_op jit(solution)/shard_map/all_gather | solution.py:749
  140.7 291.4 %reduce-scatter.5.cloned.1.call-start = ((), (), s32[]{:S(2)}) async-start(), calls=%async_computation.7 | async-start | bytes 7077888 | tf_op jit(solution)/shard_map/reduce_scatter | solution.py:756
  249.8 241.1 %reduce-scatter.7.cloned.1.call-start = ((), (), s32[]{:S(2)}) async-start(), calls=%async_computation.8 | async-start | bytes 14155776 | tf_op jit(solution)/shard_map/reduce_scatter | solution.py:756
  308.5 24.9 %collective-permute-start.26 = (bf16[256,2048]{1,0:T(8,128)(2,1)S(1)}, bf16[256,2048]{1,0:T(8,128)(2,1)}, u32[]{:S(2)}, u32[]{:S(2)}) collective-permute-start(bf16[256,2048]{1,0:T(8,128)(2,1)S(1)} %get-tuple-element.219), channel_id=1, source_target_pairs={{0,8},{8,0},{16,24},{24,16},{1,9},{9,1},{17,25},{25,17},{2,10},{10... | collective-permute-start | bytes 3145736 | tf_op jit(solution)/shard_map/ppermute | solution.py:561
  309.2 24.6 %collective-permute-start.27 = (bf16[256,2048]{1,0:T(8,128)(2,1)S(1)}, bf16[256,2048]{1,0:T(8,128)(2,1)}, u32[]{:S(2)}, u32[]{:S(2)}) collective-permute-start(bf16[256,2048]{1,0:T(8,128)(2,1)S(1)} %get-tuple-element.220), channel_id=1, source_target_pairs={{0,16},{8,24},{16,0},{24,8},{1,17},{9,25},{17,1},{25,9},{2,18},{10... | collective-permute-start | bytes 3145736 | tf_op jit(solution)/shard_map/ppermute | solution.py:561
  333.8 241.3 %reduce-scatter.9.cloned.1.call-start = ((), (), s32[]{:S(2)}) async-start(), calls=%async_computation.9 | async-start | bytes 7077888 | tf_op jit(solution)/shard_map/reduce_scatter | solution.py:756
  390.3 24.4 %collective-permute-start.32 = (bf16[256,2048]{1,0:T(8,128)(2,1)}, bf16[256,2048]{1,0:T(8,128)(2,1)S(1)}, u32[]{:S(2)}, u32[]{:S(2)}) collective-permute-start(bf16[256,2048]{1,0:T(8,128)(2,1)} %get-tuple-element.238), channel_id=1, source_target_pairs={{0,8},{8,0},{16,24},{24,16},{1,9},{9,1},{17,25},{25,17},{2,10},{10... | collective-permute-start | bytes 3145736 | tf_op jit(solution)/shard_map/ppermute | solution.py:561
  432.1 58.8 %collective-permute-start.42 = (bf16[192,2048]{1,0:T(8,128)(2,1)}, bf16[192,2048]{1,0:T(8,128)(2,1)}, u32[]{:S(2)}, u32[]{:S(2)}) collective-permute-start(bf16[192,2048]{1,0:T(8,128)(2,1)} %reduce-scatter.5.cloned.1.call-done.refs_0_), channel_id=1, source_target_pairs={{0,16},{8,24},{16,0},{24,8},{1,17},{9,25},{17,1},{25,9},{2,18},{10... | collective-permute-start | bytes 2359304 | tf_op jit(solution)/shard_map/ppermute | solution.py:561
  433.2 57.8 %collective-permute-start.41 = (bf16[192,2048]{1,0:T(8,128)(2,1)}, bf16[192,2048]{1,0:T(8,128)(2,1)}, u32[]{:S(2)}, u32[]{:S(2)}) collective-permute-start(bf16[192,2048]{1,0:T(8,128)(2,1)} %reduce-scatter.5.cloned.1.call-done.refs_0_), channel_id=1, source_target_pairs={{0,8},{8,0},{16,24},{24,16},{1,9},{9,1},{17,25},{25,17},{2,10},{10... | collective-permute-start | bytes 2359304 | tf_op jit(solution)/shard_map/ppermute | solution.py:561
  434.2 39.3 %collective-permute-start.36 = (bf16[512,512]{1,0:T(8,128)(2,1)}, bf16[512,512]{1,0:T(8,128)(2,1)S(1)}, u32[]{:S(2)}, u32[]{:S(2)}) collective-permute-start(bf16[512,512]{1,0:T(8,128)(2,1)} %get-tuple-element.248), channel_id=1, source_target_pairs={{0,8},{8,0},{16,24},{24,16},{1,9},{9,1},{17,25},{25,17},{2,10},{10... | collective-permute-start | bytes 1572872 | tf_op jit(solution)/shard_map/ppermute | solution.py:561
  435.2 38.4 %collective-permute-start.37 = (bf16[512,512]{1,0:T(8,128)(2,1)}, bf16[512,512]{1,0:T(8,128)(2,1)S(1)}, u32[]{:S(2)}, u32[]{:S(2)}) collective-permute-start(bf16[512,512]{1,0:T(8,128)(2,1)} %get-tuple-element.249), channel_id=1, source_target_pairs={{0,16},{8,24},{16,0},{24,8},{1,17},{9,25},{17,1},{25,9},{2,18},{10... | collective-permute-start | bytes 1572872 | tf_op jit(solution)/shard_map/ppermute | solution.py:561
  436.1 37.5 %collective-permute-start.38 = (bf16[512,512]{1,0:T(8,128)(2,1)S(1)}, bf16[512,512]{1,0:T(8,128)(2,1)S(1)}, u32[]{:S(2)}, u32[]{:S(2)}) collective-permute-start(bf16[512,512]{1,0:T(8,128)(2,1)S(1)} %get-tuple-element.250), channel_id=1, source_target_pairs={{0,24},{8,16},{16,8},{24,0},{1,25},{9,17},{17,9},{25,1},{2,26},{10... | collective-permute-start | bytes 1572872 | tf_op jit(solution)/shard_map/ppermute | solution.py:561
  491.0 104.0 %reduce-scatter.11.cloned.1.call-start = ((), (), s32[]{:S(2)}) async-start(), calls=%async_computation.10 | async-start | bytes 2359296 | tf_op jit(solution)/shard_map/reduce_scatter | solution.py:756
  492.2 56.2 %collective-permute-start.48 = (bf16[256,3072]{1,0:T(8,128)(2,1)}, bf16[256,3072]{1,0:T(8,128)(2,1)S(1)}, u32[]{:S(2)}, u32[]{:S(2)}) collective-permute-start(bf16[256,3072]{1,0:T(8,128)(2,1)} %reduce-scatter.7.cloned.1.call-done.refs_0_), channel_id=1, source_target_pairs={{0,16},{8,24},{16,0},{24,8},{1,17},{9,25},{17,1},{25,9},{2,18},{10... | collective-permute-start | bytes 4718600 | tf_op jit(solution)/shard_map/ppermute | solution.py:561
  493.1 55.4 %collective-permute-start.47 = (bf16[256,3072]{1,0:T(8,128)(2,1)}, bf16[256,3072]{1,0:T(8,128)(2,1)S(1)}, u32[]{:S(2)}, u32[]{:S(2)}) collective-permute-start(bf16[256,3072]{1,0:T(8,128)(2,1)} %reduce-scatter.7.cloned.1.call-done.refs_0_), channel_id=1, source_target_pairs={{0,8},{8,0},{16,24},{24,16},{1,9},{9,1},{17,25},{25,17},{2,10},{10... | collective-permute-start | bytes 4718600 | tf_op jit(solution)/shard_map/ppermute | solution.py:561
  496.7 51.8 %collective-permute-start.44 = (bf16[256,2048]{1,0:T(8,128)(2,1)S(1)}, bf16[256,2048]{1,0:T(8,128)(2,1)S(1)}, u32[]{:S(2)}, u32[]{:S(2)}) collective-permute-start(bf16[256,2048]{1,0:T(8,128)(2,1)S(1)} %get-tuple-element.263), channel_id=1, source_target_pairs={{0,8},{8,0},{16,24},{24,16},{1,9},{9,1},{17,25},{25,17},{2,10},{10... | collective-permute-start | bytes 3145736 | tf_op jit(solution)/shard_map/ppermute | solution.py:561
  498.2 50.2 %collective-permute-start.45 = (bf16[256,2048]{1,0:T(8,128)(2,1)S(1)}, bf16[256,2048]{1,0:T(8,128)(2,1)S(1)}, u32[]{:S(2)}, u32[]{:S(2)}) collective-permute-start(bf16[256,2048]{1,0:T(8,128)(2,1)S(1)} %get-tuple-element.264), channel_id=1, source_target_pairs={{0,16},{8,24},{16,0},{24,8},{1,17},{9,25},{17,1},{25,9},{2,18},{10... | collective-permute-start | bytes 3145736 | tf_op jit(solution)/shard_map/ppermute | solution.py:561
  499.5 47.5 %collective-permute-start.46 = (f32[1,256]{1,0:T(1,128)S(1)}, f32[1,256]{1,0:T(1,128)S(1)}, u32[]{:S(2)}, u32[]{:S(2)}) collective-permute-start(f32[1,256]{1,0:T(1,128)S(1)} %add.139), channel_id=1, source_target_pairs={{0,16},{8,24},{16,0},{24,8},{1,17},{9,25},{17,1},{25,9},{2,18},{10... | collective-permute-start | bytes 3080 | tf_op jit(solution)/shard_map/ppermute | solution.py:561
  550.2 24.3 %collective-permute-start.49 = (bf16[128,3072]{1,0:T(8,128)(2,1)S(1)}, bf16[128,3072]{1,0:T(8,128)(2,1)S(1)}, u32[]{:S(2)}, u32[]{:S(2)}) collective-permute-start(bf16[128,3072]{1,0:T(8,128)(2,1)S(1)} %slice.186), channel_id=1, source_target_pairs={{0,8},{8,0},{16,24},{24,16},{1,9},{9,1},{17,25},{25,17},{2,10},{10... | collective-permute-start | bytes 2359304 | tf_op jit(solution)/shard_map/ppermute | solution.py:561
  550.7 24.5 %collective-permute-start.50 = (bf16[128,3072]{1,0:T(8,128)(2,1)S(1)}, bf16[128,3072]{1,0:T(8,128)(2,1)S(1)}, u32[]{:S(2)}, u32[]{:S(2)}) collective-permute-start(bf16[128,3072]{1,0:T(8,128)(2,1)S(1)} %slice.187), channel_id=1, source_target_pairs={{0,16},{8,24},{16,0},{24,8},{1,17},{9,25},{17,1},{25,9},{2,18},{10... | collective-permute-start | bytes 2359304 | tf_op jit(solution)/shard_map/ppermute | solution.py:561
  (116 other events, 1258.4 us)
Sparse Core Ops, SparseCore 0:
  10.3 84.9 all-gather.3
  97.4 115.6 all-gather.5
  214.7 62.9 all-gather.7
  279.9 68.4 reduce-scatter.4
  350.5 127.5 reduce-scatter.6
  491.1 66.9 reduce-scatter.8
  560.9 34.0 reduce-scatter.10

commit v6 on v5

--- a/solution.py
+++ b/solution.py
@@ -375,56 +375,62 @@
 
 
 def split_columns_kernel(counts, sizes, weighed, rank_ref, *refs):
-    sources, refs = grouped(refs, counts)
-    weights, outs, sums = refs[:weighed], refs[weighed : weighed + len(sizes)], refs[-1]
+    sources = []
+    for group in counts:
+        blocks, refs = grouped(refs, group)
+        sources.append(blocks)
+    weights, outs, sums = refs[:weighed], refs[weighed:-1], refs[-1]
     block = jnp.bitwise_xor(pl.program_id(0), rank_ref[0])
-    for j, pieces in enumerate(sources):
+    for j in range(len(counts[0])):
 
         @pl.when(block == j)
-        def _(pieces=pieces):
-            top = 0
-            for piece in pieces:
-                start, stop = 0, top + piece.shape[0]
-                for size, out in zip(sizes, outs):
-                    out[top:stop, :] = piece[:, start : start + size].astype(F32)
-                    start += size
-                top = stop
-
-    if weighed:
-        part = sum(
-            jnp.sum(out[...] * weight[...].astype(F32), axis=1, keepdims=True)
-            for out, weight in zip(outs, weights)
-        )
-
-        @pl.when(pl.program_id(0) == 0)
-        def _():
-            sums[...] = jnp.zeros_like(sums)
-
-        sums[...] += part
-
-
-def split_columns(rank, pieces, sizes, weights=()):
-    count, rows = len(pieces), pieces[0][0].shape[0]
-    group_specs = [pl.BlockSpec((rows, size), lambda a, r: (0, a)) for size in sizes]
-    sum_specs = [pl.BlockSpec((rows, 1), lambda a, r: (0, 0))] if weights else []
+        def _(j=j):
+            done = 0
+            for blocks, group_sizes in zip(sources, sizes):
+                top = 0
+                for piece in blocks[j]:
+                    start, stop = 0, top + piece.shape[0]
+                    for size, out in zip(group_sizes, outs[done:]):
+                        out[top:stop, :] = piece[:, start : start + size].astype(F32)
+                        start += size
+                    top = stop
+                done += len(group_sizes)
+
+    part = sum(
+        jnp.sum(out[...] * weight[...].astype(F32), axis=1, keepdims=True)
+        for out, weight in zip(outs, weights)
+    )
+
+    @pl.when(pl.program_id(0) == 0)
+    def _():
+        sums[...] = jnp.zeros_like(sums)
+
+    sums[...] += part
+
+
+def split_columns(rank, groups, sizes, weights):
+    count, rows = len(groups[0]), groups[0][0][0].shape[0]
+    pieces, flat = sum(groups, []), sum(sizes, ())
+    part_specs = [pl.BlockSpec((rows, size), lambda a, r: (0, a)) for size in flat]
     return pl.pallas_call(
         functools.partial(
-            split_columns_kernel, [len(block) for block in pieces], sizes, len(weights)
+            split_columns_kernel, [[len(block) for block in group] for group in groups], sizes,
+            len(weights),
         ),
         grid_spec=pltpu.PrefetchScalarGridSpec(
             num_scalar_prefetch=1,
             grid=(count,),
             in_specs=flat_specs(pieces, lambda p: pl.BlockSpec(p.shape, lambda a, r: (0, 0)))
-            + group_specs[: len(weights)],
-            out_specs=group_specs + sum_specs,
-        ),
-        out_shape=[jax.ShapeDtypeStruct((rows, count * size), F32) for size in sizes]
-        + [jax.ShapeDtypeStruct((rows, 1), F32)] * len(sum_specs),
+            + part_specs[: len(weights)],
+            out_specs=part_specs + [pl.BlockSpec((rows, 1), lambda a, r: (0, 0))],
+        ),
+        out_shape=[jax.ShapeDtypeStruct((rows, count * size), F32) for size in flat]
+        + [jax.ShapeDtypeStruct((rows, 1), F32)],
         compiler_params=pltpu.CompilerParams(
             dimension_semantics=("arbitrary",), vmem_limit_bytes=VMEM_LIMIT
         ),
         cost_estimate=pl.CostEstimate(
-            flops=0, bytes_accessed=6 * rows * count * sum(sizes), transcendentals=0
+            flops=0, bytes_accessed=6 * rows * count * sum(flat), transcendentals=0
         ),
         name="split_columns",
     )(rank, *sum(pieces, []), *weights)
@@ -933,11 +939,10 @@
     attn_held, out_held, gain_sums, up_grad = sync(attn_held, out_held, gain_sums, up_grad)
     out_held = gather_turn(out_held)
     gain_sums = sum_over(gain_sums, steps[4:])
-    *attn_grads, in_sums = split_columns(
-        rank_ref, gather_pieces(attn_held), (qcols, kcols, kcols, qcols),
-        (q_weight, k_weight, v_weight, g_weight),
-    )
-    (out_grad,) = split_columns(rank_ref, gather_pieces(out_held), (dcols,))
+    *attn_grads, out_grad, in_sums = split_columns(
+        rank_ref, [gather_pieces(attn_held), gather_pieces(out_held)],
+        [(qcols, kcols, kcols, qcols), (dcols,)], (q_weight, k_weight, v_weight, g_weight),
+    )
     attn_gain_grad = in_sums[:, 0] / attn_gain.astype(F32)
     mlp_gain_grad = (gate_sums + up_sums)[:, 0] / mlp_gain.astype(F32)
 

time: 642 us -> 645 us (level)
  transfers between devices with their start and end apart: 71 -> 71, of which waited for: 33 -> 35; matrix products, arithmetic and copies ran while one was open for 35% -> 34% of each run, Pallas kernels for 11% -> 10%
where the time goes in v6:
time: 645 us; the launch traced here: 637 us
  waiting for transfers between devices  239 us (37%)
  matrix products  150 us (23%)
  Pallas kernels  74.3 us (12%)
  starting transfers between devices  69.8 us (11%)
  local copies, waits for them, and re-layouts  65.7 us (10%)
  other arithmetic  19.4 us (3%)
  between operations  18.1 us (3%)
    ppermute x64, waiting for transfers between devices, swap(): lax.ppermute(values, axis, [(i, i ^ bit) for i in range(lax.axis_size(axi...  205 us
    dot_general x24, matrix products, mm(): return lax.dot_general(left, right, dims, preferred_element_type=F32)  150 us
    ppermute x64, starting transfers between devices, swap(): lax.ppermute(values, axis, [(i, i ^ bit) for i in range(lax.axis_size(axi...  68.9 us
    unnamed x159, local copies, waits for them, and re-layouts  41.3 us
    all_gather x3, waiting for transfers between devices, gather(): return lax.all_gather(weight, 'fsdp', axis=0, tiled=True)  27.5 us
    pallas_call x1, Pallas kernels, attend_backward(): pl.pallas_call(functools.partial(attend_bwd_kernel, blocks, rows, groups,...  19.6 us
    pallas_call x3, Pallas kernels, row_call(): pl.pallas_call(kernel, grid=(2,), in_specs=[spec(a.shape) for a in arrays...  14.5 us
  transfers between devices with their start and end apart: 71, of which 35 were waited for; matrix products, arithmetic and copies ran while one was open for 34% of the time, Pallas kernels for 10%

profile of v6, /device:TPU:0, one launch (start us, length us, event | category | flops | bytes accessed | tf_op | source)
XLA Modules:
  0.0 636.7 jit_solution(17586877162452599612)
XLA Ops:
  73.5 10.5 %collective-permute-done.10 = bf16[256,2048]{1,0:T(8,128)(2,1)S(1)} collective-permute-done((bf16[256,2048]{1,0:T(8,128)(2,1)S(1)}, bf16[256,2048]{1,0:T(8,128)(2,1)S(1)}, u32[]{:S(2)}, u32[]{:S(2)}) %collective-permute-start.10) | collective-permute-done | bytes 1048608 | tf_op jit(solution)/shard_map/ppermute | solution.py:567
  112.2 10.9 %fusion.29.q_ref.k_ref.v_ref.g_ref = f32[1024,1536]{1,0:T(8,128)} fusion(bf16[1024,2048]{1,0:T(8,128)(2,1)S(1)} %copy-done.11, bf16[2048,2048]{1,0:T(8,128)(2,1)} %all-gather.4.cloned.1.call-done), kind=kOutput, calls=%fused_computation.39 | convolution fusion | flops 6442450944 | bytes 16777216 | tf_op jit(solution)/shard_map/dot_general | solution.py:26
  128.9 11.8 %attend_forward.1 = (bf16[1024,512]{1,0:T(8,128)(2,1)}, f32[1024,512]{1,0:T(8,128)}, f32[2,4,512]{2,1,0:T(4,128)}) custom-call(s32[1]{0:T(128)} %bitcast.1.rank_ref, f32[1024,1536]{1,0:T(8,128)} %fusion.29.q_ref.k_ref.v_ref.g_ref, f32[1024,1536]{1,0:T(8,128)} %fusion.29.q_ref.k_ref.v_ref.g_ref, f32[1024,1536]{1,0:T(8,128)} %fusion.29.q_ref.k_ref.v_ref.g_ref, ...), custom_call_target="tpu_custom_call" | custom-call | flops 5368709120 | bytes 9437184 | tf_op jit(solution)/shard_map/attend_forward/pallas_call | solution.py:220
  146.2 9.8 %collective-permute-done.17.from_y_ref = bf16[128,2048]{1,0:T(8,128)(2,1)S(1)} collective-permute-done((bf16[128,2048]{1,0:T(8,128)(2,1)S(1)}, bf16[128,2048]{1,0:T(8,128)(2,1)S(1)}, u32[]{:S(2)}, u32[]{:S(2)}) %collective-permute-start.17) | collective-permute-done | bytes 524320 | tf_op jit(solution)/shard_map/ppermute | solution.py:567
  163.6 12.2 %collective-permute-done.18.x_ref = bf16[256,2048]{1,0:T(8,128)(2,1)S(1)} collective-permute-done((bf16[256,2048]{1,0:T(8,128)(2,1)S(1)}, bf16[256,2048]{1,0:T(8,128)(2,1)S(1)}, u32[]{:S(2)}, u32[]{:S(2)}) %collective-permute-start.18) | collective-permute-done | bytes 1048608 | tf_op jit(solution)/shard_map/ppermute | solution.py:567
  183.1 18.4 %collective-permute-done.21 = bf16[256,2048]{1,0:T(8,128)(2,1)S(1)} collective-permute-done((bf16[256,2048]{1,0:T(8,128)(2,1)}, bf16[256,2048]{1,0:T(8,128)(2,1)S(1)}, u32[]{:S(2)}, u32[]{:S(2)}) %collective-permute-start.21) | collective-permute-done | bytes 1048608 | tf_op jit(solution)/shard_map/ppermute | solution.py:567
  215.0 10.2 %fusion.21 = f32[1024,1536]{1,0:T(8,128)S(1)} fusion(bf16[1024,2048]{1,0:T(8,128)(2,1)} %constant_dynamic-update-slice_fusion.10, bf16[2048,3072]{0,1:T(8,128)(2,1)} %all-gather.6.cloned.1.call-done), kind=kOutput, calls=%fused_computation.31 | convolution fusion | flops 6442450944 | bytes 16777216 | tf_op jit(solution)/shard_map/dot_general | solution.py:26
  225.2 12.5 %multiply_convert_fusion.2 = (bf16[1024,1536]{1,0:T(8,128)(2,1)S(1)}, f32[1024,1536]{1,0:T(8,128)}) fusion(f32[1024,1536]{1,0:T(8,128)S(1)} %fusion.21, bf16[1024,2048]{1,0:T(8,128)(2,1)} %constant_dynamic-update-slice_fusion.10, bf16[2048,3072]{0,1:T(8,128)(2,1)S(1)} %copy-done.53), kind=kOutput, calls=%fused_computation.14 | convolution fusion | flops 6451888128 | bytes 26214400 | tf_op jit(solution)/shard_map/dot_general | solution.py:26
  237.7 12.1 %convolution_convert_fusion.2 = bf16[1536,2048]{1,0:T(8,128)(2,1)} fusion(bf16[1024,1536]{1,0:T(8,128)(2,1)S(1)} %get-tuple-element.210, bf16[1024,2048]{1,0:T(8,128)(2,1)} %constant_dynamic-update-slice_fusion.5), kind=kOutput, calls=%fused_computation.8 | convolution fusion | flops 6445596672 | bytes 13631488 | tf_op jit(solution)/shard_map/dot_general | solution.py:26
  250.2 27.5 %all-gather.8.cloned.1.call-done = bf16[1536,2048]{1,0:T(8,128)(2,1)} async-done(((bf16[192,2048]{1,0:T(8,128)(2,1)}), bf16[1536,2048]{1,0:T(8,128)(2,1)}) %all-gather.8.cloned.1.call-update) | async-done | bytes 6291472 | tf_op jit(solution)/shard_map/all_gather | solution.py:755
  293.8 14.4 %multiply_convert_fusion = (bf16[1024,1536]{1,0:T(8,128)(2,1)}, bf16[1024,1536]{1,0:T(8,128)(2,1)}) fusion(f32[1024,1536]{1,0:T(8,128)} %copy-done.62, f32[1024,1536]{1,0:T(8,128)} %get-tuple-element.355, bf16[1024,2048]{1,0:T(8,128)(2,1)} %constant_dynamic-update-slice_fusion.5, bf16[1536,2048]{1,0:T(8,128)(2,1)S(1)} %copy-done.54), kind=kOutput, calls=%fused_computation.12 | convolution fusion | flops 6462898176 | bytes 29360128 | tf_op jit(solution)/shard_map/dot_general | solution.py:26
  310.1 18.7 %convolution_convert_fusion = bf16[2048,3072]{1,0:T(8,128)(2,1)} fusion(bf16[1024,2048]{1,0:T(8,128)(2,1)} %constant_dynamic-update-slice_fusion.10, bf16[1024,1536]{1,0:T(8,128)(2,1)} %get-tuple-element.223, bf16[1024,1536]{1,0:T(8,128)(2,1)S(1)} %copy-done.56), kind=kOutput, calls=%fused_computation.1 | convolution fusion | flops 12903776256 | bytes 23068672 | tf_op jit(solution)/shard_map/dot_general | solution.py:26
  364.2 17.8 %collective-permute-done.30.x_ref = bf16[256,2048]{1,0:T(8,128)(2,1)S(1)} collective-permute-done((bf16[256,2048]{1,0:T(8,128)(2,1)S(1)}, bf16[256,2048]{1,0:T(8,128)(2,1)S(1)}, u32[]{:S(2)}, u32[]{:S(2)}) %collective-permute-start.30) | collective-permute-done | bytes 1048608 | tf_op jit(solution)/shard_map/ppermute | solution.py:567
  391.7 19.4 %collective-permute-done.33 = bf16[256,2048]{1,0:T(8,128)(2,1)S(1)} collective-permute-done((bf16[256,2048]{1,0:T(8,128)(2,1)}, bf16[256,2048]{1,0:T(8,128)(2,1)S(1)}, u32[]{:S(2)}, u32[]{:S(2)}) %collective-permute-start.33) | collective-permute-done | bytes 1048608 | tf_op jit(solution)/shard_map/ppermute | solution.py:567
  415.5 8.1 %collective-permute-done.34 = bf16[128,2048]{1,0:T(8,128)(2,1)S(1)} collective-permute-done((bf16[128,2048]{1,0:T(8,128)(2,1)S(1)}, bf16[128,2048]{1,0:T(8,128)(2,1)S(1)}, u32[]{:S(2)}, u32[]{:S(2)}) %collective-permute-start.34) | collective-permute-done | bytes 524320 | tf_op jit(solution)/shard_map/ppermute | solution.py:567
  437.7 19.6 %attend_backward.1 = (bf16[1024,1536]{1,0:T(8,128)(2,1)}, f32[1,128]{1,0:T(1,128)}, f32[1,128]{1,0:T(1,128)}) custom-call(s32[1]{0:T(128)} %bitcast.1.rank_ref, f32[1024,1536]{1,0:T(8,128)} %fusion.29.q_ref.k_ref.v_ref.g_ref, f32[1024,1536]{1,0:T(8,128)} %fusion.29.q_ref.k_ref.v_ref.g_ref, f32[1024,1536]{1,0:T(8,128)} %fusion.29.q_ref.k_ref.v_ref.g_ref, ...), custom_call_target="tpu_custom_call" | custom-call | flops 13421772800 | bytes 12582912 | tf_op jit(solution)/shard_map/attend_backward/pallas_call | solution.py:257
  458.0 10.5 %convolution_convert_fusion.1 = bf16[2048,1536]{1,0:T(8,128)(2,1)} fusion(bf16[1024,2048]{1,0:T(8,128)(2,1)S(1)} %copy-done.12, bf16[1024,1536]{1,0:T(8,128)(2,1)} %get-tuple-element.257), kind=kOutput, calls=%fused_computation.7 | convolution fusion | flops 6445596672 | bytes 13631488 | tf_op jit(solution)/shard_map/dot_general | solution.py:26
  479.5 8.2 %fusion.25.whole_ref = f32[512,2048]{1,0:T(8,128)} fusion(bf16[2048,2048]{1,0:T(8,128)(2,1)} %all-gather.4.cloned.1.call-done, bf16[1024,1536]{1,0:T(8,128)(2,1)S(1)} %copy-done.59), kind=kOutput, calls=%fused_computation.35 | convolution fusion | flops 3221225472 | bytes 12058624 | tf_op jit(solution)/shard_map/dot_general | solution.py:26
  500.2 46.5 %collective-permute-done.46 = f32[1,256]{1,0:T(1,128)S(1)} collective-permute-done((f32[1,256]{1,0:T(1,128)S(1)}, f32[1,256]{1,0:T(1,128)S(1)}, u32[]{:S(2)}, u32[]{:S(2)}) %collective-permute-start.46) | collective-permute-done | bytes 1056 | tf_op jit(solution)/shard_map/ppermute | solution.py:567
  561.9 12.3 %collective-permute-done.51.refs_3_ = bf16[96,2048]{1,0:T(8,128)(2,1)S(1)} collective-permute-done((bf16[96,2048]{1,0:T(8,128)(2,1)S(1)}, bf16[96,2048]{1,0:T(8,128)(2,1)S(1)}, u32[]{:S(2)}, u32[]{:S(2)}) %collective-permute-start.51) | collective-permute-done | bytes 393248 | tf_op jit(solution)/shard_map/ppermute | solution.py:567
  582.6 5.9 weave_units.2
  588.5 6.5 %reduce-scatter.11.cloned.1.call-done.refs_5_ = bf16[256,512]{1,0:T(8,128)(2,1)} async-done(((bf16[2048,512]{1,0:T(8,128)(2,1)}), bf16[256,512]{1,0:T(8,128)(2,1)}) %reduce-scatter.11.cloned.1.call-update) | async-done | bytes 262160 | tf_op jit(solution)/shard_map/reduce_scatter | solution.py:762
  600.9 6.0 weave_units.3
  620.5 7.6 %split_columns.1 = (f32[256,2048]{1,0:T(8,128)}, f32[256,1024]{1,0:T(8,128)}, f32[256,1024]{1,0:T(8,128)}, f32[256,2048]{1,0:T(8,128)}, f32[256,2048]{1,0:T(8,128)}, /*index=5*/f32[256,1]{1,0:T(8,128)}) custom-call(s32[1]{0:T(128)} %bitcast.1.rank_ref, bf16[256,1536]{1,0:T(8,128)(2,1)} %reduce-scatter.9.cloned.1.call-done.refs_0_, ...), custom_call_target="tpu_custom_call" | custom-call | bytes 12582912 | tf_op jit(solution)/shard_map/split_columns/pallas_call | solution.py:415
  (403 shorter events, 281.3 us)
Async XLA Ops:
  7.3 99.6 %all-gather.4.cloned.1.call-start = ((), (), s32[]{:S(2)}) async-start(), calls=%async_computation.4 | async-start | bytes 9437184 | tf_op jit(solution)/shard_map/all_gather | solution.py:755
  9.6 205.3 %all-gather.6.cloned.1.call-start = ((), (), s32[]{:S(2)}) async-start(), calls=%async_computation.5 | async-start | bytes 14155776 | tf_op jit(solution)/shard_map/all_gather | solution.py:755
  9.7 33.1 %collective-permute-start.1 = (bf16[256,2048]{1,0:T(8,128)(2,1)}, bf16[256,2048]{1,0:T(8,128)(2,1)}, u32[]{:S(2)}, u32[]{:S(2)}) collective-permute-start(bf16[256,2048]{1,0:T(8,128)(2,1)} %bitcast.65), channel_id=1, source_target_pairs={{0,16},{8,24},{16,0},{24,8},{1,17},{9,25},{17,1},{25,9},{2,18},{10... | collective-permute-start | bytes 3145736 | tf_op jit(solution)/shard_map/ppermute | solution.py:567
  12.7 30.1 %collective-permute-start = (bf16[256,2048]{1,0:T(8,128)(2,1)}, bf16[256,2048]{1,0:T(8,128)(2,1)}, u32[]{:S(2)}, u32[]{:S(2)}) collective-permute-start(bf16[256,2048]{1,0:T(8,128)(2,1)} %bitcast.66), channel_id=1, source_target_pairs={{0,8},{8,0},{16,24},{24,16},{1,9},{9,1},{17,25},{25,17},{2,10},{10... | collective-permute-start | bytes 3145736 | tf_op jit(solution)/shard_map/ppermute | solution.py:567
  58.0 219.7 %all-gather.8.cloned.1.call-start = ((), (), s32[]{:S(2)}) async-start(), calls=%async_computation.6 | async-start | bytes 7077888 | tf_op jit(solution)/shard_map/all_gather | solution.py:755
  140.7 291.4 %reduce-scatter.5.cloned.1.call-start = ((), (), s32[]{:S(2)}) async-start(), calls=%async_computation.7 | async-start | bytes 7077888 | tf_op jit(solution)/shard_map/reduce_scatter | solution.py:762
  249.8 241.2 %reduce-scatter.7.cloned.1.call-start = ((), (), s32[]{:S(2)}) async-start(), calls=%async_computation.8 | async-start | bytes 14155776 | tf_op jit(solution)/shard_map/reduce_scatter | solution.py:762
  308.5 24.9 %collective-permute-start.26 = (bf16[256,2048]{1,0:T(8,128)(2,1)S(1)}, bf16[256,2048]{1,0:T(8,128)(2,1)}, u32[]{:S(2)}, u32[]{:S(2)}) collective-permute-start(bf16[256,2048]{1,0:T(8,128)(2,1)S(1)} %get-tuple-element.220), channel_id=1, source_target_pairs={{0,8},{8,0},{16,24},{24,16},{1,9},{9,1},{17,25},{25,17},{2,10},{10... | collective-permute-start | bytes 3145736 | tf_op jit(solution)/shard_map/ppermute | solution.py:567
  309.2 24.6 %collective-permute-start.27 = (bf16[256,2048]{1,0:T(8,128)(2,1)S(1)}, bf16[256,2048]{1,0:T(8,128)(2,1)}, u32[]{:S(2)}, u32[]{:S(2)}) collective-permute-start(bf16[256,2048]{1,0:T(8,128)(2,1)S(1)} %get-tuple-element.221), channel_id=1, source_target_pairs={{0,16},{8,24},{16,0},{24,8},{1,17},{9,25},{17,1},{25,9},{2,18},{10... | collective-permute-start | bytes 3145736 | tf_op jit(solution)/shard_map/ppermute | solution.py:567
  333.8 241.3 %reduce-scatter.9.cloned.1.call-start = ((), (), s32[]{:S(2)}) async-start(), calls=%async_computation.9 | async-start | bytes 7077888 | tf_op jit(solution)/shard_map/reduce_scatter | solution.py:762
  390.3 24.5 %collective-permute-start.32 = (bf16[256,2048]{1,0:T(8,128)(2,1)}, bf16[256,2048]{1,0:T(8,128)(2,1)S(1)}, u32[]{:S(2)}, u32[]{:S(2)}) collective-permute-start(bf16[256,2048]{1,0:T(8,128)(2,1)} %get-tuple-element.239), channel_id=1, source_target_pairs={{0,8},{8,0},{16,24},{24,16},{1,9},{9,1},{17,25},{25,17},{2,10},{10... | collective-permute-start | bytes 3145736 | tf_op jit(solution)/shard_map/ppermute | solution.py:567
  432.1 58.9 %collective-permute-start.42 = (bf16[192,2048]{1,0:T(8,128)(2,1)}, bf16[192,2048]{1,0:T(8,128)(2,1)}, u32[]{:S(2)}, u32[]{:S(2)}) collective-permute-start(bf16[192,2048]{1,0:T(8,128)(2,1)} %reduce-scatter.5.cloned.1.call-done.refs_0_), channel_id=1, source_target_pairs={{0,16},{8,24},{16,0},{24,8},{1,17},{9,25},{17,1},{25,9},{2,18},{10... | collective-permute-start | bytes 2359304 | tf_op jit(solution)/shard_map/ppermute | solution.py:567
  433.1 57.8 %collective-permute-start.41 = (bf16[192,2048]{1,0:T(8,128)(2,1)}, bf16[192,2048]{1,0:T(8,128)(2,1)}, u32[]{:S(2)}, u32[]{:S(2)}) collective-permute-start(bf16[192,2048]{1,0:T(8,128)(2,1)} %reduce-scatter.5.cloned.1.call-done.refs_0_), channel_id=1, source_target_pairs={{0,8},{8,0},{16,24},{24,16},{1,9},{9,1},{17,25},{25,17},{2,10},{10... | collective-permute-start | bytes 2359304 | tf_op jit(solution)/shard_map/ppermute | solution.py:567
  434.2 39.3 %collective-permute-start.36 = (bf16[512,512]{1,0:T(8,128)(2,1)}, bf16[512,512]{1,0:T(8,128)(2,1)S(1)}, u32[]{:S(2)}, u32[]{:S(2)}) collective-permute-start(bf16[512,512]{1,0:T(8,128)(2,1)} %get-tuple-element.249), channel_id=1, source_target_pairs={{0,8},{8,0},{16,24},{24,16},{1,9},{9,1},{17,25},{25,17},{2,10},{10... | collective-permute-start | bytes 1572872 | tf_op jit(solution)/shard_map/ppermute | solution.py:567
  435.2 38.4 %collective-permute-start.37 = (bf16[512,512]{1,0:T(8,128)(2,1)}, bf16[512,512]{1,0:T(8,128)(2,1)S(1)}, u32[]{:S(2)}, u32[]{:S(2)}) collective-permute-start(bf16[512,512]{1,0:T(8,128)(2,1)} %get-tuple-element.250), channel_id=1, source_target_pairs={{0,16},{8,24},{16,0},{24,8},{1,17},{9,25},{17,1},{25,9},{2,18},{10... | collective-permute-start | bytes 1572872 | tf_op jit(solution)/shard_map/ppermute | solution.py:567
  436.2 37.4 %collective-permute-start.38 = (bf16[512,512]{1,0:T(8,128)(2,1)S(1)}, bf16[512,512]{1,0:T(8,128)(2,1)S(1)}, u32[]{:S(2)}, u32[]{:S(2)}) collective-permute-start(bf16[512,512]{1,0:T(8,128)(2,1)S(1)} %get-tuple-element.251), channel_id=1, source_target_pairs={{0,24},{8,16},{16,8},{24,0},{1,25},{9,17},{17,9},{25,1},{2,26},{10... | collective-permute-start | bytes 1572872 | tf_op jit(solution)/shard_map/ppermute | solution.py:567
  491.1 103.9 %reduce-scatter.11.cloned.1.call-start = ((), (), s32[]{:S(2)}) async-start(), calls=%async_computation.10 | async-start | bytes 2359296 | tf_op jit(solution)/shard_map/reduce_scatter | solution.py:762
  492.3 56.2 %collective-permute-start.48 = (bf16[256,3072]{1,0:T(8,128)(2,1)}, bf16[256,3072]{1,0:T(8,128)(2,1)S(1)}, u32[]{:S(2)}, u32[]{:S(2)}) collective-permute-start(bf16[256,3072]{1,0:T(8,128)(2,1)} %reduce-scatter.7.cloned.1.call-done.refs_0_), channel_id=1, source_target_pairs={{0,16},{8,24},{16,0},{24,8},{1,17},{9,25},{17,1},{25,9},{2,18},{10... | collective-permute-start | bytes 4718600 | tf_op jit(solution)/shard_map/ppermute | solution.py:567
  493.1 55.4 %collective-permute-start.47 = (bf16[256,3072]{1,0:T(8,128)(2,1)}, bf16[256,3072]{1,0:T(8,128)(2,1)S(1)}, u32[]{:S(2)}, u32[]{:S(2)}) collective-permute-start(bf16[256,3072]{1,0:T(8,128)(2,1)} %reduce-scatter.7.cloned.1.call-done.refs_0_), channel_id=1, source_target_pairs={{0,8},{8,0},{16,24},{24,16},{1,9},{9,1},{17,25},{25,17},{2,10},{10... | collective-permute-start | bytes 4718600 | tf_op jit(solution)/shard_map/ppermute | solution.py:567
  496.7 51.8 %collective-permute-start.44 = (bf16[256,2048]{1,0:T(8,128)(2,1)S(1)}, bf16[256,2048]{1,0:T(8,128)(2,1)S(1)}, u32[]{:S(2)}, u32[]{:S(2)}) collective-permute-start(bf16[256,2048]{1,0:T(8,128)(2,1)S(1)} %get-tuple-element.264), channel_id=1, source_target_pairs={{0,8},{8,0},{16,24},{24,16},{1,9},{9,1},{17,25},{25,17},{2,10},{10... | collective-permute-start | bytes 3145736 | tf_op jit(solution)/shard_map/ppermute | solution.py:567
  498.2 50.3 %collective-permute-start.45 = (bf16[256,2048]{1,0:T(8,128)(2,1)S(1)}, bf16[256,2048]{1,0:T(8,128)(2,1)S(1)}, u32[]{:S(2)}, u32[]{:S(2)}) collective-permute-start(bf16[256,2048]{1,0:T(8,128)(2,1)S(1)} %get-tuple-element.265), channel_id=1, source_target_pairs={{0,16},{8,24},{16,0},{24,8},{1,17},{9,25},{17,1},{25,9},{2,18},{10... | collective-permute-start | bytes 3145736 | tf_op jit(solution)/shard_map/ppermute | solution.py:567
  499.5 47.2 %collective-permute-start.46 = (f32[1,256]{1,0:T(1,128)S(1)}, f32[1,256]{1,0:T(1,128)S(1)}, u32[]{:S(2)}, u32[]{:S(2)}) collective-permute-start(f32[1,256]{1,0:T(1,128)S(1)} %add.139), channel_id=1, source_target_pairs={{0,16},{8,24},{16,0},{24,8},{1,17},{9,25},{17,1},{25,9},{2,18},{10... | collective-permute-start | bytes 3080 | tf_op jit(solution)/shard_map/ppermute | solution.py:567
  550.2 24.2 %collective-permute-start.49 = (bf16[128,3072]{1,0:T(8,128)(2,1)S(1)}, bf16[128,3072]{1,0:T(8,128)(2,1)S(1)}, u32[]{:S(2)}, u32[]{:S(2)}) collective-permute-start(bf16[128,3072]{1,0:T(8,128)(2,1)S(1)} %slice.186), channel_id=1, source_target_pairs={{0,8},{8,0},{16,24},{24,16},{1,9},{9,1},{17,25},{25,17},{2,10},{10... | collective-permute-start | bytes 2359304 | tf_op jit(solution)/shard_map/ppermute | solution.py:567
  550.7 24.4 %collective-permute-start.50 = (bf16[128,3072]{1,0:T(8,128)(2,1)S(1)}, bf16[128,3072]{1,0:T(8,128)(2,1)S(1)}, u32[]{:S(2)}, u32[]{:S(2)}) collective-permute-start(bf16[128,3072]{1,0:T(8,128)(2,1)S(1)} %slice.187), channel_id=1, source_target_pairs={{0,16},{8,24},{16,0},{24,8},{1,17},{9,25},{17,1},{25,9},{2,18},{10... | collective-permute-start | bytes 2359304 | tf_op jit(solution)/shard_map/ppermute | solution.py:567
  (116 other events, 1242.6 us)
Sparse Core Ops, SparseCore 0:
  10.3 84.9 all-gather.3
  97.4 115.6 all-gather.5
  214.7 62.9 all-gather.7
  279.9 68.4 reduce-scatter.4
  350.5 127.5 reduce-scatter.6
  491.2 66.7 reduce-scatter.8
  560.9 34.0 reduce-scatter.10
